TPU v7x, 32 devices: a whole 2x2x4 slice. The times are simulated.
32 devices in a mesh: dp: 8 (over z, y), tensor: 4 (over x, core).
Axes of the slice: x: 2, y: 2, z: 4, core: 2. Of those that a mesh axis runs over, the one named last changes fastest.
Arguments:
- questions: bfloat16 [96, 64, 768], P(('dp', 'tensor')), may hold values from -6 to 6
- passages: bfloat16 [96, 256, 768], P(('dp', 'tensor')), may hold values from -6 to 6
- question_cotangent: bfloat16 [96, 64, 768], P(('dp', 'tensor')), may hold values from -6 to 6
- passage_cotangent: bfloat16 [96, 256, 768], P(('dp', 'tensor')), may hold values from -6 to 6
- positives: int32 [96, 4], P(('dp', 'tensor')), may hold values from 0 to 95, as said below
- positive_counts: int32 [96], P(('dp', 'tensor')), may hold values from 1 to 4, as said below
- attention_in: bfloat16 [2, 3, 768, 768], P(None, None, None, 'tensor'), may hold values from -0.21875 to 0.21875
- attention_bias: bfloat16 [2, 2, 768], P(None, None, 'tensor'), may hold values from -2 to 2
- attention_out: bfloat16 [2, 768, 768], P(None, 'tensor'), may hold values from -1.75 to 1.75
- branch_biases: bfloat16 [2, 2, 768], replicated, may hold values from -2 to 2
- norm_gains: bfloat16 [2, 2, 768], replicated, may hold values from 0.5 to 1.5
- norm_shifts: bfloat16 [2, 2, 768], replicated, may hold values from -2 to 2
- up_weight: bfloat16 [2, 768, 3072], P(None, None, 'tensor'), may hold values from -0.21875 to 0.21875
- up_bias: bfloat16 [2, 3072], P(None, 'tensor'), may hold values from -2 to 2
- down_weight: bfloat16 [2, 3072, 768], P(None, 'tensor'), may hold values from -0.15625 to 0.15625
Outputs:
- question_out: bfloat16 [96, 64, 768], P(('dp', 'tensor'))
- passage_out: bfloat16 [96, 256, 768], P(('dp', 'tensor'))
- question_losses: float32 [96], P(('dp', 'tensor'))
- question_gradient: bfloat16 [96, 64, 768], P(('dp', 'tensor'))
- passage_gradient: bfloat16 [96, 256, 768], P(('dp', 'tensor'))
- attention_in_gradient: float32 [2, 3, 768, 768], P(None, None, None, 'tensor')
- attention_bias_gradient: float32 [2, 2, 768], P(None, None, 'tensor')
- attention_out_gradient: float32 [2, 768, 768], P(None, 'tensor')
- branch_biases_gradient: float32 [2, 2, 768], replicated
- norm_gains_gradient: float32 [2, 2, 768], replicated
- norm_shifts_gradient: float32 [2, 2, 768], replicated
- up_weight_gradient: float32 [2, 768, 3072], P(None, None, 'tensor')
- up_bias_gradient: float32 [2, 3072], P(None, 'tensor')
- down_weight_gradient: float32 [2, 3072, 768], P(None, 'tensor')
Inputs may be any that keep to these rules, and one draw needn't show every extreme that they name: `positive_counts`: some question has 4 positives and another has 1. `positives`: the first positive_counts[i] entries of row i are distinct passage numbers; the remaining entries are 0 and name nothing.
All inputs are finite; a program needn't handle non-finite values.
Results may differ from a plain program's by a relative error of at most 0.02.
Values may be sent and summed in bfloat16 or wider, within the bound.
A program may use at most 192 MiB of HBM per device.

v0:
```python
from functools import partial

import jax
import jax.numpy as jnp
from jax import lax
from jax.sharding import PartitionSpec as P

D = 768
HD = 64


norm_epsilon = 1e-12


def layer_norm(summed, gain_row, shift_row):
    centered = summed - jnp.mean(summed, axis=-1, keepdims=True)
    inverse = lax.rsqrt(jnp.mean(centered * centered, axis=-1, keepdims=True) + norm_epsilon)
    scaled = centered * inverse
    return (scaled * gain_row + shift_row, scaled, inverse)


def norm_backward(upstream, scaled, inverse, gain_row):
    scaled_up = upstream * gain_row
    inner_sum = jnp.mean(scaled_up, axis=-1, keepdims=True)
    tilted = jnp.mean(scaled_up * scaled, axis=-1, keepdims=True)
    return inverse * (scaled_up - inner_sum - scaled * tilted)


def encoder_forward(tokens_share, params):
    (
        attention_in,
        attention_bias,
        attention_out,
        branch_biases,
        norm_gains,
        norm_shifts,
        up_weight,
        up_bias,
        down_weight,
    ) = params
    share_seqs, length, model_width = tokens_share.shape
    share_rows = share_seqs * length
    gathered = lax.all_gather(tokens_share, "tensor", axis=0, tiled=True)
    group_seqs = gathered.shape[0]
    all_rows = gathered.reshape(group_seqs * length, model_width)
    total_rows = all_rows.shape[0]
    local_width = attention_in.shape[2]
    head_shape = (group_seqs, length, local_width // HD, HD)
    projected = jnp.einsum(
        "td,cde->cte", all_rows, attention_in, preferred_element_type=jnp.float32
    )
    queries = (projected[0] + attention_bias[0]).astype(jnp.bfloat16).reshape(head_shape)
    key_rows = projected[1].astype(jnp.bfloat16).reshape(head_shape)
    values = (projected[2] + attention_bias[1]).astype(jnp.bfloat16).reshape(head_shape)
    scores = jnp.einsum(
        "gqhe,gkhe->ghqk", queries, key_rows, preferred_element_type=jnp.float32
    ) * HD ** (-0.5)
    row_top = jnp.max(scores, axis=-1, keepdims=True)
    log_total = row_top + jnp.log(jnp.sum(jnp.exp(scores - row_top), axis=-1, keepdims=True))
    weights_low = jnp.exp(scores - log_total).astype(jnp.bfloat16)
    mixed_rows = jnp.einsum(
        "ghqk,gkhe->gqhe", weights_low, values, preferred_element_type=jnp.float32
    )
    mixed_rows = mixed_rows.astype(jnp.bfloat16).reshape(total_rows, local_width)
    attended = (
        lax.psum_scatter(
            jnp.dot(mixed_rows, attention_out, preferred_element_type=jnp.float32).astype(
                jnp.bfloat16
            ),
            "tensor",
            scatter_dimension=0,
            tiled=True,
        ).astype(jnp.float32)
        + branch_biases[0]
    )
    residual = tokens_share.reshape(share_rows, model_width).astype(jnp.float32) + attended
    normed, scaled_one, inverse_one = layer_norm(residual, norm_gains[0], norm_shifts[0])
    normed_all = lax.all_gather(normed.astype(jnp.bfloat16), "tensor", axis=0, tiled=True)
    pre_active = jnp.dot(normed_all, up_weight, preferred_element_type=jnp.float32) + up_bias
    activated, gelu_pull = jax.vjp(partial(jax.nn.gelu, approximate=False), pre_active)
    active = activated.astype(jnp.bfloat16)
    fed_rows = (
        lax.psum_scatter(
            jnp.dot(
                lax.slice_in_dim(active, 0, lax.axis_size("tensor") * share_rows, axis=0),
                down_weight,
                preferred_element_type=jnp.float32,
            ).astype(jnp.bfloat16),
            "tensor",
            scatter_dimension=0,
            tiled=True,
        ).astype(jnp.float32)
        + branch_biases[1]
    )
    output, scaled_two, inverse_two = layer_norm(normed + fed_rows, norm_gains[1], norm_shifts[1])
    kept_state = (
        all_rows,
        queries,
        key_rows,
        values,
        log_total,
        mixed_rows,
        scaled_one,
        inverse_one,
        normed_all,
        gelu_pull,
        active,
        scaled_two,
        inverse_two,
    )
    return (output, kept_state)


def encoder_backward(upstream, kept_state, params):
    (
        attention_in,
        attention_bias,
        attention_out,
        branch_biases,
        norm_gains,
        norm_shifts,
        up_weight,
        up_bias,
        down_weight,
    ) = params
    (
        all_rows,
        queries,
        key_rows,
        values,
        log_total,
        mixed_rows,
        scaled_one,
        inverse_one,
        normed_all,
        gelu_pull,
        active,
        scaled_two,
        inverse_two,
    ) = kept_state
    total_rows = all_rows.shape[0]
    local_width = attention_in.shape[2]
    gain_two = jnp.sum(upstream * scaled_two, axis=0)
    shift_two = jnp.sum(upstream, axis=0)
    second_back = norm_backward(upstream, scaled_two, inverse_two, norm_gains[1])
    second_low = second_back.astype(jnp.bfloat16)
    bias_two = jnp.sum(second_low, axis=0, dtype=jnp.float32)
    fed_back = lax.all_gather(second_low, "tensor", axis=0, tiled=True)
    down_gradient = jnp.dot(active.T, fed_back, preferred_element_type=jnp.float32)
    active_back = jnp.dot(fed_back, down_weight.T, preferred_element_type=jnp.float32)
    upper_back = gelu_pull(active_back)[0].astype(jnp.bfloat16)
    up_gradient = jnp.dot(normed_all.T, upper_back, preferred_element_type=jnp.float32)
    up_bias_gradient = jnp.sum(upper_back, axis=0, dtype=jnp.float32)
    normed_back = (
        lax.psum_scatter(
            jnp.dot(upper_back, up_weight.T, preferred_element_type=jnp.float32).astype(
                jnp.bfloat16
            ),
            "tensor",
            scatter_dimension=0,
            tiled=True,
        ).astype(jnp.float32)
        + second_back
    )
    gain_one = jnp.sum(normed_back * scaled_one, axis=0)
    shift_one = jnp.sum(normed_back, axis=0)
    first_back = norm_backward(normed_back, scaled_one, inverse_one, norm_gains[0])
    first_low = first_back.astype(jnp.bfloat16)
    bias_one = jnp.sum(first_low, axis=0, dtype=jnp.float32)
    attended_back = lax.all_gather(first_low, "tensor", axis=0, tiled=True)
    out_gradient = jnp.dot(mixed_rows.T, attended_back, preferred_element_type=jnp.float32)
    mixed_back = jnp.dot(attended_back, attention_out.T, preferred_element_type=jnp.float32)
    mixed_back = mixed_back.astype(jnp.bfloat16).reshape(queries.shape)
    scores = jnp.einsum(
        "gqhe,gkhe->ghqk", queries, key_rows, preferred_element_type=jnp.float32
    ) * HD ** (-0.5)
    weights_full = jnp.exp(scores - log_total)
    weights_low = weights_full.astype(jnp.bfloat16)
    weight_back = jnp.einsum(
        "gqhe,gkhe->ghqk", mixed_back, values, preferred_element_type=jnp.float32
    )
    value_back = jnp.einsum(
        "ghqk,gqhe->gkhe", weights_low, mixed_back, preferred_element_type=jnp.float32
    )
    inner_sum = jnp.sum(weights_full * weight_back, axis=-1, keepdims=True)
    score_back = (weights_full * (weight_back - inner_sum)).astype(jnp.bfloat16)
    query_back = jnp.einsum(
        "ghqk,gkhe->gqhe", score_back, key_rows, preferred_element_type=jnp.float32
    ) * HD ** (-0.5)
    key_back = jnp.einsum(
        "ghqk,gqhe->gkhe", score_back, queries, preferred_element_type=jnp.float32
    ) * HD ** (-0.5)
    stacked = (
        jnp.stack([query_back, key_back, value_back])
        .astype(jnp.bfloat16)
        .reshape(3, total_rows, local_width)
    )
    in_gradient = jnp.einsum("td,cte->cde", all_rows, stacked, preferred_element_type=jnp.float32)
    bias_gradient = jnp.stack(
        [
            jnp.sum(stacked[0], axis=0, dtype=jnp.float32),
            jnp.sum(stacked[2], axis=0, dtype=jnp.float32),
        ]
    )
    input_back = (
        lax.psum_scatter(
            jnp.einsum(
                "cte,cde->td", stacked, attention_in, preferred_element_type=jnp.float32
            ).astype(jnp.bfloat16),
            "tensor",
            scatter_dimension=0,
            tiled=True,
        ).astype(jnp.float32)
        + first_back
    )
    sharded = (
        in_gradient,
        bias_gradient,
        out_gradient,
        up_gradient,
        up_bias_gradient,
        down_gradient,
    )
    small_sums = (gain_one, gain_two, shift_one, shift_two, bias_one, bias_two)
    return (input_back, sharded, small_sums)


def whole_sum(parts):
    return lax.psum((parts[0], parts[1], parts[2], parts[3], parts[4], parts[5]), "dp")


def body(
    questions,
    passages,
    question_cotangent,
    passage_cotangent,
    positives,
    positive_counts,
    attention_in,
    attention_bias,
    attention_out,
    branch_biases,
    norm_gains,
    norm_shifts,
    up_weight,
    up_bias,
    down_weight,
):
    parameters = (
        attention_in,
        attention_bias,
        attention_out,
        branch_biases,
        norm_gains,
        norm_shifts,
        up_weight,
        up_bias,
        down_weight,
    )
    question_params = tuple((array_item[0] for array_item in parameters))
    passage_params = tuple((array_item[1] for array_item in parameters))
    question_seqs, question_length, model_width = questions.shape
    passage_seqs, passage_length, _unused = passages.shape
    score_scale = 2.7 * D ** (-0.5)
    question_rows, question_kept = encoder_forward(questions, question_params)
    passage_rows, passage_kept = encoder_forward(passages, passage_params)
    question_cls = question_rows.reshape(question_seqs, question_length, model_width)[:, 0].astype(
        jnp.bfloat16
    )
    passage_cls = passage_rows.reshape(passage_seqs, passage_length, model_width)[:, 0].astype(
        jnp.bfloat16
    )
    all_cls = lax.all_gather(passage_cls, ("dp", "tensor"), axis=0, tiled=True)
    passage_total = all_cls.shape[0]
    scores = jnp.dot(question_cls, all_cls.T, preferred_element_type=jnp.float32) * score_scale
    row_top = jnp.max(scores, axis=1, keepdims=True)
    shifted = jnp.exp(scores - row_top)
    all_total = jnp.sum(shifted, axis=1, keepdims=True)
    slot_live = jnp.arange(positives.shape[1], dtype=jnp.int32)[None, :] < positive_counts[:, None]
    matches = (
        positives[:, :, None] == jnp.arange(passage_total, dtype=jnp.int32)[None, None, :]
    ) & slot_live[:, :, None]
    positive_marks = jnp.sum(matches.astype(jnp.float32), axis=1)
    positive_total = jnp.sum(positive_marks * shifted, axis=1, keepdims=True)
    question_losses = (jnp.log(all_total) - jnp.log(positive_total))[:, 0]
    score_back = (shifted / all_total - positive_marks * shifted / positive_total).astype(
        jnp.bfloat16
    )
    question_cls_back = (
        jnp.dot(score_back, all_cls, preferred_element_type=jnp.float32) * score_scale
    )
    passage_cls_back = lax.psum_scatter(
        jnp.dot(score_back.T, question_cls, preferred_element_type=jnp.float32) * score_scale,
        ("dp", "tensor"),
        scatter_dimension=0,
        tiled=True,
    )
    question_upstream = question_cotangent.astype(jnp.float32).at[:, 0, :].add(question_cls_back)
    question_upstream = question_upstream.reshape(question_seqs * question_length, model_width)
    passage_upstream = passage_cotangent.astype(jnp.float32).at[:, 0, :].add(passage_cls_back)
    passage_upstream = passage_upstream.reshape(passage_seqs * passage_length, model_width)
    question_back, question_sharded, question_small = encoder_backward(
        question_upstream, question_kept, question_params
    )
    passage_back, passage_sharded, passage_small = encoder_backward(
        passage_upstream, passage_kept, passage_params
    )
    joined = tuple(
        (
            jnp.stack([front_part, back_part])
            for front_part, back_part in zip(question_sharded, passage_sharded)
        )
    )
    totals = whole_sum(joined)
    gain_stack = jnp.stack(
        [
            jnp.stack([question_small[0], question_small[1]]),
            jnp.stack([passage_small[0], passage_small[1]]),
        ]
    )
    shift_stack = jnp.stack(
        [
            jnp.stack([question_small[2], question_small[3]]),
            jnp.stack([passage_small[2], passage_small[3]]),
        ]
    )
    bias_stack = jnp.stack(
        [
            jnp.stack([question_small[4], question_small[5]]),
            jnp.stack([passage_small[4], passage_small[5]]),
        ]
    )
    gain_sum, shift_sum, bias_sum = lax.psum(
        (gain_stack, shift_stack, bias_stack), ("dp", "tensor")
    )
    return (
        question_rows.reshape(questions.shape).astype(jnp.bfloat16),
        passage_rows.reshape(passages.shape).astype(jnp.bfloat16),
        question_losses,
        question_back.reshape(questions.shape).astype(jnp.bfloat16),
        passage_back.reshape(passages.shape).astype(jnp.bfloat16),
        totals[0],
        totals[1],
        totals[2],
        bias_sum,
        gain_sum,
        shift_sum,
        totals[3],
        totals[4],
        totals[5],
    )


def solution(mesh):
    in_specs = (
        P(("dp", "tensor"), None, None),
        P(("dp", "tensor"), None, None),
        P(("dp", "tensor"), None, None),
        P(("dp", "tensor"), None, None),
        P(("dp", "tensor"), None),
        P(("dp", "tensor")),
        P(None, None, None, "tensor"),
        P(None, None, "tensor"),
        P(None, "tensor", None),
        P(),
        P(),
        P(),
        P(None, None, "tensor"),
        P(None, "tensor"),
        P(None, "tensor", None),
    )
    out_specs = (
        P(("dp", "tensor"), None, None),
        P(("dp", "tensor"), None, None),
        P(("dp", "tensor")),
        P(("dp", "tensor"), None, None),
        P(("dp", "tensor"), None, None),
        P(None, None, None, "tensor"),
        P(None, None, "tensor"),
        P(None, "tensor", None),
        P(),
        P(),
        P(),
        P(None, None, "tensor"),
        P(None, "tensor"),
        P(None, "tensor", None),
    )
    return jax.shard_map(body, mesh=mesh, in_specs=in_specs, out_specs=out_specs, check_vma=False)
```

profile of v0, /device:TPU:0, one launch (start us, length us, event | category | flops | bytes accessed | tf_op | source)
XLA Modules:
  0.0 1245.8 jit_solution(15330254340414894985)
XLA Ops:
  9.8 19.9 %all-gather.10.cloned.1.call-done = bf16[12,64,768]{2,1,0:T(8,128)(2,1)} async-done(((bf16[3,64,768]{2,1,0:T(8,128)(2,1)}), bf16[12,64,768]{2,1,0:T(8,128)(2,1)}) %all-gather.10.cloned.1.call-update) | async-done | bytes 1179664 | tf_op jit(solution)/shard_map/all_gather | solution.py:43
  41.7 27.1 %all-gather.14.cloned.1.call-done = bf16[12,256,768]{2,1,0:T(8,128)(2,1)} async-done(((bf16[3,256,768]{2,1,0:T(8,128)(2,1)}), bf16[12,256,768]{2,1,0:T(8,128)(2,1)}) %all-gather.14.cloned.1.call-update) | async-done | bytes 4718608 | tf_op jit(solution)/shard_map/all_gather | solution.py:43
  68.8 5.1 convolution_bitcast_fusion
  77.4 4.3 squeeze.32
  83.9 6.0 multiply_reduce_fusion.1
  90.0 2.9 squeeze.31
  92.9 5.6 exponential_reduce_fusion
  103.6 3.6 convolution_convert_fusion.2
  113.5 41.8 %reduce-scatter.13.cloned.1.call-done = bf16[768,768]{1,0:T(8,128)(2,1)} async-done(((bf16[3072,768]{1,0:T(8,128)(2,1)}), bf16[768,768]{1,0:T(8,128)(2,1)}) %reduce-scatter.13.cloned.1.call-update) | async-done | bytes 1179664 | tf_op jit(solution)/shard_map/reduce_scatter | solution.py:66
  159.8 15.0 %all-gather.12.cloned.1.call-done = bf16[768,768]{1,0:T(8,128)(2,1)} async-done(((bf16[192,768]{1,0:T(8,128)(2,1)}), bf16[768,768]{1,0:T(8,128)(2,1)}) %all-gather.12.cloned.1.call-update) | async-done | bytes 1179664 | tf_op jit(solution)/shard_map/all_gather | solution.py:78
  174.9 9.6 multiply_convert_fusion.4
  186.6 27.7 %all-gather.16.cloned.1.call-done = bf16[3072,768]{1,0:T(8,128)(2,1)} async-done(((bf16[768,768]{1,0:T(8,128)(2,1)}), bf16[3072,768]{1,0:T(8,128)(2,1)}) %all-gather.16.cloned.1.call-update) | async-done | bytes 4718608 | tf_op jit(solution)/shard_map/all_gather | solution.py:78
  214.4 26.6 %multiply_convert_fusion.1 = (bf16[3072,768]{1,0:T(8,128)(2,1)S(1)}, f32[3072,768]{1,0:T(8,128)}, f32[3072,768]{1,0:T(8,128)}) fusion(f32[768]{0:T(1024)S(1)} %get-tuple-element.66, bf16[3072,768]{1,0:T(8,128)(2,1)} %all-gather.16.cloned.1.call-done, bf16[2,768,768]{2,1,0:T(8,128)(2,1)} %param.31), kind=kOutput, calls=%fused_computation.7 | convolution fusion | flops 3779592192 | bytes 29494272 | tf_op jit(solution)/shard_map/dot_general | solution.py:79
  243.1 5.5 convolution_convert_fusion.1
  254.6 42.0 %reduce-scatter.15.cloned.1.call-done = bf16[768,768]{1,0:T(8,128)(2,1)} async-done(((bf16[3072,768]{1,0:T(8,128)(2,1)}), bf16[768,768]{1,0:T(8,128)(2,1)}) %reduce-scatter.15.cloned.1.call-update) | async-done | bytes 1179664 | tf_op jit(solution)/shard_map/reduce_scatter | solution.py:83
  296.6 2.7 fusion.111
  300.6 41.4 %all-gather = bf16[96,1,768]{2,1,0:T(2,128)(2,1)S(1)} all-gather(bf16[3,1,768]{2,1,0:T(2,128)(2,1)S(1)} %slice.245), channel_id=2, replica_groups=mesh['dp'=8,'tensor'=4] {'dp','tensor'}, dimensions={0}, use_global_device_ids=true | all-gather | bytes 152064 | tf_op jit(solution)/shard_map/all_gather | solution.py:273
  352.8 3.0 convert_reduce_fusion.8
  355.9 3.9 copy_convert_fusion
  359.8 114.8 %all-reduce.7.cloned.1.call-done = f32[96,768]{1,0:T(8,128)} async-done(((f32[96,768]{1,0:T(8,128)}), f32[96,768]{1,0:T(8,128)}) %all-reduce.7.cloned.1.call-update) | async-done | bytes 294928
  476.1 3.9 copy.229
  485.2 3.2 fusion.8
  488.4 2.8 convert_reduce_fusion.4
  491.3 3.9 all-gather.18.cloned.1.call-done
  495.2 5.5 convert_reduce_fusion.3
  503.1 31.8 %all-gather.22.cloned.1.call-done = bf16[3072,768]{1,0:T(8,128)(2,1)} async-done(((bf16[768,768]{1,0:T(8,128)(2,1)}), bf16[3072,768]{1,0:T(8,128)(2,1)}) %all-gather.22.cloned.1.call-update) | async-done | bytes 4718608 | tf_op jit(solution)/shard_map/all_gather | solution.py:148
  534.9 13.6 %convert_reduce_fusion = (f32[768]{0:T(1024)}, bf16[3072,768]{1,0:T(8,128)(2,1)S(1)}) fusion(f32[3072,768]{1,0:T(8,128)} %get-tuple-element.98, bf16[3072,768]{1,0:T(8,128)(2,1)} %all-gather.22.cloned.1.call-done, bf16[2,768,768]{2,1,0:T(8,128)(2,1)} %param.33, f32[3072,768]{1,0:T(8,128)} %get-tuple-element.114, f32[768]{0:T(1024)S(1)} %copy-done.91), kind=kOutput, calls=%fused_computation.3 | convolution fusion | flops 3663985920 | bytes 29497344 | tf_op jit(solution)/shard_map/dot_general | solution.py:150
  550.7 5.6 convolution_convert_fusion
  556.3 7.4 reduce-scatter.17.cloned.1.call-done
  568.4 46.4 %reduce-scatter.21.cloned.1.call-done = bf16[768,768]{1,0:T(8,128)(2,1)} async-done(((bf16[3072,768]{1,0:T(8,128)(2,1)}), bf16[768,768]{1,0:T(8,128)(2,1)}) %reduce-scatter.21.cloned.1.call-update) | async-done | bytes 1179664 | tf_op jit(solution)/shard_map/reduce_scatter | solution.py:155
  614.8 3.6 multiply_reduce_fusion.3
  621.5 12.8 %all-gather.20.cloned.1.call-done = bf16[768,768]{1,0:T(8,128)(2,1)} async-done(((bf16[192,768]{1,0:T(8,128)(2,1)}), bf16[768,768]{1,0:T(8,128)(2,1)}) %all-gather.20.cloned.1.call-update) | async-done | bytes 1179664 | tf_op jit(solution)/shard_map/all_gather | solution.py:170
  650.0 3.6 bitcast_convert_fusion.1
  653.9 20.0 %all-gather.24.cloned.1.call-done = bf16[3072,768]{1,0:T(8,128)(2,1)} async-done(((bf16[768,768]{1,0:T(8,128)(2,1)}), bf16[3072,768]{1,0:T(8,128)(2,1)}) %all-gather.24.cloned.1.call-update) | async-done | bytes 4718608 | tf_op jit(solution)/shard_map/all_gather | solution.py:170
  673.9 5.0 convolution_convert_fusion.3
  681.5 8.3 multiply_reduce_fusion
  689.8 11.5 multiply_convert_fusion
  701.3 3.7 convert_reduce_fusion.2
  714.2 6.0 convert_reduce_fusion.1
  726.1 5.6 bitcast_convert_fusion
  738.8 8.4 convolution_bitcast_fusion.2
  747.2 2.7 pad_maximum_fusion
  750.0 3.9 convolution_bitcast_fusion.1
  758.9 2.9 convolution_bitcast_fusion.5
  767.5 42.8 %all-reduce.1 = (f32[2,2,768]{2,1,0:T(2,128)}, f32[2,2,768]{2,1,0:T(2,128)}, f32[2,2,768]{2,1,0:T(2,128)}) all-reduce(f32[2,2,768]{2,1,0:T(2,128)S(1)} %pad_maximum_fusion.4, f32[2,2,768]{2,1,0:T(2,128)S(1)} %pad_maximum_fusion.5, f32[2,2,768]{2,1,0:T(2,128)S(1)} %pad_maximum_fusion.6), channel_id=1, replica_groups=mesh['dp'=8,'tensor'=4] {'dp','tensor'}, use_global_device_ids=true, to_apply=%region_46.0 | all-reduce | flops 9216 | bytes 73728 | tf_op jit(solution)/shard_map/psum | solution.py:333
  810.4 39.0 %all-reduce.2 = (f32[2,2,192]{2,1,0:T(2,128)}, f32[2,768]{1,0:T(2,128)}) all-reduce(f32[2,2,192]{2,1,0:T(2,128)S(1)} %pad_maximum_fusion.8, f32[2,768]{1,0:T(2,128)S(1)} %pad_maximum_fusion.7), channel_id=1, replica_groups=mesh['dp'=8,'tensor'=4] {'dp'}, use_global_device_ids=true, to_apply=%region_40.0 | all-reduce | flops 2304 | bytes 18432 | tf_op jit(solution)/shard_map/psum | solution.py:229
  852.0 375.5 %all-reduce.9.cloned.1.call-done = (f32[2,3,768,192]{2,3,1,0:T(8,128)}, f32[2,192,768]{2,1,0:T(8,128)}, f32[2,768,768]{2,1,0:T(8,128)}, f32[2,768,768]{2,1,0:T(8,128)}) async-done(((f32[2,3,768,192]{2,3,1,0:T(8,128)}, f32[2,192,768]{2,1,0:T(8,128)}, f32[2,768,768]{2,1,0:T(8,128)}, f32[2,768,768]{2,1,0:T(8,128)}), (f32[2,3,768,192]{2,3,1,0:T(8,128)}, f32[2,192,768]{2,1,0:T(8,128)}, f32[2,768,768]{2,1,0:T(8,128)}, ...) | async-done | bytes 14155792 | tf_op jit(solution)/shard_map/psum | solution.py:229
  1227.4 4.3 copy.322
  (456 shorter events, 136.9 us)
Async XLA Ops:
  7.2 22.6 %all-gather.10.cloned.1.call-start = ((), (), s32[]{:S(2)}) async-start(), calls=%async_computation.8 | async-start | bytes 1474560 | tf_op jit(solution)/shard_map/all_gather | solution.py:43
  7.9 60.9 %all-gather.14.cloned.1.call-start = ((), (), s32[]{:S(2)}) async-start(), calls=%async_computation.12 | async-start | bytes 5898240 | tf_op jit(solution)/shard_map/all_gather | solution.py:43
  8.7 100.6 %reduce-scatter.9.cloned.1.call-start = ((), (), s32[]{:S(2)}) async-start(), calls=%async_computation.9 | async-start | bytes 1474560 | tf_op jit(solution)/shard_map/reduce_scatter | solution.py:66
  40.1 33.8 %copy-start.36 = (bf16[768,192]{0,1:T(8,128)(2,1)}, bf16[768,192]{0,1:T(8,128)(2,1)S(1)}, u32[]{:S(2)}) copy-start(bf16[768,192]{0,1:T(8,128)(2,1)S(1)} %reshape.501) | copy-start | bytes 884740
  41.6 113.7 %reduce-scatter.13.cloned.1.call-start = ((), (), s32[]{:S(2)}) async-start(), calls=%async_computation.13 | async-start | bytes 5898240 | tf_op jit(solution)/shard_map/reduce_scatter | solution.py:66
  107.3 48.1 %copy-start.2 = (bf16[3,256,768]{2,1,0:T(8,128)(2,1)S(1)}, bf16[3,256,768]{2,1,0:T(8,128)(2,1)}, u32[]{:S(2)}) copy-start(bf16[3,256,768]{2,1,0:T(8,128)(2,1)} %param.20) | copy-start | bytes 3538948
  107.3 67.5 %all-gather.12.cloned.1.call-start = ((), (), s32[]{:S(2)}) async-start(), calls=%async_computation.10 | async-start | bytes 1474560 | tf_op jit(solution)/shard_map/all_gather | solution.py:78
  109.2 48.7 %copy-start.69 = (f32[768]{0:T(1024)}, f32[768]{0:T(1024)S(1)}, u32[]{:S(2)}) copy-start(f32[768]{0:T(1024)S(1)} %get-tuple-element.61) | copy-start | bytes 9220
  109.2 143.3 %copy-start.56 = (f32[768]{0:T(1024)}, f32[768]{0:T(1024)S(1)}, u32[]{:S(2)}) copy-start(f32[768]{0:T(1024)S(1)} %get-tuple-element.135) | copy-start | bytes 9220
  111.6 46.3 %copy-start.89 = (f32[192]{0:T(256)}, f32[192]{0:T(256)S(1)}, u32[]{:S(2)}) copy-start(f32[192]{0:T(256)S(1)} %add_rsqrt_fusion.3) | copy-start | bytes 2308
  113.5 137.7 %copy-start.20 = (f32[192,768]{1,0:T(8,128)}, f32[192,768]{1,0:T(8,128)S(1)}, u32[]{:S(2)}) copy-start(f32[192,768]{1,0:T(8,128)S(1)} %get-tuple-element.104) | copy-start | bytes 1769476
  113.5 100.9 %all-gather.16.cloned.1.call-start = ((), (), s32[]{:S(2)}) async-start(), calls=%async_computation.14 | async-start | bytes 5898240 | tf_op jit(solution)/shard_map/all_gather | solution.py:78
  159.7 91.5 %reduce-scatter.11.cloned.1.call-start = ((), (), s32[]{:S(2)}) async-start(), calls=%async_computation.11 | async-start | bytes 1474560 | tf_op jit(solution)/shard_map/reduce_scatter | solution.py:83
  159.8 24.7 %copy-start.92 = (f32[768]{0:T(1024)}, f32[768]{0:T(1024)S(1)}, u32[]{:S(2)}) copy-start(f32[768]{0:T(1024)S(1)} %get-tuple-element.67) | copy-start | bytes 9220
  159.8 54.5 %copy-start.90 = (f32[768]{0:T(1024)}, f32[768]{0:T(1024)S(1)}, u32[]{:S(2)}) copy-start(f32[768]{0:T(1024)S(1)} %get-tuple-element.66) | copy-start | bytes 9220
  186.6 110.1 %reduce-scatter.15.cloned.1.call-start = ((), (), s32[]{:S(2)}) async-start(), calls=%async_computation.15 | async-start | bytes 5898240 | tf_op jit(solution)/shard_map/reduce_scatter | solution.py:83
  214.3 28.8 %copy-start.101 = (bf16[2,768,768]{2,1,0:T(8,128)(2,1)S(1)}, bf16[2,768,768]{2,1,0:T(8,128)(2,1)}, u32[]{:S(2)}) copy-start(bf16[2,768,768]{2,1,0:T(8,128)(2,1)} %param.33) | copy-start | bytes 7077892
  248.6 226.0 %all-reduce.7.cloned.1.call-start = ((), (), s32[]{:S(2)}) async-start(), calls=%async_computation.24 | async-start | bytes 589824
  252.3 44.3 %copy-start.70 = (f32[192]{0:T(256)}, f32[192]{0:T(256)S(1)}, u32[]{:S(2)}) copy-start(f32[192]{0:T(256)S(1)} %broadcast_multiply_fusion.10) | copy-start | bytes 2308
  252.6 44.1 %copy-start.76 = (f32[192]{0:T(256)}, f32[192]{0:T(256)S(1)}, u32[]{:S(2)}) copy-start(f32[192]{0:T(256)S(1)} %add_rsqrt_fusion.2) | copy-start | bytes 2308
  299.8 42.2 %copy-start.71 = (bf16[3,1,768]{2,1,0:T(2,128)(2,1)S(1)}, bf16[3,1,768]{2,1,0:T(2,128)(2,1)}, u32[]{:S(2)}) copy-start(bf16[3,1,768]{2,1,0:T(2,128)(2,1)} %slice.244) | copy-start | bytes 13828
  299.8 42.4 %copy-start.75 = (f32[3,96]{1,0:T(4,128)S(1)}, f32[3,96]{1,0:T(4,128)}, u32[]{:S(2)}) copy-start(f32[3,96]{1,0:T(4,128)} %convert_reduce_fusion.10) | copy-start | bytes 3460
  299.8 42.6 %copy-start.22 = (f32[3,64,768]{2,0,1:T(4,128)S(1)}, f32[3,64,768]{2,0,1:T(4,128)}, u32[]{:S(2)}) copy-start(f32[3,64,768]{2,0,1:T(4,128)} %copy_convert_fusion.1) | copy-start | bytes 1769476
  299.9 43.8 %copy-start.67 = (f32[768]{0:T(1024)}, f32[768]{0:T(1024)S(1)}, u32[]{:S(2)}) copy-start(f32[768]{0:T(1024)S(1)} %add_rsqrt_fusion) | copy-start | bytes 9220
  300.1 43.5 %copy-start.57 = (f32[768]{0:T(1024)S(1)}, f32[768]{0:T(1024)}, u32[]{:S(2)}) copy-start(f32[768]{0:T(1024)} %copy-done.56) | copy-start | bytes 9220
  300.5 44.0 %copy-start.41 = (bf16[768,768]{1,0:T(8,128)(2,1)}, bf16[768,768]{1,0:T(8,128)(2,1)S(1)}, u32[]{:S(2)}) copy-start(bf16[768,768]{1,0:T(8,128)(2,1)S(1)} %add_convert_fusion.5) | copy-start | bytes 3538948
  352.7 142.4 %all-gather.18.cloned.1.call-start = ((), (), s32[]{:S(2)}) async-start(), calls=%async_computation.16 | async-start | bytes 1474560 | tf_op jit(solution)/shard_map/all_gather | solution.py:148
  355.8 179.0 %all-gather.22.cloned.1.call-start = ((), (), s32[]{:S(2)}) async-start(), calls=%async_computation.20 | async-start | bytes 5898240 | tf_op jit(solution)/shard_map/all_gather | solution.py:148
  491.2 72.6 %reduce-scatter.17.cloned.1.call-start = ((), (), s32[]{:S(2)}) async-start(), calls=%async_computation.17 | async-start | bytes 1474560 | tf_op jit(solution)/shard_map/reduce_scatter | solution.py:155
  500.7 34.2 %copy-start.91 = (f32[768]{0:T(1024)S(1)}, f32[768]{0:T(1024)}, u32[]{:S(2)}) copy-start(f32[768]{0:T(1024)} %copy-done.90) | copy-start | bytes 9220
  502.8 111.9 %reduce-scatter.21.cloned.1.call-start = ((), (), s32[]{:S(2)}) async-start(), calls=%async_computation.21 | async-start | bytes 5898240 | tf_op jit(solution)/shard_map/reduce_scatter | solution.py:155
  534.9 15.8 %copy-start.103 = (bf16[2,768,768]{2,1,0:T(8,128)(2,1)S(1)}, bf16[2,768,768]{2,1,0:T(8,128)(2,1)}, u32[]{:S(2)}) copy-start(bf16[2,768,768]{2,1,0:T(8,128)(2,1)} %param.31) | copy-start | bytes 7077892
  556.3 58.5 %copy-start.4 = (bf16[768,768]{1,0:T(8,128)(2,1)S(1)}, bf16[768,768]{1,0:T(8,128)(2,1)}, u32[]{:S(2)}) copy-start(bf16[768,768]{1,0:T(8,128)(2,1)} %reduce-scatter.13.cloned.1.call-done) | copy-start | bytes 3538948
  556.3 78.0 %all-gather.20.cloned.1.call-start = ((), (), s32[]{:S(2)}) async-start(), calls=%async_computation.18 | async-start | bytes 1474560 | tf_op jit(solution)/shard_map/all_gather | solution.py:170
  568.3 105.5 %all-gather.24.cloned.1.call-start = ((), (), s32[]{:S(2)}) async-start(), calls=%async_computation.22 | async-start | bytes 5898240 | tf_op jit(solution)/shard_map/all_gather | solution.py:170
  618.4 15.9 %copy-start.49 = (bf16[2,192,768]{2,1,0:T(8,128)(2,1)S(1)}, bf16[2,192,768]{2,1,0:T(8,128)(2,1)}, u32[]{:S(2)}) copy-start(bf16[2,192,768]{2,1,0:T(8,128)(2,1)} %param.27) | copy-start | bytes 1769476
  621.0 16.3 %copy-start.6 = (f32[12,3,64,64]{2,3,1,0:T(8,128)S(1)}, f32[12,3,64,64]{2,3,1,0:T(8,128)}, u32[]{:S(2)}) copy-start(f32[12,3,64,64]{2,3,1,0:T(8,128)} %copy-done.5) | copy-start | bytes 1769476
  621.0 16.3 %copy-start.25 = (bf16[12,64,3,64]{3,1,2,0:T(8,128)(2,1)S(1)}, bf16[12,64,3,64]{3,1,2,0:T(8,128)(2,1)}, u32[]{:S(2)}) copy-start(bf16[12,64,3,64]{3,1,2,0:T(8,128)(2,1)} %copy-done.24) | copy-start | bytes 884740
  621.0 16.3 %copy-start.46 = (f32[12,3,64]{2,1,0:T(4,128)S(1)}, f32[12,3,64]{2,1,0:T(4,128)}, u32[]{:S(2)}) copy-start(f32[12,3,64]{2,1,0:T(4,128)} %copy-done.45) | copy-start | bytes 27652
  621.1 144.5 %reduce-scatter.19.cloned.1.call-start = ((), (), s32[]{:S(2)}) async-start(), calls=%async_computation.19 | async-start | bytes 1474560 | tf_op jit(solution)/shard_map/reduce_scatter | solution.py:206
  650.0 23.9 %copy-start.50 = (bf16[2,192,768]{2,1,0:T(8,128)(2,1)S(1)}, bf16[2,192,768]{2,1,0:T(8,128)(2,1)}, u32[]{:S(2)}) copy-start(bf16[2,192,768]{2,1,0:T(8,128)(2,1)} %param.27) | copy-start | bytes 1769476
  653.7 195.8 %reduce-scatter.23.cloned.1.call-start = ((), (), s32[]{:S(2)}) async-start(), calls=%async_computation.23 | async-start | bytes 5898240 | tf_op jit(solution)/shard_map/reduce_scatter | solution.py:206
  689.8 11.5 copy-start.13
  731.7 495.7 %all-reduce.9.cloned.1.call-start = ((), (), s32[]{:S(2)}) async-start(), calls=%async_computation.25 | async-start | bytes 28311552 | tf_op jit(solution)/shard_map/psum | solution.py:229
  736.9 13.0 %slice-start.10 = ((s8[4718592]{0:T(1024)(128)(4,1)}), s8[4194304]{0:T(1024)(128)(4,1)S(1)}, s32[]{:S(2)}) async-start(s8[4718592]{0:T(1024)(128)(4,1)} %bitcast.286), calls=%async_computation.36 | async-start | bytes 8388608
  737.9 12.0 slice-start.8
  747.2 11.7 slice-start.4
  764.0 85.4 %copy-start.19 = (f32[768,768]{1,0:T(8,128)S(1)}, f32[768,768]{1,0:T(8,128)}, u32[]{:S(2)}) copy-start(f32[768,768]{1,0:T(8,128)} %get-tuple-element.91) | copy-start | bytes 7077892
  (96 other events, 276.6 us)
Sparse Core Ops, SparseCore 0:
  9.6 20.1 all-gather.9
  31.3 37.4 all-gather.13
  72.0 25.7 reduce-scatter.8
  107.4 47.9 reduce-scatter.12
  157.4 17.4 all-gather.11
  176.8 37.4 all-gather.15
  217.5 25.7 reduce-scatter.10
  248.8 47.8 reduce-scatter.14
  352.9 121.7 all-reduce.6
  476.7 18.3 all-gather.17
  497.4 37.4 all-gather.21
  538.0 25.6 reduce-scatter.16
  566.9 47.8 reduce-scatter.20
  616.8 17.4 all-gather.19
  636.4 37.4 all-gather.23
  677.0 25.7 reduce-scatter.18
  731.9 48.3 reduce-scatter.22
  786.7 440.7 all-reduce.8
where the time goes:
time: 1260 us; the launch traced here: 1250 us
  waiting for transfers between devices  788 us (63%)
  matrix products  155 us (12%)
  blocking collectives  123 us (10%)
  other arithmetic  84.8 us (7%)
  local copies, waits for them, and re-layouts  77.3 us (6%)
  between operations  16.4 us (1%)
    psum x1, waiting for transfers between devices, whole_sum(): lax.psum((parts[0], parts[1], parts[2], parts[3], parts[4], parts[5]), 'dp')  375 us
    unnamed x19, waiting for transfers between devices  116 us
    reduce_scatter x2, waiting for transfers between devices, encoder_backward(): lax.psum_scatter(jnp.dot(upper_back, up_weight.T, preferred_element_type=...  53.8 us
    all_gather x2, waiting for transfers between devices, encoder_forward(): gathered = lax.all_gather(tokens_share, 'tensor', axis=0, tiled=True)  47.1 us
    psum x1, blocking collectives, body(): lax.psum((gain_stack, shift_stack, bias_stack), ('dp', 'tensor'))  42.8 us
    all_gather x2, waiting for transfers between devices, encoder_forward(): lax.all_gather(normed.astype(jnp.bfloat16), 'tensor', axis=0, tiled=True)  42.8 us
    reduce_scatter x2, waiting for transfers between devices, encoder_forward(): lax.psum_scatter(jnp.dot(lax.slice_in_dim(active, 0, lax.axis_size('tenso...  42 us
    reduce_scatter x2, waiting for transfers between devices, encoder_forward(): lax.psum_scatter(jnp.dot(mixed_rows, attention_out, preferred_element_typ...  41.8 us
  transfers between devices with their start and end apart: 18, of which 14 were waited for; matrix products, arithmetic and copies ran while one was open for 22% of the time, Pallas kernels for 0%

commit v1 on v0

v1 whole, which is shorter than its diff:
```python
import functools

import jax
import jax.numpy as jnp
from jax import lax
from jax.experimental import pallas as pl
from jax.experimental.pallas import tpu as pltpu
from jax.sharding import PartitionSpec as P

D = 768
MESH = pl.DeviceIdType.MESH
bf16, f32 = jnp.bfloat16, jnp.float32
VM = pl.BlockSpec(memory_space=pltpu.VMEM)
ANY = pl.BlockSpec(memory_space=pl.ANY)
SDS = jax.ShapeDtypeStruct


def place():
    dp, t = lax.axis_index("dp"), lax.axis_index("tensor")
    return dict(dp=dp, t=t, x=lax.div(t, 2), c=lax.rem(t, 2), y=lax.rem(dp, 2),
                z=lax.rem(lax.div(dp, 2), 4), o=lax.div(dp, 8))


def device(p, c=None, x=None, y=None, z=None, o=None):
    g = lambda v, k: p[k] if v is None else v
    return (g(o, "o") * 8 + g(z, "z") * 2 + g(y, "y"), g(x, "x") * 2 + g(c, "c"))


def greet(peers):
    bar = pltpu.get_barrier_semaphore()
    for q in peers:
        pl.semaphore_signal(bar, inc=1, device_id=q, device_id_type=MESH)
    pl.semaphore_wait(bar, len(peers))


def remote(src, dst, ssem, rsem, dev):
    return pltpu.make_async_remote_copy(src, dst, ssem, rsem, device_id=dev, device_id_type=MESH)


R = 64
MACRO = 256
HALF = D // 2
MACROS = 18
STEPS = MACROS * 4 + 1
LAG = dict(c=2, x=2, y=2, z=2, a=2)


def sum_kernel(outer, *refs):
    ops, refs = refs[:17], refs[17:]
    (out_ref, small_ref, made, crecv, xsend, xkeep, xrecv, ysend, ykeep, yrecv, zsend, zrecv, fin, osend, orecv,
     c_ss, c_rs, x_ss, x_rs, y_ss, y_rs, z_ss, z_rs, a_ss, a_rs, o_ss, o_rs, w_ss, w_rs, l_sem, t_ss, t_rs) = refs
    first_ref, per_encoder = ops[0], (ops[9:17], ops[1:9])
    p = place()
    sib, xp, yp = device(p, c=1 - p["c"]), device(p, x=1 - p["x"]), device(p, y=1 - p["y"])
    zs = [lax.rem(p["z"] + j, 4) for j in (1, 2, 3)]
    zp = [device(p, z=v) for v in zs]
    op = [device(p, o=lax.rem(p["o"] + j, outer)) for j in range(1, outer)]
    diag = device(p, x=1 - p["x"], c=1 - p["c"])
    greet([sib, xp, yp, diag] + zp + op)
    dc, dx, dy, dz, da = (LAG[k] for k in "cxyza")
    lx = dc
    ly = lx + dx
    lz = ly + dy
    la = lz + dz
    lf = la + da
    m16 = lambda v, n: pl.ds(pl.multiple_of(v, 16), n)

    def made_at(u, c):
        return made.at[lax.rem(lax.div(u, 4), 2), :, c, m16(lax.rem(u, 4) * R, R)]

    def c_copy(u):
        k = lax.rem(u, 2 * dc)
        return remote(made_at(u, 1 - p["c"]), crecv.at[k], c_ss.at[k], c_rs.at[k], sib)

    def x_copy(u):
        k = lax.rem(u, 2 * dx)
        return remote(xsend.at[k], xrecv.at[k], x_ss.at[k], x_rs.at[k], xp)

    def y_copy(u):
        k = lax.rem(u, 2 * dy)
        return remote(ysend.at[k], yrecv.at[k], y_ss.at[k], y_rs.at[k], yp)

    def z_copy(u, j):
        k = lax.rem(u, 2 * dz)
        return remote(zsend.at[k, m16(zs[j] * 16, 16)], zrecv.at[k, 2 - j], z_ss.at[k, j], z_rs.at[k, 2 - j], zp[j])

    def z_wait(u):
        k = lax.rem(u, 2 * dz)
        for j in range(3):
            c = remote(zsend.at[k, m16(0, 16)], zrecv.at[k, j], z_ss.at[k, j], z_rs.at[k, j], zp[j])
            c.wait_send()
            c.wait_recv()

    def a_copy(u, j):
        k = lax.rem(u, 3 * da)
        a = fin.at[k, m16(p["z"] * 16, 16)]
        return remote(a, a, a_ss.at[k, j], a_rs.at[k, 2 - j], zp[j])

    def a_wait(u):
        k = lax.rem(u, 3 * da)
        for j in range(3):
            a = fin.at[k, m16(0, 16)]
            c = remote(a, a, a_ss.at[k, j], a_rs.at[k, j], zp[j])
            c.wait_send()
            c.wait_recv()

    def target(u):
        m = lax.div(u, 4)
        g = lax.div(m, 3)
        spot_ = jnp.where(m == MACROS, MACROS, (lax.rem(g, 3) * 2 + 1 - lax.div(g, 3)) * 3 + lax.rem(m, 3))
        return out_ref.at[spot_, m16(lax.rem(u, 4) * R, R), pl.ds(pl.multiple_of(p["y"] * HALF, 128), HALF)]

    def w_remote(u):
        k = lax.rem(u, 3 * da)
        return remote(fin.at[k], target(u), w_ss.at[k], w_rs.at[k], yp)

    def w_local(u):
        k = lax.rem(u, 3 * da)
        return pltpu.make_async_copy(fin.at[k], target(u), l_sem.at[k])

    def when(u, fn):
        @pl.when(jnp.logical_and(u >= 0, u < STEPS))
        def _():
            fn(u)

    def finish(u):
        a_wait(u)
        w_remote(u).start()
        w_local(u).start()

    def finished(u):
        c = w_remote(u)
        c.wait_send()
        c.wait_recv()
        w_local(u).wait()

    def take_z(u):
        z_wait(u)
        k = lax.rem(u, 2 * dz)
        mine = m16(p["z"] * 16, 16)
        v = zsend[k, mine].astype(f32)
        for j in range(3):
            v = v + zrecv[k, j].astype(f32)
        if outer > 1:
            osend[...] = v.astype(bf16)
            for j in range(outer - 1):
                remote(osend, orecv.at[outer - 2 - j], o_ss.at[j], o_rs.at[outer - 2 - j], op[j]).start()
            for j in range(outer - 1):
                c = remote(osend, orecv.at[j], o_ss.at[j], o_rs.at[j], op[j])
                c.wait_send()
                c.wait_recv()
            v = osend[...].astype(f32)
            for j in range(outer - 1):
                v = v + orecv[j].astype(f32)
        fin[lax.rem(u, 3 * da), mine] = v.astype(bf16)
        for j in range(3):
            a_copy(u, j).start()

    def take_y(u):
        c = y_copy(u)
        c.wait_send()
        c.wait_recv()
        k = lax.rem(u, 2 * dy)
        zsend[lax.rem(u, 2 * dz)] = (ykeep[k] + yrecv[k].astype(f32)).astype(bf16)
        for j in range(3):
            z_copy(u, j).start()

    def take_x(u):
        c = x_copy(u)
        c.wait_send()
        c.wait_recv()
        k = lax.rem(u, 2 * dx)
        ky = lax.rem(u, 2 * dy)
        ysend[ky] = (xkeep[k, 1 - p["y"]] + xrecv[k, 1 - p["y"]].astype(f32)).astype(bf16)
        y_copy(u).start()
        ykeep[ky] = xkeep[k, p["y"]] + xrecv[k, p["y"]].astype(f32)

    def take_c(u):
        c = c_copy(u)
        c.wait_send()
        c.wait_recv()
        k = lax.rem(u, 2 * dc)
        kx = lax.rem(u, 2 * dx)
        o = 1 - p["x"]
        own = lambda x: made[lax.rem(lax.div(u, 4), 2), x, p["c"], m16(lax.rem(u, 4) * R, R)].astype(f32)
        v = (own(o) + crecv[k, o].astype(f32)).astype(bf16)
        xsend[kx, 0] = v[:, :HALF]
        xsend[kx, 1] = v[:, HALF:]
        x_copy(u).start()
        v = own(p["x"]) + crecv[k, p["x"]].astype(f32)
        xkeep[kx, 0] = v[:, :HALF]
        xkeep[kx, 1] = v[:, HALF:]

    def make(m):
        slot = lax.rem(m, 2)
        g = lax.div(m, 3)
        r = lax.rem(m, 3)
        for e in (0, 1):
            gate_, df, hb, du, o, da_, dqkv, x_ = per_encoder[e]

            @pl.when(g == (1 - e) * 3)
            def _():
                cols = pl.ds(pl.multiple_of(r * MACRO, 128), MACRO)
                for t in range(4):
                    made[slot, t // 2, t % 2] = dot(gate_[t, :, cols], df[...], 0, 0).astype(bf16)

            @pl.when(g == (1 - e) * 3 + 1)
            def _():
                cols = pl.ds(pl.multiple_of(r * MACRO, 128), MACRO)
                for t in range(4):
                    made[slot, t // 2, t % 2] = dot(hb[:, cols], du[t], 0, 0).astype(bf16)

            for rr in range(3):
                @pl.when(m == ((1 - e) * 3 + 2) * 3 + rr)
                def _():
                    for t in range(4):
                        at = rr * MACRO
                        while at < (rr + 1) * MACRO:
                            j, off = at // 192, at % 192
                            n = min(192 - off, (rr + 1) * MACRO - at)
                            src = dqkv[j * D + t * 192 + off : j * D + t * 192 + off + n, :] if j < 3 else o[t * 192 + off : t * 192 + off + n, :]
                            made[slot, t // 2, t % 2, at - rr * MACRO : at - rr * MACRO + n] = dot(
                                src, x_[...] if j < 3 else da_[...], 1, 0).astype(bf16)
                            at += n

        @pl.when(m == MACROS)
        def _():
            made[slot, :, :, 0:R] = first_ref[...]

    def fetch(u):
        @pl.when(lax.rem(u, 4) == 0)
        def _():
            make(lax.div(u, 4))

        c_copy(u).start()

    def step(s, _):
        when(s - lf - da, finished)
        when(s - lf, finish)
        when(s - la, take_z)
        when(s - lz, take_y)
        when(s - ly, take_x)
        when(s - lx, take_c)
        when(s, fetch)
        return _

    lax.fori_loop(0, STEPS + lf + da, step, 0)
    x, c = p["x"], p["c"]
    own = out_ref.at[MACROS, pl.ds(0, 16)]
    sends = [remote(own, small_ref.at[x, c], t_ss.at[i], t_rs.at[i], dev) for i, dev in enumerate((sib, xp, diag))]
    for cp in sends:
        cp.start()
    mine = pltpu.make_async_copy(own, small_ref.at[x, c], l_sem.at[0])
    mine.start()
    mine.wait()
    for i, (a, b) in enumerate(((x, 1 - c), (1 - x, c), (1 - x, 1 - c))):
        sends[i].wait_send()
        remote(own, small_ref.at[a, b], t_ss.at[i], t_rs.at[i], sib).wait_recv()


def grad_sum(first, per_encoder, dp, cid=3):
    outer = dp // 8
    dma = pltpu.SemaphoreType.DMA
    dc, dx, dy, dz, da = (LAG[k] for k in "cxyza")
    no = max(outer - 1, 1)
    vm = pltpu.VMEM
    args = [first.reshape(2, 2, R, D)] + list(per_encoder[1]) + list(per_encoder[0])
    return pl.pallas_call(
        functools.partial(sum_kernel, outer),
        out_shape=(SDS((MACROS + 1, MACRO, D), bf16), SDS((2, 2, 16, D), bf16)),
        in_specs=[VM] * len(args),
        out_specs=(ANY, VM),
        scratch_shapes=[
            vm((2, 2, 2, MACRO, D), bf16), vm((2 * dc, 2, R, D), bf16),
            vm((2 * dx, 2, R, HALF), bf16), vm((2 * dx, 2, R, HALF), f32), vm((2 * dx, 2, R, HALF), bf16),
            vm((2 * dy, R, HALF), bf16), vm((2 * dy, R, HALF), f32), vm((2 * dy, R, HALF), bf16),
            vm((2 * dz, R, HALF), bf16), vm((2 * dz, 3, 16, HALF), bf16),
            vm((3 * da, R, HALF), bf16),
            vm((16, HALF), bf16), vm((no, 16, HALF), bf16),
            dma((2 * dc,)), dma((2 * dc,)), dma((2 * dx,)), dma((2 * dx,)),
            dma((2 * dy,)), dma((2 * dy,)), dma((2 * dz, 3)), dma((2 * dz, 3)),
            dma((3 * da, 3)), dma((3 * da, 3)), dma((no,)), dma((no,)),
            dma((3 * da,)), dma((3 * da,)), dma((3 * da,)), dma((3,)), dma((3,)),
        ],
        compiler_params=pltpu.CompilerParams(collective_id=cid, has_side_effects=True, vmem_limit_bytes=60 * 2**20),
    )(*args)


CH = 6
PLAN = ((0, 1), (1, 1), (2, 1), (0, 0), (1, 0), (2, 0))


def gather_kernel(io_ref, up_ref, down_ref, b_ref, out_ref, bias_ref, held, *sems):
    (x_ss, x_rs, y_ss, y_rs, z_ss, z_rs, y2_ss, y2_rs, z2_ss, z2_rs, sib_ss, sib_rs, f_ss, f_rs, b_ss, b_rs, in_sem, back_sem) = sems
    p = place()
    zb = lax.rem(p["z"], 2)
    sib, xp, yp = device(p, c=1 - p["c"]), device(p, x=1 - p["x"]), device(p, y=1 - p["y"])
    zp = device(p, z=p["z"] + 1 - 2 * zb)
    diag = device(p, x=1 - p["x"], c=1 - p["c"])
    greet([sib, xp, yp, zp, diag])
    x, c, y = p["x"], p["c"], p["y"]
    quarter, half = D // 4, D // 8
    rows = lambda q: pl.ds(pl.multiple_of(q * quarter, 16), quarter)
    hrows = lambda q, k: pl.ds(pl.multiple_of(q * quarter + k * half, 16), half)
    mine, qy, qz, dg = y * 2 + zb, (1 - y) * 2 + zb, y * 2 + 1 - zb, (1 - y) * 2 + 1 - zb
    source = lambda h: (io_ref, up_ref, down_ref)[PLAN[h][0]].at[PLAN[h][1]]
    started = []

    def go(cp):
        cp.start()
        started.append(cp)

    for i, dev in enumerate((sib, xp, diag)):
        go(remote(b_ref, bias_ref.at[x, c], b_ss.at[i], b_rs.at[i], dev))
    ins, backs = [], []
    for h in range(CH):
        go(remote(source(h).at[rows(mine)], out_ref.at[x, c, h, rows(mine)], x_ss.at[h], x_rs.at[h], xp))
        go(remote(source(h), out_ref.at[x, c, h], sib_ss.at[h], sib_rs.at[h], sib))
        ins.append(pltpu.make_async_copy(source(h), held.at[h], in_sem.at[h]))
        ins[h].start()
    bias_ref[x, c] = b_ref[...]
    for h in range(CH):
        ins[h].wait()
        backs.append(pltpu.make_async_copy(held.at[h], out_ref.at[x, c, h], back_sem.at[h]))
        backs[h].start()

    def whole(h, q, ss, rs, dev):
        a = out_ref.at[1 - x, c, h, rows(q)]
        return remote(a, a, ss, rs, dev)

    def part(h, q, k, ss, rs, dev):
        a = out_ref.at[1 - x, c, h, hrows(q, k)]
        return remote(a, a, ss.at[h], rs.at[h], dev)

    def first(h):
        whole(h, mine, x_ss.at[h], x_rs.at[h], xp).wait_recv()
        go(whole(h, mine, y_ss.at[h], y_rs.at[h], yp))
        go(whole(h, mine, z_ss.at[h], z_rs.at[h], zp))
        go(whole(h, mine, f_ss.at[h, 0], f_rs.at[h, 0], sib))

    def second(h):
        whole(h, qy, y_ss.at[h], y_rs.at[h], yp).wait_recv()
        go(part(h, qy, 1, z2_ss, z2_rs, zp))
        go(whole(h, qy, f_ss.at[h, 1], f_rs.at[h, 1], sib))
        whole(h, qz, z_ss.at[h], z_rs.at[h], zp).wait_recv()
        go(part(h, qz, 0, y2_ss, y2_rs, yp))
        go(whole(h, qz, f_ss.at[h, 2], f_rs.at[h, 2], sib))

    def third(h):
        part(h, dg, 0, y2_ss, y2_rs, yp).wait_recv()
        part(h, dg, 1, z2_ss, z2_rs, zp).wait_recv()
        go(whole(h, dg, f_ss.at[h, 3], f_rs.at[h, 3], sib))

    def arrived(h):
        a = out_ref.at[x, 1 - c, h]
        remote(a, a, sib_ss.at[h], sib_rs.at[h], sib).wait_recv()
        for i, q in enumerate((mine, qy, qz, dg)):
            a = out_ref.at[1 - x, 1 - c, h, rows(q)]
            remote(a, a, f_ss.at[h, i], f_rs.at[h, i], sib).wait_recv()
        backs[h].wait()

    for h in range(CH + 2):
        if h < CH:
            first(h)
        if 0 <= h - 1 < CH:
            second(h - 1)
        if 0 <= h - 2 < CH:
            third(h - 2)
    for h in range(CH):
        arrived(h)
    for cp in started:
        cp.wait_send()
    for i, (a, b) in enumerate(((x, 1 - c), (1 - x, c), (1 - x, 1 - c))):
        remote(b_ref, bias_ref.at[a, b], b_ss.at[i], b_rs.at[i], sib).wait_recv()


def weight_gather(io, up, down, bias_rows, cid=1):
    dma = pltpu.SemaphoreType.DMA
    return pl.pallas_call(
        gather_kernel,
        out_shape=(SDS((2, 2, CH, D, D), bf16), SDS((2, 2, 16, D), bf16)),
        in_specs=[ANY, ANY, ANY, VM],
        out_specs=(ANY, VM),
        scratch_shapes=[pltpu.VMEM((CH, D, D), bf16)] + [dma((CH,))] * 12 + [dma((CH, 4))] * 2 + [dma((3,))] * 2 + [dma((CH,))] * 2,
        compiler_params=pltpu.CompilerParams(collective_id=cid, has_side_effects=True, vmem_limit_bytes=32 * 2**20),
    )(io, up, down, bias_rows)


HD = 64
EPS = 1e-12


def dot(a, b, ca, cb):
    return lax.dot_general(a, b, (((ca,), (cb,)), ((), ())), preferred_element_type=f32)


def gelu_pair(u):
    a = jnp.abs(u) * 0.7071067811865476
    t = 1.0 / (1.0 + 0.3275911 * a)
    e = jnp.exp(-(a * a))
    poly = t * (0.254829592 + t * (-0.284496736 + t * (1.421413741 + t * (-1.453152027 + t * 1.061405429))))
    tail = 0.5 * poly * e
    cdf = jnp.where(u >= 0, 1.0 - tail, tail)
    return u * cdf, cdf + u * (e * 0.3989422804014327)


def loop(n, fn):
    def run(i, c):
        fn(i)
        return c

    lax.fori_loop(0, n, run, 0)


def norm(r, gain, shift):
    c = r - jnp.mean(r, axis=-1, keepdims=True)
    inv = lax.rsqrt(jnp.mean(c * c, axis=-1, keepdims=True) + EPS)
    n = c * inv
    return n * gain + shift, n, inv


def spot(seqs, length):
    tokens = seqs * length
    if length % 128 == 0:
        return length, seqs, 1
    return tokens, 1, seqs


W_SHAPES = ((3 * D, D), (D, D), (4, D, D), (4, D, D))


def load_weights(e, w_ref, win, wout, up, down, sem):
    base = 3 * (1 - e)
    q = D // 4
    kinds = [[], [], [], []]
    for t in range(4):
        src = w_ref.at[t // 2, t % 2]
        for j in range(3):
            kinds[0].append((src.at[base, pl.ds(j * q, q)], win.at[pl.ds(j * D + t * q, q)]))
        kinds[1].append((src.at[base, pl.ds(3 * q, q)], wout.at[pl.ds(t * q, q)]))
        kinds[2].append((src.at[base + 1], up.at[t]))
        kinds[3].append((src.at[base + 2], down.at[t]))
    n = 0
    copies = []
    for kind in kinds:
        copies.append([pltpu.make_async_copy(a, b, sem.at[n + i]) for i, (a, b) in enumerate(kind)])
        n += len(kind)

    def ready(k):
        for cp in copies[k]:
            cp.wait()

    for kind in copies:
        for cp in kind:
            cp.start()
    return ready


def forward_kernel(e, seqs, length, x_ref, w_ref, bcol_ref, ub_ref, vec_ref,
                   y_ref, qkv_ref, p_ref, o_ref, n1_ref, i1_ref, hb_ref, g_ref, d_ref, n2_ref, i2_ref, h_s, f_s, win_ref, wout_ref, up_ref, down_ref, w_sem):
    ready = load_weights(e, w_ref, win_ref, wout_ref, up_ref, down_ref, w_sem)
    ready(0)
    group, groups, per = spot(seqs, length)
    tokens = seqs * length
    blocks = tokens // group
    span = lambda i, n: pl.ds(pl.multiple_of(i * n, n), n)
    vec = lambda i: vec_ref[i : i + 1, :]

    def project(i):
        r = span(i, 256)
        v = (dot(win_ref[r, :], x_ref[...], 1, 1) + bcol_ref[r, :]).astype(bf16)
        qkv_ref[r, :] = v * jnp.where(i < 3, 0.125, 1.0).astype(bf16)

    loop(9, project)
    ready(1)

    for g in range(groups):
        tok = slice(g * group, (g + 1) * group)

        def heads(i):
            for k in range(2):
                h = i * 2 + k
                q = qkv_ref[pl.ds(pl.multiple_of(h * HD, HD), HD), tok]
                kk = qkv_ref[pl.ds(pl.multiple_of(D + h * HD, HD), HD), tok]
                vv = qkv_ref[pl.ds(pl.multiple_of(2 * D + h * HD, HD), HD), tok]
                s = dot(kk, q, 0, 0)
                if per > 1:
                    a = lax.broadcasted_iota(jnp.int32, s.shape, 0) // length
                    b = lax.broadcasted_iota(jnp.int32, s.shape, 1) // length
                    s = jnp.where(a == b, s, -1e30)
                e = jnp.exp(s - jnp.max(s, axis=0, keepdims=True))
                p = (e * (1.0 / jnp.sum(e, axis=0, keepdims=True))).astype(bf16)
                p_ref[g * 12 + h] = p
                o_ref[pl.ds(pl.multiple_of(h * HD, HD), HD), tok] = dot(vv, p, 1, 0).astype(bf16)

        loop(6, heads)

    for b in range(blocks):
        tok = slice(b * group, (b + 1) * group)
        r = dot(o_ref[:, tok], wout_ref[...], 0, 0) + x_ref[tok, :].astype(f32) + vec(4)
        h, n, inv = norm(r, vec(0), vec(2))
        h_s[tok, :] = h
        hb_ref[tok, :] = h.astype(bf16)
        n1_ref[tok, :] = n.astype(bf16)
        i1_ref[tok, :] = inv

    ready(2)
    ready(3)

    def hidden(i):
        for b in range(blocks):
            tok = slice(b * group, (b + 1) * group)
            for k in range(3):
                c = slice(k * 256, (k + 1) * 256)
                u = dot(hb_ref[tok, :], up_ref[i, :, c], 1, 0) + ub_ref[i, :, c]
                g, d = gelu_pair(u)
                g_ref[i, tok, c] = g.astype(bf16)
                d_ref[i, tok, c] = d.astype(bf16)
            part = dot(g_ref[i, tok, :], down_ref[i], 1, 0)
            f_s[tok, :] = jnp.where(i == 0, part, f_s[tok, :] + part)

    loop(4, hidden)
    for b in range(blocks):
        tok = slice(b * group, (b + 1) * group)
        y, n, inv = norm(h_s[tok, :] + (f_s[tok, :] + vec(5)), vec(1), vec(3))
        y_ref[tok, :] = y.astype(bf16)
        n2_ref[tok, :] = n.astype(bf16)
        i2_ref[tok, :] = inv


def encoder_forward(e, x, w, bias_col, up_rows, vec):
    seqs, length, _ = x.shape
    t = seqs * length
    group, groups, _ = spot(seqs, length)
    outs = (SDS((t, D), bf16), SDS((3 * D, t), bf16), SDS((groups * 12, group, group), bf16), SDS((D, t), bf16), SDS((t, D), bf16), SDS((t, 1), f32),
            SDS((t, D), bf16), SDS((4, t, D), bf16), SDS((4, t, D), bf16), SDS((t, D), bf16), SDS((t, 1), f32))
    return pl.pallas_call(
        functools.partial(forward_kernel, e, seqs, length), out_shape=outs, in_specs=[VM, ANY, VM, VM, VM], out_specs=(VM,) * len(outs),
        scratch_shapes=[pltpu.VMEM((t, D), f32), pltpu.VMEM((t, D), f32)] + [pltpu.VMEM(s, bf16) for s in W_SHAPES] + [pltpu.SemaphoreType.DMA((24,))],
        compiler_params=pltpu.CompilerParams(vmem_limit_bytes=60 * 2**20),
    )(x.reshape(t, D), w, bias_col, up_rows, vec)


def norm_back(dz, n, inv):
    return inv * (dz - jnp.mean(dz, axis=-1, keepdims=True) - n * jnp.mean(dz * n, axis=-1, keepdims=True))


def backward_kernel(e, seqs, length, cot_ref, dc_ref, n2_ref, i2_ref, d_ref, w_ref, n1_ref, i1_ref,
                    qkv_ref, p_ref, vec_ref, df_ref, du_ref, da_ref, dqkv_ref, dx_ref, sum_ref, r2_s, r1_s, dh_s, do_s, win_ref, wout_ref, up_ref, down_ref, w_sem):
    ready = load_weights(e, w_ref, win_ref, wout_ref, up_ref, down_ref, w_sem)
    group, groups, per = spot(seqs, length)
    tokens = seqs * length
    blocks = tokens // group
    vec = lambda i: vec_ref[i : i + 1, :]
    col = lambda a: jnp.sum(a, axis=0, keepdims=True)
    sum_ref[...] = jnp.zeros_like(sum_ref)

    def add(row, v):
        sum_ref[row : row + 1, :] += v

    for b in range(blocks):
        tok = slice(b * group, (b + 1) * group)
        dy = cot_ref[tok, :].astype(f32)
        pos = lax.broadcasted_iota(jnp.int32, (group, 1), 0)
        for k in range(per):
            dy = dy + jnp.where(pos == k * length, dc_ref[b * per + k : b * per + k + 1, :], 0.0)
        n = n2_ref[tok, :].astype(f32)
        add(5, col(dy * n))
        add(7, col(dy))
        r2 = norm_back(dy * vec(1), n, i2_ref[tok, :])
        r2_s[tok, :] = r2
        df = r2.astype(bf16)
        df_ref[tok, :] = df
        add(3, col(df.astype(f32)))

    ready(3)
    ready(2)

    def hidden(i):
        for b in range(blocks):
            tok = slice(b * group, (b + 1) * group)
            for k in range(3):
                c = slice(k * 256, (k + 1) * 256)
                du = (dot(df_ref[tok, :], down_ref[i, c, :], 1, 1) * d_ref[i, tok, c].astype(f32)).astype(bf16)
                du_ref[i, tok, c] = du
                sum_ref[pl.ds(8 + i, 1), c] += col(du.astype(f32))
            part = dot(du_ref[i, tok, :], up_ref[i], 1, 1)
            dh_s[tok, :] = jnp.where(i == 0, part, dh_s[tok, :] + part)

    loop(4, hidden)
    for b in range(blocks):
        tok = slice(b * group, (b + 1) * group)
        dh = dh_s[tok, :] + r2_s[tok, :]
        n = n1_ref[tok, :].astype(f32)
        add(4, col(dh * n))
        add(6, col(dh))
        r1 = norm_back(dh * vec(0), n, i1_ref[tok, :])
        r1_s[tok, :] = r1
        da = r1.astype(bf16)
        da_ref[tok, :] = da
        add(2, col(da.astype(f32)))

    span = lambda i, n: pl.ds(pl.multiple_of(i * n, n), n)

    def outward(i):
        do_s[span(i, 256), :] = dot(wout_ref[span(i, 256), :], da_ref[...], 1, 1).astype(bf16)

    ready(1)
    loop(3, outward)
    for g in range(groups):
        tok = slice(g * group, (g + 1) * group)

        def heads(i):
            for k in range(2):
                h = i * 2 + k
                at = lambda base: pl.ds(pl.multiple_of(base + h * HD, HD), HD)
                q, kk, vv, do = qkv_ref[at(0), tok], qkv_ref[at(D), tok], qkv_ref[at(2 * D), tok], do_s[at(0), tok]
                pb = p_ref[g * 12 + h]
                p = pb.astype(f32)
                dp = dot(vv, do, 0, 0)
                ds = (p * (dp - jnp.sum(p * dp, axis=0, keepdims=True))).astype(bf16)
                dqkv_ref[at(0), tok] = (dot(kk, ds, 1, 0) * 0.125).astype(bf16)
                dqkv_ref[at(D), tok] = dot(q, ds, 1, 1).astype(bf16)
                dqkv_ref[at(2 * D), tok] = dot(do, pb, 1, 1).astype(bf16)

        loop(6, heads)
    ready(0)
    ones = jnp.ones((8, tokens), bf16)
    add(0, dot(ones, dqkv_ref[0:D, :], 1, 1)[0:1])
    add(1, dot(ones, dqkv_ref[2 * D :, :], 1, 1)[0:1])
    for b in range(blocks):
        tok = slice(b * group, (b + 1) * group)
        dx_ref[tok, :] = (dot(dqkv_ref[:, tok], win_ref[...], 0, 0) + r1_s[tok, :]).astype(bf16)


def encoder_backward(e, cot, dc, kept, w, vec):
    seqs, length, _ = cot.shape
    t = seqs * length
    qkv, p, o, n1, i1, hb, g, d, n2, i2 = kept
    outs = (SDS((t, D), bf16), SDS((4, t, D), bf16), SDS((t, D), bf16), SDS((3 * D, t), bf16), SDS((t, D), bf16), SDS((16, D), f32))
    args = (cot.reshape(t, D), dc, n2, i2, d, w, n1, i1, qkv, p, vec)
    return pl.pallas_call(
        functools.partial(backward_kernel, e, seqs, length), out_shape=outs, in_specs=[VM] * 5 + [ANY] + [VM] * 5, out_specs=(VM,) * len(outs),
        scratch_shapes=[pltpu.VMEM((t, D), f32), pltpu.VMEM((t, D), f32), pltpu.VMEM((t, D), f32), pltpu.VMEM((D, t), bf16)] + [pltpu.VMEM(s, bf16) for s in W_SHAPES] + [pltpu.SemaphoreType.DMA((24,))],
        compiler_params=pltpu.CompilerParams(vmem_limit_bytes=60 * 2**20),
    )(*args)
def cls_kernel(n, own_ref, out_ref, a_ss, a_rs, b_ss, b_rs):
    dp, t = lax.axis_index("dp"), lax.axis_index("tensor")
    ring = [lax.rem(dp + j, n) for j in range(1, n)]
    group = [lax.rem(t + j, 4) for j in range(1, 4)]
    greet([(q, t) for q in ring] + [(dp, q) for q in group])
    out_ref[t, dp] = own_ref[...]
    first = [remote(own_ref, out_ref.at[t, dp], a_ss.at[j], a_rs.at[n - 2 - j], (q, t)) for j, q in enumerate(ring)]
    for cp in first:
        cp.start()
    for j, q in enumerate(ring):
        a = out_ref.at[t, q]
        remote(a, a, a_ss.at[j], a_rs.at[j], (q, t)).wait_recv()
    second = [remote(out_ref.at[t], out_ref.at[t], b_ss.at[j], b_rs.at[2 - j], (dp, q)) for j, q in enumerate(group)]
    for cp in second:
        cp.start()
    for j, q in enumerate(group):
        a = out_ref.at[q]
        remote(a, a, b_ss.at[j], b_rs.at[j], (dp, q)).wait_recv()
    for cp in first + second:
        cp.wait_send()


def cls_gather(own, n, cid=2):
    dma = pltpu.SemaphoreType.DMA
    return pl.pallas_call(
        functools.partial(cls_kernel, n),
        out_shape=jax.ShapeDtypeStruct((4, n, 16, D), bf16),
        in_specs=[pl.BlockSpec(memory_space=pltpu.VMEM)],
        out_specs=pl.BlockSpec(memory_space=pltpu.VMEM),
        scratch_shapes=[dma((n - 1,)), dma((n - 1,)), dma((3,)), dma((3,))],
        compiler_params=pltpu.CompilerParams(collective_id=cid, has_side_effects=True, vmem_limit_bytes=48 * 2**20),
    )(own)


def mm(a, b, dims):
    return lax.dot_general(a, b, (dims, ((), ())), preferred_element_type=f32)


def body(n_dp, questions, passages, question_cotangent, passage_cotangent, positives, positive_counts,
         attention_in, attention_bias, attention_out, branch_biases, norm_gains, norm_shifts, up_weight, up_bias, down_weight):
    q4 = D // 4
    io = jnp.concatenate([attention_in.transpose(0, 1, 3, 2).reshape(2, 3 * q4, D), attention_out], axis=1)
    bias_rows = jnp.concatenate([attention_bias.reshape(1, D), up_bias, jnp.zeros((13, D), bf16)])
    weights, biases = weight_gather(io, up_weight, down_weight, bias_rows)
    biases = biases.reshape(4, 16, D).astype(f32)
    full_att = biases[:, 0].reshape(4, 2, 2, q4).transpose(1, 2, 0, 3).reshape(2, 2, D)
    nothing = jnp.zeros((2, D), f32)
    kept, ys, vecs = [], [], []
    for e, x in enumerate((questions, passages)):
        vec = jnp.concatenate([norm_gains[e].astype(f32), norm_shifts[e].astype(f32), branch_biases[e].astype(f32), nothing])
        bias_col = jnp.concatenate([full_att[e, 0], nothing[0], full_att[e, 1]]).reshape(3 * D, 1)
        y, *k = encoder_forward(e, x, weights, bias_col, biases[:, 1 + e : 2 + e], vec)
        kept.append(k)
        ys.append(y)
        vecs.append(vec)
    nq, np_ = questions.shape[0], passages.shape[0]
    total = np_ * n_dp * 4
    cq = ys[0].reshape(questions.shape)[:, 0]
    cp = ys[1].reshape(passages.shape)[:, 0]
    live = jnp.arange(positives.shape[1], dtype=jnp.int32)[None, :] < positive_counts[:, None]
    marks = jnp.sum(((positives[:, :, None] == jnp.arange(D, dtype=jnp.int32)[None, None, :]) & live[:, :, None]).astype(f32), axis=1)
    payload = jnp.concatenate([cq, cp, marks.astype(bf16), jnp.zeros((16 - 2 * nq - np_, D), bf16)])
    every = cls_gather(payload, n_dp).transpose(1, 0, 2, 3).reshape(n_dp * 4, 16, D)
    all_q = every[:, :nq].reshape(-1, D)
    all_p = every[:, nq : nq + np_].reshape(-1, D)
    all_m = every[:, nq + np_ : 2 * nq + np_].reshape(-1, D)[:, :total].astype(f32)
    scale = 2.7 * D**-0.5
    scores = mm(all_q, all_p, ((1,), (1,))) * scale
    shifted = jnp.exp(scores - jnp.max(scores, axis=1, keepdims=True))
    all_total = jnp.sum(shifted, axis=1, keepdims=True)
    positive_total = jnp.sum(all_m * shifted, axis=1, keepdims=True)
    losses = (jnp.log(all_total) - jnp.log(positive_total))[:, 0]
    ds = (shifted / all_total - all_m * shifted / positive_total).astype(bf16)
    index = lax.axis_index("dp") * 4 + lax.axis_index("tensor")
    losses = lax.dynamic_slice_in_dim(losses, index * nq, nq, 0)
    dcq = mm(lax.dynamic_slice_in_dim(ds, index * nq, nq, 0), all_p, ((1,), (0,))) * scale
    dcp = mm(lax.dynamic_slice_in_dim(ds, index * np_, np_, 1), all_q, ((0,), (0,))) * scale
    dxs, operands, smalls = [], [], []
    for e, (cot, dc, x) in enumerate(((question_cotangent, dcq, questions), (passage_cotangent, dcp, passages))):
        dc = jnp.concatenate([dc, jnp.zeros((8 - dc.shape[0], D), f32)])
        df, du, da, dqkv, dx, s = encoder_backward(e, cot, dc, kept[e][:2] + [kept[e][2]] + kept[e][3:], weights, vecs[e])
        qkv, p, o, n1, i1, hb, g, d, n2, i2 = kept[e]
        dxs.append(dx)
        operands.append((g, df, hb, du, o, da, dqkv, x.reshape(-1, D)))
        smalls.append(s)
    both = jnp.stack(smalls)
    rows12 = jnp.concatenate([both[:, 2:4].reshape(4, D), both[:, 4:6].reshape(4, D), both[:, 6:8].reshape(4, D)]).reshape(4, 3, D)
    att = both[:, 0:2].reshape(2, 2, 4, q4).transpose(2, 0, 1, 3).reshape(4, 1, D)
    up = both[:, 8:12].transpose(1, 0, 2)
    first = jnp.concatenate([att, up, rows12, jnp.zeros((4, R - 6, D), f32)], axis=1).astype(bf16)
    out, small = grad_sum(first, operands, n_dp)
    res = out[:MACROS].reshape(3, 2, D, D)
    own_small = out[MACROS, :16].astype(f32)
    rep = small.reshape(4, 16, D)[:, 3:6].reshape(12, D).astype(f32)
    return (
        ys[0].reshape(questions.shape), ys[1].reshape(passages.shape), losses,
        dxs[0].reshape(questions.shape), dxs[1].reshape(passages.shape),
        res[2, :, : 3 * q4].reshape(2, 3, q4, D).transpose(0, 1, 3, 2).astype(f32), own_small[0].reshape(2, 2, q4),
        res[2, :, 3 * q4 :].astype(f32), rep[0:4].reshape(2, 2, D), rep[4:8].reshape(2, 2, D), rep[8:12].reshape(2, 2, D),
        res[1].astype(f32), own_small[1:3], res[0].astype(f32))


def solution(mesh):
    both = ("dp", "tensor")
    seq, rep = P(both, None, None), P()
    w4, w3, o3 = P(None, None, None, "tensor"), P(None, None, "tensor"), P(None, "tensor", None)
    in_specs = (seq, seq, seq, seq, P(both, None), P(both), w4, w3, o3, rep, rep, rep, w3, P(None, "tensor"), o3)
    out_specs = (seq, seq, P(both), seq, seq, w4, w3, o3, rep, rep, rep, w3, P(None, "tensor"), o3)
    return jax.shard_map(functools.partial(body, mesh.shape["dp"]), mesh=mesh, in_specs=in_specs, out_specs=out_specs, check_vma=False)
```

time: 1260 us -> 472 us (0.37)
  waiting for transfers between devices: 788 us -> 0 us
  Pallas kernels: 0 us -> 428 us
  matrix products: 155 us -> 0.6 us
  blocking collectives: 123 us -> 0 us
  other arithmetic: 84.8 us -> 16.7 us
  local copies, waits for them, and re-layouts: 77.3 us -> 22.8 us
  between operations: 16.4 us -> 1.17 us
    pallas_call x0 -> x7, Pallas kernels: none -> 428 us  [the longest x1 201 us: grad_sum(): pl.pallas_call(functools.partial(sum_kernel, outer), out_shape=(SDS((MACR...]
    psum x1 -> x0, waiting for transfers between devices: 375 us -> none  [whole_sum(): lax.psum((parts[0], parts[1], parts[2], parts[3], parts[4], parts[5]), 'dp')]
    all_gather x8 -> x0, waiting for transfers between devices: 158 us -> none  [the longest x2 47.1 us: encoder_forward(): gathered = lax.all_gather(tokens_share, 'tensor', axis=0, tiled=True)]
    dot_general x39 -> x3, matrix products: 155 us -> 0.6 us  [mm(): return lax.dot_general(a, b, (dims, ((), ())), preferred_element_type=f32)]
    reduce_scatter x8 -> x0, waiting for transfers between devices: 138 us -> none  [the longest x2 53.8 us: encoder_backward(): lax.psum_scatter(jnp.dot(upper_back, up_weight.T, preferred_element_type=...]
    unnamed x19 -> x0, waiting for transfers between devices: 116 us -> none
    psum x2 -> x0, blocking collectives: 81.8 us -> none  [the longest x1 42.8 us: body(): lax.psum((gain_stack, shift_stack, bias_stack), ('dp', 'tensor'))]
    all_gather x1 -> x0, blocking collectives: 41.4 us -> none  [body(): all_cls = lax.all_gather(passage_cls, ('dp', 'tensor'), axis=0, tiled=True)]
  transfers between devices with their start and end apart: 18 -> 0, of which waited for: 14 -> 0; matrix products, arithmetic and copies ran while one was open for 22% -> 0% of each run, Pallas kernels for 0% -> 0%
where the time goes in v1:
time: 472 us; the launch traced here: 469 us
  Pallas kernels  428 us (91%)
  local copies, waits for them, and re-layouts  22.8 us (5%)
  other arithmetic  16.7 us (4%)
    pallas_call x1, Pallas kernels, grad_sum(): pl.pallas_call(functools.partial(sum_kernel, outer), out_shape=(SDS((MACR...  201 us
    pallas_call x1, Pallas kernels, weight_gather(): pl.pallas_call(gather_kernel, out_shape=(SDS((2, 2, CH, D, D), bf16), SDS...  74.3 us
    pallas_call x2, Pallas kernels, encoder_backward(): pl.pallas_call(functools.partial(backward_kernel, e, seqs, length), out_s...  72.7 us
    pallas_call x2, Pallas kernels, encoder_forward(): pl.pallas_call(functools.partial(forward_kernel, e, seqs, length), out_sh...  62 us
    pallas_call x1, Pallas kernels, cls_gather(): pl.pallas_call(functools.partial(cls_kernel, n), out_shape=jax.ShapeDtype...  17.8 us

profile of v1, /device:TPU:0, one launch (start us, length us, event | category | flops | bytes accessed | tf_op | source)
XLA Modules:
  0.0 469.0 jit_solution(12093481785544477733)
XLA Ops:
  0.7 1.8 pad_maximum_fusion.io_ref
  2.8 1.7 copy-done
  4.4 1.7 copy-done.1
  6.1 74.3 %shard_map.254 = (bf16[2,2,6,768,768]{4,3,2,1,0:T(8,128)(2,1)}, bf16[2,2,16,768]{3,2,1,0:T(8,128)(2,1)S(1)}) custom-call(bf16[2,768,768]{2,1,0:T(8,128)(2,1)S(1)} %pad_maximum_fusion.io_ref, bf16[2,768,768]{2,1,0:T(8,128)(2,1)S(1)} %copy-done, bf16[2,768,768]{2,1,0:T(8,128)(2,1)S(1)} %copy-done.1, bf16[16,768]{1,0:T(8,128)(2,1)S(1)} %maximum_maximum_fusion.1.b_ref), custom_call_target="tpu_custom_call" | custom-call | tf_op jit(solution)/shard_map/pallas_call | solution.py:379
  80.4 0.6 fusion.12
  81.0 0.1 reshape_squeeze.7
  81.1 0.1 reshape.214
  81.3 1.4 reshape.249.bcol_ref
  82.8 0.7 maximum_maximum_fusion.3
  83.5 17.6 %shard_map.255 = (bf16[192,768]{1,0:T(8,128)(2,1)}, bf16[2304,192]{1,0:T(8,128)(2,1)}, bf16[12,192,192]{2,1,0:T(8,128)(2,1)}, bf16[768,192]{1,0:T(8,128)(2,1)}, ...) custom-call(bf16[192,768]{1,0:T(8,128)(2,1)} %bitcast.87, ...), custom_call_target="tpu_custom_call" | custom-call | tf_op jit(solution)/shard_map/pallas_call | solution.py:537
  101.1 1.4 reshape.250.bcol_ref
  102.5 44.4 %shard_map.256 = (bf16[768,768]{1,0:T(8,128)(2,1)}, bf16[2304,768]{1,0:T(8,128)(2,1)}, bf16[36,256,256]{2,1,0:T(8,128)(2,1)}, bf16[768,768]{1,0:T(8,128)(2,1)}, ...) custom-call(bf16[768,768]{1,0:T(8,128)(2,1)} %bitcast.82, ...), custom_call_target="tpu_custom_call" | custom-call | tf_op jit(solution)/shard_map/pallas_call | solution.py:537
  147.0 0.1 convert_reduce_fusion
  147.1 0.8 slice.166
  147.9 0.8 slice.165
  148.8 17.8 %shard_map.257 = bf16[4,8,16,768]{3,2,1,0:T(8,128)(2,1)S(1)} custom-call(bf16[16,768]{1,0:T(8,128)(2,1)S(1)} %maximum_maximum_fusion.4.own_ref), custom_call_target="tpu_custom_call" | custom-call | tf_op jit(solution)/shard_map/pallas_call | solution.py:671
  166.7 0.2 fusion.11
  166.9 0.1 reshape.221
  167.1 0.1 reshape.222
  167.2 0.2 fusion.14
  167.4 0.1 reshape.223
  167.5 0.1 copy.55
  167.7 0.6 dynamic_slice.9
  168.3 0.2 convolution_multiply_fusion.2
  168.6 0.6 concatenate.49.dc_ref
  169.2 18.7 %shard_map.258 = (bf16[192,768]{1,0:T(8,128)(2,1)}, bf16[4,192,768]{2,1,0:T(8,128)(2,1)}, bf16[192,768]{1,0:T(8,128)(2,1)}, bf16[2304,192]{1,0:T(8,128)(2,1)}, b...) custom-call(bf16[192,768]{1,0:T(8,128)(2,1)} %bitcast.89, f32[8,768]{1,0:T(8,128)} %concatenate.49.dc_ref, ...), custom_call_target="tpu_custom_call" | custom-call | tf_op jit(solution)/shard_map/pallas_call | solution.py:642
  187.9 0.1 convolution_multiply_fusion.1
  188.1 0.6 concatenate.50.dc_ref
  188.7 53.9 %shard_map.259 = (bf16[768,768]{1,0:T(8,128)(2,1)}, bf16[4,768,768]{2,1,0:T(8,128)(2,1)}, bf16[768,768]{1,0:T(8,128)(2,1)}, bf16[2304,768]{1,0:T(8,128)(2,1)}, b...) custom-call(bf16[768,768]{1,0:T(8,128)(2,1)} %bitcast.86, f32[8,768]{1,0:T(8,128)} %concatenate.50.dc_ref, ...), custom_call_target="tpu_custom_call" | custom-call | tf_op jit(solution)/shard_map/pallas_call | solution.py:642
  242.7 0.9 maximum_convert_fusion.4
  243.7 0.8 maximum_convert_fusion
  244.8 0.8 maximum_maximum_fusion.refs_0_
  245.6 201.1 %shard_map.260 = (bf16[19,256,768]{2,1,0:T(8,128)(2,1)}, bf16[2,2,16,768]{3,2,1,0:T(8,128)(2,1)}) custom-call(bf16[2,2,64,768]{3,2,1,0:T(8,128)(2,1)} %maximum_maximum_fusion.refs_0_, bf16[4,768,768]{2,1,0:T(8,128)(2,1)} %get-tuple-element.74.refs_1_, bf16[768,768]{1,0:T(8,128)(2,1)} %get-tuple-element.75.refs_2_, ...), custom_call_target="tpu_custom_call" | custom-call | tf_op jit(solution)/shard_map/pallas_call | solution.py:268
  446.7 3.5 slice.145
  450.2 0.1 slice.172
  450.3 2.4 convert_bitcast_fusion
  452.7 1.5 copy-done.2
  454.2 0.7 slice_convert_fusion.1
  454.9 0.7 reshape_squeeze.8
  455.6 2.2 fusion
  457.8 0.8 slice_convert_fusion
  458.6 0.6 reshape.234
  459.2 0.6 reshape.235
  459.8 0.6 reshape.236
  460.5 2.7 fusion.10
  463.1 2.5 bitcast_convert_fusion.1
  465.7 0.6 slice_bitcast_fusion.2
  466.3 2.5 bitcast_convert_fusion
  (58 shorter events, 1.2 us)
Async XLA Ops:
  0.6 1.9 copy-start.9
  0.7 2.0 copy-start.7
  2.8 1.7 copy-start
  4.4 1.7 copy-start.1
  6.1 76.6 %copy-start.4 = (bf16[2,2,768]{2,1,0:T(2,128)(2,1)S(1)}, bf16[2,2,768]{2,1,0:T(2,128)(2,1)}, u32[]{:S(2)}) copy-start(bf16[2,2,768]{2,1,0:T(2,128)(2,1)} %param.24) | copy-start | bytes 18436
  6.1 76.6 %copy-start.5 = (bf16[2,2,768]{2,1,0:T(2,128)(2,1)S(1)}, bf16[2,2,768]{2,1,0:T(2,128)(2,1)}, u32[]{:S(2)}) copy-start(bf16[2,2,768]{2,1,0:T(2,128)(2,1)} %param.26) | copy-start | bytes 18436
  6.1 76.6 %copy-start.6 = (bf16[2,2,768]{2,1,0:T(2,128)(2,1)S(1)}, bf16[2,2,768]{2,1,0:T(2,128)(2,1)}, u32[]{:S(2)}) copy-start(bf16[2,2,768]{2,1,0:T(2,128)(2,1)} %param.25) | copy-start | bytes 18436
  102.5 44.4 %copy-start.10 = (s32[3]{0:T(128)S(1)}, s32[3]{0:T(128)}, u32[]{:S(2)}) copy-start(s32[3]{0:T(128)} %param.20) | copy-start | bytes 40
  102.5 44.4 %copy-start.8 = (s32[3,4]{1,0:T(4,128)S(1)}, s32[3,4]{1,0:T(4,128)}, u32[]{:S(2)}) copy-start(s32[3,4]{1,0:T(4,128)} %param.19) | copy-start | bytes 148
  188.7 54.0 %copy-start.3 = (f32[16,768]{1,0:T(8,128)S(1)}, f32[16,768]{1,0:T(8,128)}, u32[]{:S(2)}) copy-start(f32[16,768]{1,0:T(8,128)} %get-tuple-element.72) | copy-start | bytes 147460
  450.2 4.0 copy-start.2

commit v2 on v1

--- a/solution.py
+++ b/solution.py
@@ -42,14 +42,205 @@
 HALF = D // 2
 MACROS = 18
 STEPS = MACROS * 4 + 1
-LAG = dict(c=2, x=2, y=2, z=2, a=2)
-
-
-def sum_kernel(outer, *refs):
-    ops, refs = refs[:17], refs[17:]
-    (out_ref, small_ref, made, crecv, xsend, xkeep, xrecv, ysend, ykeep, yrecv, zsend, zrecv, fin, osend, orecv,
+VMEM_LIMIT = 64 * 2**20
+LAG = dict(c=2, x=3, y=3, z=2, a=2)
+
+
+KEPT = ("cot", "n2", "i2", "d", "g", "hb", "n1", "i1", "qkv", "o", "x", "p")
+
+
+def held_names(e):
+    return tuple(k for k in KEPT[:11] if e == 0 or k not in ("o", "x"))
+
+
+def back_kernel(outer, sizes, *refs):
+    w_ref, dc_ref, vec_ref = refs[:3]
+    hbm = [dict(zip(KEPT, refs[3 + 12 * e : 15 + 12 * e])) for e in (0, 1)]
+    refs = refs[27:]
+    (out_ref, rows_ref, small_ref, *dx_ref), refs = refs[:5], refs[5:]
+    buf = []
+    for e in (0, 1):
+        names = held_names(e) + ("df", "da", "r", "dh", "do")
+        buf.append(dict(zip(names, refs[: len(names)])))
+        refs = refs[len(names) :]
+    (p0_ref, win, wout, up, down, sums, load_sem, dx_sem, w_sem,
+     made, crecv, xs, xrecv, ys, yrecv, zsum, zrecv, fin, osend, orecv,
      c_ss, c_rs, x_ss, x_rs, y_ss, y_rs, z_ss, z_rs, a_ss, a_rs, o_ss, o_rs, w_ss, w_rs, l_sem, t_ss, t_rs) = refs
-    first_ref, per_encoder = ops[0], (ops[9:17], ops[1:9])
+    buf[1]["p"], buf[0]["p"] = buf[1]["g"], p0_ref
+    buf[1]["o"], buf[1]["x"] = buf[1]["n2"], buf[1]["n1"]
+
+    def load(e, name):
+        return pltpu.make_async_copy(hbm[e][name], buf[e][name], load_sem.at[e, KEPT.index(name)])
+
+    def weights(e, kind):
+        return weight_copies(e, w_ref, (win, wout, up, down), w_sem, kind)
+
+    def begin(*copies):
+        for cp in copies:
+            cp.start()
+
+    def ready(*copies):
+        for cp in copies:
+            cp.wait()
+
+    begin(*[load(1, k) for k in ("cot", "n2", "i2")])
+    begin(*[load(1, "d")], *weights(1, 3), *[load(1, k) for k in ("g",)], *weights(1, 2))
+    begin(*[load(0, k) for k in ("cot", "n2", "i2")], *[load(1, k) for k in ("n1", "i1")], *weights(1, 1))
+    begin(*[load(0, k) for k in ("g", "d")], *[load(1, k) for k in ("hb", "qkv")])
+    begin(*[load(0, k) for k in ("hb", "n1", "i1", "qkv", "o", "x", "p")], *weights(1, 0))
+
+    vec = lambda e, i: vec_ref[e, i : i + 1, :]
+    col = lambda a: jnp.sum(a, axis=0, keepdims=True)
+    sums[...] = jnp.zeros_like(sums)
+
+    def add(e, row, v):
+        sums[e, row : row + 1, :] += v
+
+    def tokens(e, b):
+        n = spot(*sizes[e])[0]
+        return pl.ds(b * n, n) if isinstance(b, int) else pl.ds(pl.multiple_of(b * n, n), n)
+
+    def norm2(e, b):
+        group, groups, per = spot(*sizes[e])
+        w, tok = buf[e], tokens(e, b)
+        dy = w["cot"][tok, :].astype(f32)
+        pos = lax.broadcasted_iota(jnp.int32, (group, 1), 0)
+        for k in range(per):
+            dy = dy + jnp.where(pos == k * sizes[e][1], dc_ref[e, b * per + k : b * per + k + 1, :], 0.0)
+        n = w["n2"][tok, :].astype(f32)
+        add(e, 5, col(dy * n))
+        add(e, 7, col(dy))
+        r2 = norm_back(dy * vec(e, 1), n, w["i2"][tok, :])
+        w["r"][tok, :] = r2
+        df = r2.astype(bf16)
+        w["df"][tok, :] = df
+        add(e, 3, col(df.astype(f32)))
+
+    def hidden(e, i, b):
+        w, tok = buf[e], tokens(e, b)
+        for k in range(3):
+            c = slice(k * 256, (k + 1) * 256)
+            du = (dot(w["df"][tok, :], down[i, c, :], 1, 1) * w["d"][i, tok, c].astype(f32)).astype(bf16)
+            w["d"][i, tok, c] = du
+            sums[e, pl.ds(8 + i, 1), c] += col(du.astype(f32))
+        part = dot(w["d"][i, tok, :], up[i], 1, 1)
+        w["dh"][tok, :] = jnp.where(i == 0, part, w["dh"][tok, :] + part)
+
+    def norm1(e, b):
+        w, tok = buf[e], tokens(e, b)
+        dh = w["dh"][tok, :] + w["r"][tok, :]
+        n = w["n1"][tok, :].astype(f32)
+        add(e, 4, col(dh * n))
+        add(e, 6, col(dh))
+        r1 = norm_back(dh * vec(e, 0), n, w["i1"][tok, :])
+        w["r"][tok, :] = r1
+        da = r1.astype(bf16)
+        w["da"][tok, :] = da
+        add(e, 2, col(da.astype(f32)))
+        w["do"][:, tok] = dot(wout[...], da, 1, 1).astype(bf16)
+
+    def head(e, g, h):
+        w, tok = buf[e], tokens(e, g)
+        at = lambda base: pl.ds(pl.multiple_of(base + h * HD, HD), HD)
+        q, kk, vv, do = w["qkv"][at(0), tok], w["qkv"][at(D), tok], w["qkv"][at(2 * D), tok], w["do"][at(0), tok]
+        pb = w["p"][p_at(e, sizes[e], g, h)]
+        p = pb.astype(f32)
+        dp = dot(vv, do, 0, 0)
+        ds = (p * (dp - jnp.sum(p * dp, axis=0, keepdims=True))).astype(bf16)
+        w["qkv"][at(0), tok] = (dot(kk, ds, 1, 0) * 0.125).astype(bf16)
+        w["qkv"][at(D), tok] = dot(q, ds, 1, 1).astype(bf16)
+        w["qkv"][at(2 * D), tok] = dot(do, pb, 1, 1).astype(bf16)
+
+    def input_back(e, b):
+        w, tok = buf[e], tokens(e, b)
+        w["cot"][tok, :] = (dot(w["qkv"][:, tok], win[...], 0, 0) + w["r"][tok, :]).astype(bf16)
+
+    def dx_copy(e):
+        return pltpu.make_async_copy(buf[e]["cot"], dx_ref[e], dx_sem.at[e])
+
+    def bias_sums(e):
+        w = buf[e]
+        ones = jnp.ones((8, w["da"].shape[0]), bf16)
+        add(e, 0, dot(ones, w["qkv"][0:D, :], 1, 1)[0:1])
+        add(e, 1, dot(ones, w["qkv"][2 * D :, :], 1, 1)[0:1])
+
+    def at_step(s, first, fn, count=1):
+        @pl.when(jnp.logical_and(s >= first, s < first + count))
+        def _():
+            fn(s - first)
+
+    def work(s):
+        @pl.when(jnp.logical_and(s < 16, lax.rem(s, 4) > 0))
+        def _():
+            idx = lax.div(s, 4) * 3 + lax.rem(s, 4) - 1
+            hidden(1, lax.div(idx, 3), lax.rem(idx, 3))
+
+        def s4(_):
+            ready(*[load(0, k) for k in ("cot", "n2", "i2")])
+            norm2(0, 0)
+
+        def s9(_):
+            begin(load(1, "p"))
+
+        def s16(_):
+            begin(*weights(0, 3), *weights(0, 2))
+            ready(*[load(1, k) for k in ("n1", "i1")], *weights(1, 1))
+
+        def s20(_):
+            begin(load(1, "x"), *weights(0, 1))
+            ready(*weights(0, 3), *weights(0, 2), load(0, "d"))
+
+        def s25(_):
+            ready(load(0, "n1"), load(0, "i1"), *weights(0, 1))
+            norm1(0, 0)
+
+        def s26(_):
+            ready(load(1, "qkv"), load(1, "p"))
+
+        def att1(a):
+            for k in range(2):
+                head(1, lax.div(a, 6), lax.rem(a, 6) * 2 + k)
+
+        def s45(_):
+            bias_sums(1)
+            ready(*weights(1, 0))
+
+        def s49(_):
+            begin(dx_copy(1))
+            begin(*weights(0, 0))
+            ready(load(0, "qkv"), load(0, "p"))
+
+        def att0(a):
+            for k in range(2):
+                head(0, 0, a * 2 + k)
+
+        def s57(_):
+            bias_sums(0)
+            ready(*weights(0, 0))
+            input_back(0, 0)
+            begin(dx_copy(0))
+
+        at_step(s, 4, s4)
+        at_step(s, 9, s9)
+        at_step(s, 16, s16)
+        at_step(s, 17, lambda b: norm1(1, b), 3)
+        at_step(s, 20, s20)
+        at_step(s, 21, lambda i: hidden(0, i, 0), 4)
+        at_step(s, 25, s25)
+        at_step(s, 26, s26)
+        at_step(s, 27, att1, 18)
+        at_step(s, 45, s45)
+        at_step(s, 46, lambda b: input_back(1, b), 3)
+        at_step(s, 49, s49)
+        at_step(s, 51, att0, 6)
+        at_step(s, 57, s57)
+
+    ready(*[load(1, k) for k in ("cot", "n2", "i2")])
+    for b in range(3):
+        norm2(1, b)
+    begin(load(1, "o"))
+    ready(load(1, "d"), load(1, "g"), *weights(1, 3), *weights(1, 2))
+
     p = place()
     sib, xp, yp = device(p, c=1 - p["c"]), device(p, x=1 - p["x"]), device(p, y=1 - p["y"])
     zs = [lax.rem(p["z"] + j, 4) for j in (1, 2, 3)]
@@ -64,6 +255,8 @@
     la = lz + dz
     lf = la + da
     m16 = lambda v, n: pl.ds(pl.multiple_of(v, 16), n)
+    mine16 = m16(p["z"] * 16, 16)
+    half = lambda y: pl.ds(pl.multiple_of(y * HALF, 128), HALF)
 
     def made_at(u, c):
         return made.at[lax.rem(lax.div(u, 4), 2), :, c, m16(lax.rem(u, 4) * R, R)]
@@ -74,158 +267,167 @@
 
     def x_copy(u):
         k = lax.rem(u, 2 * dx)
-        return remote(xsend.at[k], xrecv.at[k], x_ss.at[k], x_rs.at[k], xp)
+        return remote(xs.at[k, 1 - p["x"]], xrecv.at[k], x_ss.at[k], x_rs.at[k], xp)
 
     def y_copy(u):
         k = lax.rem(u, 2 * dy)
-        return remote(ysend.at[k], yrecv.at[k], y_ss.at[k], y_rs.at[k], yp)
+        return remote(ys.at[k, :, half(1 - p["y"])], yrecv.at[k], y_ss.at[k], y_rs.at[k], yp)
 
     def z_copy(u, j):
         k = lax.rem(u, 2 * dz)
-        return remote(zsend.at[k, m16(zs[j] * 16, 16)], zrecv.at[k, 2 - j], z_ss.at[k, j], z_rs.at[k, 2 - j], zp[j])
-
-    def z_wait(u):
+        return remote(zsum.at[k, m16(zs[j] * 16, 16)], zrecv.at[k, m16(32 - 16 * j, 16)], z_ss.at[k], z_rs.at[k], zp[j])
+
+    def z_all(u):
         k = lax.rem(u, 2 * dz)
-        for j in range(3):
-            c = remote(zsend.at[k, m16(0, 16)], zrecv.at[k, j], z_ss.at[k, j], z_rs.at[k, j], zp[j])
-            c.wait_send()
-            c.wait_recv()
+        return remote(zsum.at[k, m16(0, 48)], zrecv.at[k], z_ss.at[k], z_rs.at[k], zp[0])
 
     def a_copy(u, j):
         k = lax.rem(u, 3 * da)
-        a = fin.at[k, m16(p["z"] * 16, 16)]
-        return remote(a, a, a_ss.at[k, j], a_rs.at[k, 2 - j], zp[j])
-
-    def a_wait(u):
+        a = fin.at[k, mine16]
+        return remote(a, a, a_ss.at[k], a_rs.at[k], zp[j])
+
+    def a_all(u):
         k = lax.rem(u, 3 * da)
-        for j in range(3):
-            a = fin.at[k, m16(0, 16)]
-            c = remote(a, a, a_ss.at[k, j], a_rs.at[k, j], zp[j])
-            c.wait_send()
-            c.wait_recv()
+        a = fin.at[k, m16(0, 48)]
+        return remote(a, a, a_ss.at[k], a_rs.at[k], zp[0])
+
+    def both(c):
+        c.wait_send()
+        c.wait_recv()
 
     def target(u):
         m = lax.div(u, 4)
         g = lax.div(m, 3)
-        spot_ = jnp.where(m == MACROS, MACROS, (lax.rem(g, 3) * 2 + 1 - lax.div(g, 3)) * 3 + lax.rem(m, 3))
-        return out_ref.at[spot_, m16(lax.rem(u, 4) * R, R), pl.ds(pl.multiple_of(p["y"] * HALF, 128), HALF)]
-
-    def w_remote(u):
+        return out_ref.at[(lax.div(g, 2) * 2 + 1 - lax.rem(g, 2)) * 3 + lax.rem(m, 3), m16(lax.rem(u, 4) * R, R), half(p["y"])]
+
+    def w_remote(u, dst):
         k = lax.rem(u, 3 * da)
-        return remote(fin.at[k], target(u), w_ss.at[k], w_rs.at[k], yp)
-
-    def w_local(u):
+        return remote(fin.at[k], dst, w_ss.at[k], w_rs.at[k], yp)
+
+    def w_local(u, dst):
         k = lax.rem(u, 3 * da)
-        return pltpu.make_async_copy(fin.at[k], target(u), l_sem.at[k])
-
-    def when(u, fn):
-        @pl.when(jnp.logical_and(u >= 0, u < STEPS))
+        return pltpu.make_async_copy(fin.at[k], dst, l_sem.at[k])
+
+    def when(u, fn, n=STEPS):
+        @pl.when(jnp.logical_and(u >= 0, u < n))
         def _():
             fn(u)
 
     def finish(u):
-        a_wait(u)
-        w_remote(u).start()
-        w_local(u).start()
+        both(a_all(u))
+
+        @pl.when(u < STEPS - 1)
+        def _():
+            w_remote(u, target(u)).start()
+            w_local(u, target(u)).start()
+
+        @pl.when(u == STEPS - 1)
+        def _():
+            w_remote(u, rows_ref.at[:, half(p["y"])]).start()
+            w_local(u, rows_ref.at[:, half(p["y"])]).start()
 
     def finished(u):
-        c = w_remote(u)
-        c.wait_send()
-        c.wait_recv()
-        w_local(u).wait()
+        @pl.when(u < STEPS - 1)
+        def _():
+            both(w_remote(u, target(u)))
+            w_local(u, target(u)).wait()
+
+        @pl.when(u == STEPS - 1)
+        def _():
+            both(w_remote(u, rows_ref.at[:, half(p["y"])]))
+            w_local(u, rows_ref.at[:, half(p["y"])]).wait()
 
     def take_z(u):
-        z_wait(u)
+        both(z_all(u))
         k = lax.rem(u, 2 * dz)
-        mine = m16(p["z"] * 16, 16)
-        v = zsend[k, mine].astype(f32)
+        v = zsum[k, mine16].astype(f32)
         for j in range(3):
-            v = v + zrecv[k, j].astype(f32)
+            v = v + zrecv[k, 16 * j : 16 * j + 16].astype(f32)
         if outer > 1:
             osend[...] = v.astype(bf16)
             for j in range(outer - 1):
                 remote(osend, orecv.at[outer - 2 - j], o_ss.at[j], o_rs.at[outer - 2 - j], op[j]).start()
             for j in range(outer - 1):
-                c = remote(osend, orecv.at[j], o_ss.at[j], o_rs.at[j], op[j])
-                c.wait_send()
-                c.wait_recv()
+                both(remote(osend, orecv.at[j], o_ss.at[j], o_rs.at[j], op[j]))
             v = osend[...].astype(f32)
             for j in range(outer - 1):
                 v = v + orecv[j].astype(f32)
-        fin[lax.rem(u, 3 * da), mine] = v.astype(bf16)
+        fin[lax.rem(u, 3 * da), mine16] = v.astype(bf16)
         for j in range(3):
             a_copy(u, j).start()
 
     def take_y(u):
-        c = y_copy(u)
-        c.wait_send()
-        c.wait_recv()
+        both(y_copy(u))
         k = lax.rem(u, 2 * dy)
-        zsend[lax.rem(u, 2 * dz)] = (ykeep[k] + yrecv[k].astype(f32)).astype(bf16)
+        zsum[lax.rem(u, 2 * dz)] = ys[k, :, half(p["y"])] + yrecv[k]
         for j in range(3):
             z_copy(u, j).start()
 
     def take_x(u):
-        c = x_copy(u)
-        c.wait_send()
-        c.wait_recv()
+        both(x_copy(u))
         k = lax.rem(u, 2 * dx)
-        ky = lax.rem(u, 2 * dy)
-        ysend[ky] = (xkeep[k, 1 - p["y"]] + xrecv[k, 1 - p["y"]].astype(f32)).astype(bf16)
+        ys[lax.rem(u, 2 * dy)] = xs[k, p["x"]] + xrecv[k]
         y_copy(u).start()
-        ykeep[ky] = xkeep[k, p["y"]] + xrecv[k, p["y"]].astype(f32)
 
     def take_c(u):
-        c = c_copy(u)
-        c.wait_send()
-        c.wait_recv()
+        both(c_copy(u))
         k = lax.rem(u, 2 * dc)
         kx = lax.rem(u, 2 * dx)
+        own = lambda x: made[lax.rem(lax.div(u, 4), 2), x, p["c"], m16(lax.rem(u, 4) * R, R)]
         o = 1 - p["x"]
-        own = lambda x: made[lax.rem(lax.div(u, 4), 2), x, p["c"], m16(lax.rem(u, 4) * R, R)].astype(f32)
-        v = (own(o) + crecv[k, o].astype(f32)).astype(bf16)
-        xsend[kx, 0] = v[:, :HALF]
-        xsend[kx, 1] = v[:, HALF:]
+        xs[kx, o] = own(o) + crecv[k, o]
         x_copy(u).start()
-        v = own(p["x"]) + crecv[k, p["x"]].astype(f32)
-        xkeep[kx, 0] = v[:, :HALF]
-        xkeep[kx, 1] = v[:, HALF:]
+        xs[kx, p["x"]] = own(p["x"]) + crecv[k, p["x"]]
 
     def make(m):
         slot = lax.rem(m, 2)
         g = lax.div(m, 3)
         r = lax.rem(m, 3)
+        cols = pl.ds(pl.multiple_of(r * MACRO, 128), MACRO)
         for e in (0, 1):
-            gate_, df, hb, du, o, da_, dqkv, x_ = per_encoder[e]
-
-            @pl.when(g == (1 - e) * 3)
+            w = buf[e]
+
+            @pl.when(g == 1 - e)
             def _():
-                cols = pl.ds(pl.multiple_of(r * MACRO, 128), MACRO)
+                if e == 0:
+                    @pl.when(r == 0)
+                    def _():
+                        ready(load(0, "g"))
                 for t in range(4):
-                    made[slot, t // 2, t % 2] = dot(gate_[t, :, cols], df[...], 0, 0).astype(bf16)
-
-            @pl.when(g == (1 - e) * 3 + 1)
+                    made[slot, t // 2, t % 2] = dot(w["g"][t, :, cols], w["df"][...], 0, 0).astype(bf16)
+
+            @pl.when(g == 3 - e)
             def _():
-                cols = pl.ds(pl.multiple_of(r * MACRO, 128), MACRO)
+                @pl.when(r == 0)
+                def _():
+                    ready(load(e, "hb"))
                 for t in range(4):
-                    made[slot, t // 2, t % 2] = dot(hb[:, cols], du[t], 0, 0).astype(bf16)
+                    made[slot, t // 2, t % 2] = dot(w["hb"][:, cols], w["d"][t], 0, 0).astype(bf16)
 
             for rr in range(3):
-                @pl.when(m == ((1 - e) * 3 + 2) * 3 + rr)
+                @pl.when(m == (5 - e) * 3 + rr)
                 def _():
+                    if rr == 0:
+                        ready(load(e, "o"), load(e, "x"))
                     for t in range(4):
                         at = rr * MACRO
                         while at < (rr + 1) * MACRO:
                             j, off = at // 192, at % 192
                             n = min(192 - off, (rr + 1) * MACRO - at)
-                            src = dqkv[j * D + t * 192 + off : j * D + t * 192 + off + n, :] if j < 3 else o[t * 192 + off : t * 192 + off + n, :]
+                            src = w["qkv"][j * D + t * 192 + off : j * D + t * 192 + off + n, :] if j < 3 else w["o"][t * 192 + off : t * 192 + off + n, :]
                             made[slot, t // 2, t % 2, at - rr * MACRO : at - rr * MACRO + n] = dot(
-                                src, x_[...] if j < 3 else da_[...], 1, 0).astype(bf16)
+                                src, w["x"][...] if j < 3 else w["da"][...], 1, 0).astype(bf16)
                             at += n
 
         @pl.when(m == MACROS)
         def _():
-            made[slot, :, :, 0:R] = first_ref[...]
+            row = lambda e, i: sums[e, i : i + 1, :]
+            shared = [row(e, i + k) for i in (2, 4, 6) for e in (0, 1) for k in (0, 1)]
+            for t in range(4):
+                v = [row(0, 0), row(0, 1), row(1, 0), row(1, 1), row(0, 8 + t), row(1, 8 + t)] + shared[3 * t : 3 * t + 3]
+                v = jnp.concatenate(v + [jnp.zeros((7, D), f32)], axis=0)
+                made[slot, t // 2, t % 2, 0:16] = v.astype(bf16)
+                made[slot, t // 2, t % 2, 16:R] = jnp.zeros((R - 16, D), bf16)
 
     def fetch(u):
         @pl.when(lax.rem(u, 4) == 0)
@@ -242,47 +444,50 @@
         when(s - ly, take_x)
         when(s - lx, take_c)
         when(s, fetch)
+        work(s)
         return _
 
     lax.fori_loop(0, STEPS + lf + da, step, 0)
+    ready(dx_copy(0), dx_copy(1))
     x, c = p["x"], p["c"]
-    own = out_ref.at[MACROS, pl.ds(0, 16)]
+    own = rows_ref.at[pl.ds(0, 16)]
     sends = [remote(own, small_ref.at[x, c], t_ss.at[i], t_rs.at[i], dev) for i, dev in enumerate((sib, xp, diag))]
     for cp in sends:
         cp.start()
-    mine = pltpu.make_async_copy(own, small_ref.at[x, c], l_sem.at[0])
-    mine.start()
-    mine.wait()
+    small_ref[x, c] = rows_ref[0:16]
     for i, (a, b) in enumerate(((x, 1 - c), (1 - x, c), (1 - x, 1 - c))):
         sends[i].wait_send()
         remote(own, small_ref.at[a, b], t_ss.at[i], t_rs.at[i], sib).wait_recv()
 
 
-def grad_sum(first, per_encoder, dp, cid=3):
+def backward(w_all, dc, vec, kept, sizes, dp, cid=3):
     outer = dp // 8
     dma = pltpu.SemaphoreType.DMA
-    dc, dx, dy, dz, da = (LAG[k] for k in "cxyza")
+    lc, lx, ly, lz, la = (LAG[k] for k in "cxyza")
     no = max(outer - 1, 1)
-    vm = pltpu.VMEM
-    args = [first.reshape(2, 2, R, D)] + list(per_encoder[1]) + list(per_encoder[0])
+    vm = lambda s, t=bf16: pltpu.VMEM(s, t)
+    scratch = []
+    for e in (0, 1):
+        n = sizes[e][0] * sizes[e][1]
+        scratch += [vm(kept[e][k].shape, kept[e][k].dtype) for k in held_names(e)]
+        scratch += [vm((n, D)), vm((n, D)), vm((n, D), f32), vm((n, D), f32), vm((D, n))]
+    args = [w_all, dc, vec] + [kept[e][k] for e in (0, 1) for k in KEPT]
     return pl.pallas_call(
-        functools.partial(sum_kernel, outer),
-        out_shape=(SDS((MACROS + 1, MACRO, D), bf16), SDS((2, 2, 16, D), bf16)),
-        in_specs=[VM] * len(args),
-        out_specs=(ANY, VM),
-        scratch_shapes=[
-            vm((2, 2, 2, MACRO, D), bf16), vm((2 * dc, 2, R, D), bf16),
-            vm((2 * dx, 2, R, HALF), bf16), vm((2 * dx, 2, R, HALF), f32), vm((2 * dx, 2, R, HALF), bf16),
-            vm((2 * dy, R, HALF), bf16), vm((2 * dy, R, HALF), f32), vm((2 * dy, R, HALF), bf16),
-            vm((2 * dz, R, HALF), bf16), vm((2 * dz, 3, 16, HALF), bf16),
-            vm((3 * da, R, HALF), bf16),
-            vm((16, HALF), bf16), vm((no, 16, HALF), bf16),
-            dma((2 * dc,)), dma((2 * dc,)), dma((2 * dx,)), dma((2 * dx,)),
-            dma((2 * dy,)), dma((2 * dy,)), dma((2 * dz, 3)), dma((2 * dz, 3)),
-            dma((3 * da, 3)), dma((3 * da, 3)), dma((no,)), dma((no,)),
-            dma((3 * da,)), dma((3 * da,)), dma((3 * da,)), dma((3,)), dma((3,)),
+        functools.partial(back_kernel, outer, sizes),
+        out_shape=(SDS((MACROS, MACRO, D), bf16), SDS((R, D), bf16), SDS((2, 2, 16, D), bf16),
+                   SDS(kept[0]["x"].shape, bf16), SDS(kept[1]["x"].shape, bf16)),
+        in_specs=[ANY, VM, VM] + [ANY] * 24,
+        out_specs=(ANY, VM, VM, ANY, ANY),
+        scratch_shapes=scratch + [
+            vm(kept[0]["p"].shape), *[vm(s) for s in W_SHAPES], vm((2, 16, D), f32), dma((2, 12)), dma((2,)), dma((24,)),
+            vm((2, 2, 2, MACRO, D)), vm((2 * lc, 2, R, D)), vm((2 * lx, 2, R, D)), vm((2 * lx, R, D)),
+            vm((2 * ly, R, D)), vm((2 * ly, R, HALF)), vm((2 * lz, R, HALF)), vm((2 * lz, 48, HALF)), vm((3 * la, R, HALF)),
+            vm((16, HALF)), vm((no, 16, HALF)),
+            dma((2 * lc,)), dma((2 * lc,)), dma((2 * lx,)), dma((2 * lx,)), dma((2 * ly,)), dma((2 * ly,)),
+            dma((2 * lz,)), dma((2 * lz,)), dma((3 * la,)), dma((3 * la,)), dma((no,)), dma((no,)),
+            dma((3 * la,)), dma((3 * la,)), dma((3 * la,)), dma((3,)), dma((3,)),
         ],
-        compiler_params=pltpu.CompilerParams(collective_id=cid, has_side_effects=True, vmem_limit_bytes=60 * 2**20),
+        compiler_params=pltpu.CompilerParams(collective_id=cid, has_side_effects=True, vmem_limit_bytes=VMEM_LIMIT),
     )(*args)
 
 
@@ -429,31 +634,42 @@
 W_SHAPES = ((3 * D, D), (D, D), (4, D, D), (4, D, D))
 
 
-def load_weights(e, w_ref, win, wout, up, down, sem):
-    base = 3 * (1 - e)
-    q = D // 4
-    kinds = [[], [], [], []]
+def weight_copies(e, w_ref, refs, sem, kind):
+    base, q = 3 * (1 - e), D // 4
+    dst = refs[kind]
+    pairs = []
     for t in range(4):
         src = w_ref.at[t // 2, t % 2]
-        for j in range(3):
-            kinds[0].append((src.at[base, pl.ds(j * q, q)], win.at[pl.ds(j * D + t * q, q)]))
-        kinds[1].append((src.at[base, pl.ds(3 * q, q)], wout.at[pl.ds(t * q, q)]))
-        kinds[2].append((src.at[base + 1], up.at[t]))
-        kinds[3].append((src.at[base + 2], down.at[t]))
-    n = 0
-    copies = []
-    for kind in kinds:
-        copies.append([pltpu.make_async_copy(a, b, sem.at[n + i]) for i, (a, b) in enumerate(kind)])
-        n += len(kind)
+        if kind == 0:
+            pairs += [(src.at[base, pl.ds(j * q, q)], dst.at[pl.ds(j * D + t * q, q)]) for j in range(3)]
+        elif kind == 1:
+            pairs.append((src.at[base, pl.ds(3 * q, q)], dst.at[pl.ds(t * q, q)]))
+        else:
+            pairs.append((src.at[base + kind - 1], dst.at[t]))
+    first = (0, 12, 16, 20)[kind]
+    return [pltpu.make_async_copy(a, b, sem.at[first + i]) for i, (a, b) in enumerate(pairs)]
+
+
+def load_weights(e, w_ref, win, wout, up, down, sem):
+    copies = [weight_copies(e, w_ref, (win, wout, up, down), sem, k) for k in range(4)]
+    for kind in copies:
+        for cp in kind:
+            cp.start()
 
     def ready(k):
         for cp in copies[k]:
             cp.wait()
 
-    for kind in copies:
-        for cp in kind:
-            cp.start()
     return ready
+
+
+def p_at(e, size, g, h):
+    group, groups, _ = spot(*size)
+    if groups == 1:
+        return (h,)
+    return (h // 3 if isinstance(h, int) else lax.div(h, 3),
+            pl.ds(g * group if isinstance(g, int) else pl.multiple_of(g * group, group), group),
+            pl.ds(pl.multiple_of((h % 3 if isinstance(h, int) else lax.rem(h, 3)) * group, 128), group))
 
 
 def forward_kernel(e, seqs, length, x_ref, w_ref, bcol_ref, ub_ref, vec_ref,
@@ -490,7 +706,7 @@
                     s = jnp.where(a == b, s, -1e30)
                 e = jnp.exp(s - jnp.max(s, axis=0, keepdims=True))
                 p = (e * (1.0 / jnp.sum(e, axis=0, keepdims=True))).astype(bf16)
-                p_ref[g * 12 + h] = p
+                p_ref[p_at(e, (seqs, length), g, h)] = p
                 o_ref[pl.ds(pl.multiple_of(h * HD, HD), HD), tok] = dot(vv, p, 1, 0).astype(bf16)
 
         loop(6, heads)
@@ -532,7 +748,7 @@
     seqs, length, _ = x.shape
     t = seqs * length
     group, groups, _ = spot(seqs, length)
-    outs = (SDS((t, D), bf16), SDS((3 * D, t), bf16), SDS((groups * 12, group, group), bf16), SDS((D, t), bf16), SDS((t, D), bf16), SDS((t, 1), f32),
+    outs = (SDS((t, D), bf16), SDS((3 * D, t), bf16), SDS((4, t, D) if groups > 1 else (12, group, group), bf16), SDS((D, t), bf16), SDS((t, D), bf16), SDS((t, 1), f32),
             SDS((t, D), bf16), SDS((4, t, D), bf16), SDS((4, t, D), bf16), SDS((t, D), bf16), SDS((t, 1), f32))
     return pl.pallas_call(
         functools.partial(forward_kernel, e, seqs, length), out_shape=outs, in_specs=[VM, ANY, VM, VM, VM], out_specs=(VM,) * len(outs),
@@ -545,105 +761,6 @@
     return inv * (dz - jnp.mean(dz, axis=-1, keepdims=True) - n * jnp.mean(dz * n, axis=-1, keepdims=True))
 
 
-def backward_kernel(e, seqs, length, cot_ref, dc_ref, n2_ref, i2_ref, d_ref, w_ref, n1_ref, i1_ref,
-                    qkv_ref, p_ref, vec_ref, df_ref, du_ref, da_ref, dqkv_ref, dx_ref, sum_ref, r2_s, r1_s, dh_s, do_s, win_ref, wout_ref, up_ref, down_ref, w_sem):
-    ready = load_weights(e, w_ref, win_ref, wout_ref, up_ref, down_ref, w_sem)
-    group, groups, per = spot(seqs, length)
-    tokens = seqs * length
-    blocks = tokens // group
-    vec = lambda i: vec_ref[i : i + 1, :]
-    col = lambda a: jnp.sum(a, axis=0, keepdims=True)
-    sum_ref[...] = jnp.zeros_like(sum_ref)
-
-    def add(row, v):
-        sum_ref[row : row + 1, :] += v
-
-    for b in range(blocks):
-        tok = slice(b * group, (b + 1) * group)
-        dy = cot_ref[tok, :].astype(f32)
-        pos = lax.broadcasted_iota(jnp.int32, (group, 1), 0)
-        for k in range(per):
-            dy = dy + jnp.where(pos == k * length, dc_ref[b * per + k : b * per + k + 1, :], 0.0)
-        n = n2_ref[tok, :].astype(f32)
-        add(5, col(dy * n))
-        add(7, col(dy))
-        r2 = norm_back(dy * vec(1), n, i2_ref[tok, :])
-        r2_s[tok, :] = r2
-        df = r2.astype(bf16)
-        df_ref[tok, :] = df
-        add(3, col(df.astype(f32)))
-
-    ready(3)
-    ready(2)
-
-    def hidden(i):
-        for b in range(blocks):
-            tok = slice(b * group, (b + 1) * group)
-            for k in range(3):
-                c = slice(k * 256, (k + 1) * 256)
-                du = (dot(df_ref[tok, :], down_ref[i, c, :], 1, 1) * d_ref[i, tok, c].astype(f32)).astype(bf16)
-                du_ref[i, tok, c] = du
-                sum_ref[pl.ds(8 + i, 1), c] += col(du.astype(f32))
-            part = dot(du_ref[i, tok, :], up_ref[i], 1, 1)
-            dh_s[tok, :] = jnp.where(i == 0, part, dh_s[tok, :] + part)
-
-    loop(4, hidden)
-    for b in range(blocks):
-        tok = slice(b * group, (b + 1) * group)
-        dh = dh_s[tok, :] + r2_s[tok, :]
-        n = n1_ref[tok, :].astype(f32)
-        add(4, col(dh * n))
-        add(6, col(dh))
-        r1 = norm_back(dh * vec(0), n, i1_ref[tok, :])
-        r1_s[tok, :] = r1
-        da = r1.astype(bf16)
-        da_ref[tok, :] = da
-        add(2, col(da.astype(f32)))
-
-    span = lambda i, n: pl.ds(pl.multiple_of(i * n, n), n)
-
-    def outward(i):
-        do_s[span(i, 256), :] = dot(wout_ref[span(i, 256), :], da_ref[...], 1, 1).astype(bf16)
-
-    ready(1)
-    loop(3, outward)
-    for g in range(groups):
-        tok = slice(g * group, (g + 1) * group)
-
-        def heads(i):
-            for k in range(2):
-                h = i * 2 + k
-                at = lambda base: pl.ds(pl.multiple_of(base + h * HD, HD), HD)
-                q, kk, vv, do = qkv_ref[at(0), tok], qkv_ref[at(D), tok], qkv_ref[at(2 * D), tok], do_s[at(0), tok]
-                pb = p_ref[g * 12 + h]
-                p = pb.astype(f32)
-                dp = dot(vv, do, 0, 0)
-                ds = (p * (dp - jnp.sum(p * dp, axis=0, keepdims=True))).astype(bf16)
-                dqkv_ref[at(0), tok] = (dot(kk, ds, 1, 0) * 0.125).astype(bf16)
-                dqkv_ref[at(D), tok] = dot(q, ds, 1, 1).astype(bf16)
-                dqkv_ref[at(2 * D), tok] = dot(do, pb, 1, 1).astype(bf16)
-
-        loop(6, heads)
-    ready(0)
-    ones = jnp.ones((8, tokens), bf16)
-    add(0, dot(ones, dqkv_ref[0:D, :], 1, 1)[0:1])
-    add(1, dot(ones, dqkv_ref[2 * D :, :], 1, 1)[0:1])
-    for b in range(blocks):
-        tok = slice(b * group, (b + 1) * group)
-        dx_ref[tok, :] = (dot(dqkv_ref[:, tok], win_ref[...], 0, 0) + r1_s[tok, :]).astype(bf16)
-
-
-def encoder_backward(e, cot, dc, kept, w, vec):
-    seqs, length, _ = cot.shape
-    t = seqs * length
-    qkv, p, o, n1, i1, hb, g, d, n2, i2 = kept
-    outs = (SDS((t, D), bf16), SDS((4, t, D), bf16), SDS((t, D), bf16), SDS((3 * D, t), bf16), SDS((t, D), bf16), SDS((16, D), f32))
-    args = (cot.reshape(t, D), dc, n2, i2, d, w, n1, i1, qkv, p, vec)
-    return pl.pallas_call(
-        functools.partial(backward_kernel, e, seqs, length), out_shape=outs, in_specs=[VM] * 5 + [ANY] + [VM] * 5, out_specs=(VM,) * len(outs),
-        scratch_shapes=[pltpu.VMEM((t, D), f32), pltpu.VMEM((t, D), f32), pltpu.VMEM((t, D), f32), pltpu.VMEM((D, t), bf16)] + [pltpu.VMEM(s, bf16) for s in W_SHAPES] + [pltpu.SemaphoreType.DMA((24,))],
-        compiler_params=pltpu.CompilerParams(vmem_limit_bytes=60 * 2**20),
-    )(*args)
 def cls_kernel(n, own_ref, out_ref, a_ss, a_rs, b_ss, b_rs):
     dp, t = lax.axis_index("dp"), lax.axis_index("tensor")
     ring = [lax.rem(dp + j, n) for j in range(1, n)]
@@ -721,29 +838,23 @@
     losses = lax.dynamic_slice_in_dim(losses, index * nq, nq, 0)
     dcq = mm(lax.dynamic_slice_in_dim(ds, index * nq, nq, 0), all_p, ((1,), (0,))) * scale
     dcp = mm(lax.dynamic_slice_in_dim(ds, index * np_, np_, 1), all_q, ((0,), (0,))) * scale
-    dxs, operands, smalls = [], [], []
-    for e, (cot, dc, x) in enumerate(((question_cotangent, dcq, questions), (passage_cotangent, dcp, passages))):
-        dc = jnp.concatenate([dc, jnp.zeros((8 - dc.shape[0], D), f32)])
-        df, du, da, dqkv, dx, s = encoder_backward(e, cot, dc, kept[e][:2] + [kept[e][2]] + kept[e][3:], weights, vecs[e])
+    pad = jnp.zeros((8 - nq, D), f32)
+    dc = jnp.stack([jnp.concatenate([dcq, pad]), jnp.concatenate([dcp, pad])])
+    for e, (cot, x) in enumerate(((question_cotangent, questions), (passage_cotangent, passages))):
         qkv, p, o, n1, i1, hb, g, d, n2, i2 = kept[e]
-        dxs.append(dx)
-        operands.append((g, df, hb, du, o, da, dqkv, x.reshape(-1, D)))
-        smalls.append(s)
-    both = jnp.stack(smalls)
-    rows12 = jnp.concatenate([both[:, 2:4].reshape(4, D), both[:, 4:6].reshape(4, D), both[:, 6:8].reshape(4, D)]).reshape(4, 3, D)
-    att = both[:, 0:2].reshape(2, 2, 4, q4).transpose(2, 0, 1, 3).reshape(4, 1, D)
-    up = both[:, 8:12].transpose(1, 0, 2)
-    first = jnp.concatenate([att, up, rows12, jnp.zeros((4, R - 6, D), f32)], axis=1).astype(bf16)
-    out, small = grad_sum(first, operands, n_dp)
-    res = out[:MACROS].reshape(3, 2, D, D)
-    own_small = out[MACROS, :16].astype(f32)
-    rep = small.reshape(4, 16, D)[:, 3:6].reshape(12, D).astype(f32)
+        kept[e] = dict(cot=cot.reshape(-1, D), n2=n2, i2=i2, d=d, g=g, hb=hb, n1=n1, i1=i1, qkv=qkv, o=o, x=x.reshape(-1, D), p=p)
+    sizes = (questions.shape[:2], passages.shape[:2])
+    out, own_rows, small, *dxs = backward(weights, dc, jnp.stack(vecs), kept, sizes, n_dp)
+    res = out.reshape(3, 2, D, D)
+    own_small = own_rows[:16].astype(f32)
+    rep = small.reshape(4, 16, D)[:, 6:9].reshape(12, D).astype(f32)
+    att = lax.dynamic_slice_in_dim(own_small[0:4], lax.axis_index("tensor") * q4, q4, 1)
     return (
         ys[0].reshape(questions.shape), ys[1].reshape(passages.shape), losses,
         dxs[0].reshape(questions.shape), dxs[1].reshape(passages.shape),
-        res[2, :, : 3 * q4].reshape(2, 3, q4, D).transpose(0, 1, 3, 2).astype(f32), own_small[0].reshape(2, 2, q4),
+        res[2, :, : 3 * q4].reshape(2, 3, q4, D).transpose(0, 1, 3, 2).astype(f32), att.reshape(2, 2, q4),
         res[2, :, 3 * q4 :].astype(f32), rep[0:4].reshape(2, 2, D), rep[4:8].reshape(2, 2, D), rep[8:12].reshape(2, 2, D),
-        res[1].astype(f32), own_small[1:3], res[0].astype(f32))
+        res[1].astype(f32), own_small[4:6], res[0].astype(f32))
 
 
 def solution(mesh):

time: 472 us -> 397 us (0.84)
  Pallas kernels: 428 us -> 360 us
  local copies, waits for them, and re-layouts: 22.8 us -> 16.5 us
    pallas_call x3 -> x1, Pallas kernels: 274 us -> 206 us  [backward(): pl.pallas_call(functools.partial(back_kernel, outer, sizes), out_shape=(S...]
where the time goes in v2:
time: 397 us
  Pallas kernels  360 us (91%)
  other arithmetic  18.8 us (5%)
  local copies, waits for them, and re-layouts  16.5 us (4%)
    pallas_call x1, Pallas kernels, backward(): pl.pallas_call(functools.partial(back_kernel, outer, sizes), out_shape=(S...  206 us
    pallas_call x1, Pallas kernels, weight_gather(): pl.pallas_call(gather_kernel, out_shape=(SDS((2, 2, CH, D, D), bf16), SDS...  74.3 us
    pallas_call x2, Pallas kernels, encoder_forward(): pl.pallas_call(functools.partial(forward_kernel, e, seqs, length), out_sh...  62 us
    pallas_call x1, Pallas kernels, cls_gather(): pl.pallas_call(functools.partial(cls_kernel, n), out_shape=jax.ShapeDtype...  17.8 us

profile of v2, /device:TPU:0, one launch (start us, length us, event | category | flops | bytes accessed | tf_op | source)
XLA Modules:
  0.0 396.7 jit_solution(4172683184040157232)
XLA Ops:
  0.7 0.7 iota_compare_fusion.1
  1.6 0.8 reshape.184
  2.4 0.8 convert_reduce_fusion
  3.2 0.7 bitcast_convert_fusion.5
  3.9 0.8 maximum_maximum_fusion.b_ref
  4.6 0.7 bitcast_convert_fusion.3
  5.4 0.7 fusion.11
  6.1 0.6 pad_maximum_fusion.2.refs_2_
  6.7 2.0 pad_maximum_fusion.io_ref
  8.7 0.4 copy-done
  9.1 0.7 copy-done.1
  9.8 74.3 %shard_map.254 = (bf16[2,2,6,768,768]{4,3,2,1,0:T(8,128)(2,1)}, bf16[2,2,16,768]{3,2,1,0:T(8,128)(2,1)S(1)}) custom-call(bf16[2,768,768]{2,1,0:T(8,128)(2,1)S(1)} %pad_maximum_fusion.io_ref, bf16[2,768,768]{2,1,0:T(8,128)(2,1)S(1)} %copy-done, bf16[2,768,768]{2,1,0:T(8,128)(2,1)S(1)} %copy-done.1, bf16[16,768]{1,0:T(8,128)(2,1)S(1)} %maximum_maximum_fusion.b_ref), custom_call_target="tpu_custom_call" | custom-call | tf_op jit(solution)/shard_map/pallas_call | solution.py:584
  84.1 0.6 fusion.14
  84.7 0.1 reshape_squeeze.4
  85.0 1.4 reshape.218.bcol_ref
  86.4 1.4 reshape.217.bcol_ref
  87.8 17.6 %shard_map.255 = (bf16[192,768]{1,0:T(8,128)(2,1)}, bf16[2304,192]{1,0:T(8,128)(2,1)}, bf16[12,192,192]{2,1,0:T(8,128)(2,1)}, bf16[768,192]{1,0:T(8,128)(2,1)}, ...) custom-call(bf16[192,768]{1,0:T(8,128)(2,1)} %bitcast.86, ...), custom_call_target="tpu_custom_call" | custom-call | tf_op jit(solution)/shard_map/pallas_call | solution.py:753
  105.4 0.8 slice.129
  106.2 44.3 %shard_map.256 = (bf16[768,768]{1,0:T(8,128)(2,1)}, bf16[2304,768]{1,0:T(8,128)(2,1)}, bf16[4,768,768]{2,1,0:T(8,128)(2,1)}, bf16[768,768]{1,0:T(8,128)(2,1)}, b...) custom-call(bf16[768,768]{1,0:T(8,128)(2,1)} %bitcast.80, ...), custom_call_target="tpu_custom_call" | custom-call | tf_op jit(solution)/shard_map/pallas_call | solution.py:753
  150.5 0.8 slice.130
  151.4 17.8 %shard_map.257 = bf16[4,8,16,768]{3,2,1,0:T(8,128)(2,1)S(1)} custom-call(bf16[16,768]{1,0:T(8,128)(2,1)S(1)} %maximum_maximum_fusion.3.own_ref), custom_call_target="tpu_custom_call" | custom-call | tf_op jit(solution)/shard_map/pallas_call | solution.py:788
  169.3 0.2 fusion.13
  169.5 0.1 reshape.194
  169.6 0.1 copy.47
  169.7 0.1 reshape.193
  169.9 0.1 reshape.192
  170.0 0.2 fusion.16
  170.3 0.1 convolution_multiply_fusion.1
  170.4 0.2 convolution_multiply_fusion.2
  170.7 0.6 dynamic_slice.12
  171.3 0.6 pad_maximum_fusion.1.refs_1_
  171.9 205.8 %shard_map.258 = (bf16[18,256,768]{2,1,0:T(8,128)(2,1)}, bf16[64,768]{1,0:T(8,128)(2,1)}, bf16[2,2,16,768]{3,2,1,0:T(8,128)(2,1)}, bf16[192,768]{1,0:T(8,128)(2,1)}, bf16[768,768]{1,0:T(8,128)(2,1)}) custom-call(bf16[2,2,6,768,768]{4,3,2,1,0:T(8,128)(2,1)} %get-tuple-element.43.w_ref.refs_0_, f32[2,8,768]{2,1,0:T(8,128)} %pad_maximum_fusion.1.refs_1_, ...), custom_call_target="tpu_custom_call" | custom-call | tf_op jit(solution)/shard_map/pallas_call | solution.py:475
  377.8 0.7 slice_convert_fusion.1
  378.5 0.6 slice.142
  379.2 0.6 reshape.200
  379.8 0.9 slice_convert_fusion
  380.8 0.6 reshape.204
  381.4 0.6 reshape.203
  382.0 0.6 reshape.202
  382.6 2.2 fusion
  384.8 1.7 slice.135
  386.5 2.1 convert_bitcast_fusion
  388.6 0.8 copy-done.2
  389.5 0.3 fusion.12
  389.8 2.5 bitcast_convert_fusion.1
  392.4 2.5 bitcast_convert_fusion
  394.9 0.7 copy.56
  395.6 1.0 copy.57
  (33 shorter events, 0.8 us)
Async XLA Ops:
  6.7 2.4 copy-start
  6.7 3.1 copy-start.1
  384.8 4.7 %copy-start.2 = (bf16[18,256,768]{2,1,0:T(8,128)(2,1)S(1)}, bf16[18,256,768]{2,1,0:T(8,128)(2,1)}, u32[]{:S(2)}) copy-start(bf16[18,256,768]{2,1,0:T(8,128)(2,1)} %get-tuple-element.69) | copy-start | bytes 21233668
  392.4 2.6 copy-start.4
  392.4 3.3 copy-start.3

commit v3 on v2

--- a/solution.py
+++ b/solution.py
@@ -47,6 +47,10 @@
 
 
 KEPT = ("cot", "n2", "i2", "d", "g", "hb", "n1", "i1", "qkv", "o", "x", "p")
+
+
+def cls_row(sizes, e):
+    return sizes[0][0] if e else 0
 
 
 def held_names(e):
@@ -106,7 +110,7 @@
         dy = w["cot"][tok, :].astype(f32)
         pos = lax.broadcasted_iota(jnp.int32, (group, 1), 0)
         for k in range(per):
-            dy = dy + jnp.where(pos == k * sizes[e][1], dc_ref[e, b * per + k : b * per + k + 1, :], 0.0)
+            dy = dy + jnp.where(pos == k * sizes[e][1], dc_ref[e, cls_row(sizes, e) + b * per + k : cls_row(sizes, e) + b * per + k + 1, :], 0.0)
         n = w["n2"][tok, :].astype(f32)
         add(e, 5, col(dy * n))
         add(e, 7, col(dy))
@@ -491,106 +495,6 @@
     )(*args)
 
 
-CH = 6
-PLAN = ((0, 1), (1, 1), (2, 1), (0, 0), (1, 0), (2, 0))
-
-
-def gather_kernel(io_ref, up_ref, down_ref, b_ref, out_ref, bias_ref, held, *sems):
-    (x_ss, x_rs, y_ss, y_rs, z_ss, z_rs, y2_ss, y2_rs, z2_ss, z2_rs, sib_ss, sib_rs, f_ss, f_rs, b_ss, b_rs, in_sem, back_sem) = sems
-    p = place()
-    zb = lax.rem(p["z"], 2)
-    sib, xp, yp = device(p, c=1 - p["c"]), device(p, x=1 - p["x"]), device(p, y=1 - p["y"])
-    zp = device(p, z=p["z"] + 1 - 2 * zb)
-    diag = device(p, x=1 - p["x"], c=1 - p["c"])
-    greet([sib, xp, yp, zp, diag])
-    x, c, y = p["x"], p["c"], p["y"]
-    quarter, half = D // 4, D // 8
-    rows = lambda q: pl.ds(pl.multiple_of(q * quarter, 16), quarter)
-    hrows = lambda q, k: pl.ds(pl.multiple_of(q * quarter + k * half, 16), half)
-    mine, qy, qz, dg = y * 2 + zb, (1 - y) * 2 + zb, y * 2 + 1 - zb, (1 - y) * 2 + 1 - zb
-    source = lambda h: (io_ref, up_ref, down_ref)[PLAN[h][0]].at[PLAN[h][1]]
-    started = []
-
-    def go(cp):
-        cp.start()
-        started.append(cp)
-
-    for i, dev in enumerate((sib, xp, diag)):
-        go(remote(b_ref, bias_ref.at[x, c], b_ss.at[i], b_rs.at[i], dev))
-    ins, backs = [], []
-    for h in range(CH):
-        go(remote(source(h).at[rows(mine)], out_ref.at[x, c, h, rows(mine)], x_ss.at[h], x_rs.at[h], xp))
-        go(remote(source(h), out_ref.at[x, c, h], sib_ss.at[h], sib_rs.at[h], sib))
-        ins.append(pltpu.make_async_copy(source(h), held.at[h], in_sem.at[h]))
-        ins[h].start()
-    bias_ref[x, c] = b_ref[...]
-    for h in range(CH):
-        ins[h].wait()
-        backs.append(pltpu.make_async_copy(held.at[h], out_ref.at[x, c, h], back_sem.at[h]))
-        backs[h].start()
-
-    def whole(h, q, ss, rs, dev):
-        a = out_ref.at[1 - x, c, h, rows(q)]
-        return remote(a, a, ss, rs, dev)
-
-    def part(h, q, k, ss, rs, dev):
-        a = out_ref.at[1 - x, c, h, hrows(q, k)]
-        return remote(a, a, ss.at[h], rs.at[h], dev)
-
-    def first(h):
-        whole(h, mine, x_ss.at[h], x_rs.at[h], xp).wait_recv()
-        go(whole(h, mine, y_ss.at[h], y_rs.at[h], yp))
-        go(whole(h, mine, z_ss.at[h], z_rs.at[h], zp))
-        go(whole(h, mine, f_ss.at[h, 0], f_rs.at[h, 0], sib))
-
-    def second(h):
-        whole(h, qy, y_ss.at[h], y_rs.at[h], yp).wait_recv()
-        go(part(h, qy, 1, z2_ss, z2_rs, zp))
-        go(whole(h, qy, f_ss.at[h, 1], f_rs.at[h, 1], sib))
-        whole(h, qz, z_ss.at[h], z_rs.at[h], zp).wait_recv()
-        go(part(h, qz, 0, y2_ss, y2_rs, yp))
-        go(whole(h, qz, f_ss.at[h, 2], f_rs.at[h, 2], sib))
-
-    def third(h):
-        part(h, dg, 0, y2_ss, y2_rs, yp).wait_recv()
-        part(h, dg, 1, z2_ss, z2_rs, zp).wait_recv()
-        go(whole(h, dg, f_ss.at[h, 3], f_rs.at[h, 3], sib))
-
-    def arrived(h):
-        a = out_ref.at[x, 1 - c, h]
-        remote(a, a, sib_ss.at[h], sib_rs.at[h], sib).wait_recv()
-        for i, q in enumerate((mine, qy, qz, dg)):
-            a = out_ref.at[1 - x, 1 - c, h, rows(q)]
-            remote(a, a, f_ss.at[h, i], f_rs.at[h, i], sib).wait_recv()
-        backs[h].wait()
-
-    for h in range(CH + 2):
-        if h < CH:
-            first(h)
-        if 0 <= h - 1 < CH:
-            second(h - 1)
-        if 0 <= h - 2 < CH:
-            third(h - 2)
-    for h in range(CH):
-        arrived(h)
-    for cp in started:
-        cp.wait_send()
-    for i, (a, b) in enumerate(((x, 1 - c), (1 - x, c), (1 - x, 1 - c))):
-        remote(b_ref, bias_ref.at[a, b], b_ss.at[i], b_rs.at[i], sib).wait_recv()
-
-
-def weight_gather(io, up, down, bias_rows, cid=1):
-    dma = pltpu.SemaphoreType.DMA
-    return pl.pallas_call(
-        gather_kernel,
-        out_shape=(SDS((2, 2, CH, D, D), bf16), SDS((2, 2, 16, D), bf16)),
-        in_specs=[ANY, ANY, ANY, VM],
-        out_specs=(ANY, VM),
-        scratch_shapes=[pltpu.VMEM((CH, D, D), bf16)] + [dma((CH,))] * 12 + [dma((CH, 4))] * 2 + [dma((3,))] * 2 + [dma((CH,))] * 2,
-        compiler_params=pltpu.CompilerParams(collective_id=cid, has_side_effects=True, vmem_limit_bytes=32 * 2**20),
-    )(io, up, down, bias_rows)
-
-
 HD = 64
 EPS = 1e-12
 
@@ -650,19 +554,6 @@
     return [pltpu.make_async_copy(a, b, sem.at[first + i]) for i, (a, b) in enumerate(pairs)]
 
 
-def load_weights(e, w_ref, win, wout, up, down, sem):
-    copies = [weight_copies(e, w_ref, (win, wout, up, down), sem, k) for k in range(4)]
-    for kind in copies:
-        for cp in kind:
-            cp.start()
-
-    def ready(k):
-        for cp in copies[k]:
-            cp.wait()
-
-    return ready
-
-
 def p_at(e, size, g, h):
     group, groups, _ = spot(*size)
     if groups == 1:
@@ -672,185 +563,399 @@
             pl.ds(pl.multiple_of((h % 3 if isinstance(h, int) else lax.rem(h, 3)) * group, 128), group))
 
 
-def forward_kernel(e, seqs, length, x_ref, w_ref, bcol_ref, ub_ref, vec_ref,
-                   y_ref, qkv_ref, p_ref, o_ref, n1_ref, i1_ref, hb_ref, g_ref, d_ref, n2_ref, i2_ref, h_s, f_s, win_ref, wout_ref, up_ref, down_ref, w_sem):
-    ready = load_weights(e, w_ref, win_ref, wout_ref, up_ref, down_ref, w_sem)
-    ready(0)
-    group, groups, per = spot(seqs, length)
-    tokens = seqs * length
-    blocks = tokens // group
-    span = lambda i, n: pl.ds(pl.multiple_of(i * n, n), n)
-    vec = lambda i: vec_ref[i : i + 1, :]
-
-    def project(i):
-        r = span(i, 256)
-        v = (dot(win_ref[r, :], x_ref[...], 1, 1) + bcol_ref[r, :]).astype(bf16)
-        qkv_ref[r, :] = v * jnp.where(i < 3, 0.125, 1.0).astype(bf16)
-
-    loop(9, project)
-    ready(1)
-
-    for g in range(groups):
-        tok = slice(g * group, (g + 1) * group)
-
-        def heads(i):
-            for k in range(2):
-                h = i * 2 + k
-                q = qkv_ref[pl.ds(pl.multiple_of(h * HD, HD), HD), tok]
-                kk = qkv_ref[pl.ds(pl.multiple_of(D + h * HD, HD), HD), tok]
-                vv = qkv_ref[pl.ds(pl.multiple_of(2 * D + h * HD, HD), HD), tok]
-                s = dot(kk, q, 0, 0)
-                if per > 1:
-                    a = lax.broadcasted_iota(jnp.int32, s.shape, 0) // length
-                    b = lax.broadcasted_iota(jnp.int32, s.shape, 1) // length
-                    s = jnp.where(a == b, s, -1e30)
-                e = jnp.exp(s - jnp.max(s, axis=0, keepdims=True))
-                p = (e * (1.0 / jnp.sum(e, axis=0, keepdims=True))).astype(bf16)
-                p_ref[p_at(e, (seqs, length), g, h)] = p
-                o_ref[pl.ds(pl.multiple_of(h * HD, HD), HD), tok] = dot(vv, p, 1, 0).astype(bf16)
-
-        loop(6, heads)
-
-    for b in range(blocks):
-        tok = slice(b * group, (b + 1) * group)
-        r = dot(o_ref[:, tok], wout_ref[...], 0, 0) + x_ref[tok, :].astype(f32) + vec(4)
-        h, n, inv = norm(r, vec(0), vec(2))
-        h_s[tok, :] = h
-        hb_ref[tok, :] = h.astype(bf16)
-        n1_ref[tok, :] = n.astype(bf16)
-        i1_ref[tok, :] = inv
-
-    ready(2)
-    ready(3)
-
-    def hidden(i):
-        for b in range(blocks):
-            tok = slice(b * group, (b + 1) * group)
-            for k in range(3):
-                c = slice(k * 256, (k + 1) * 256)
-                u = dot(hb_ref[tok, :], up_ref[i, :, c], 1, 0) + ub_ref[i, :, c]
-                g, d = gelu_pair(u)
-                g_ref[i, tok, c] = g.astype(bf16)
-                d_ref[i, tok, c] = d.astype(bf16)
-            part = dot(g_ref[i, tok, :], down_ref[i], 1, 0)
-            f_s[tok, :] = jnp.where(i == 0, part, f_s[tok, :] + part)
-
-    loop(4, hidden)
-    for b in range(blocks):
-        tok = slice(b * group, (b + 1) * group)
-        y, n, inv = norm(h_s[tok, :] + (f_s[tok, :] + vec(5)), vec(1), vec(3))
-        y_ref[tok, :] = y.astype(bf16)
-        n2_ref[tok, :] = n.astype(bf16)
-        i2_ref[tok, :] = inv
-
-
-def encoder_forward(e, x, w, bias_col, up_rows, vec):
-    seqs, length, _ = x.shape
-    t = seqs * length
-    group, groups, _ = spot(seqs, length)
-    outs = (SDS((t, D), bf16), SDS((3 * D, t), bf16), SDS((4, t, D) if groups > 1 else (12, group, group), bf16), SDS((D, t), bf16), SDS((t, D), bf16), SDS((t, 1), f32),
-            SDS((t, D), bf16), SDS((4, t, D), bf16), SDS((4, t, D), bf16), SDS((t, D), bf16), SDS((t, 1), f32))
-    return pl.pallas_call(
-        functools.partial(forward_kernel, e, seqs, length), out_shape=outs, in_specs=[VM, ANY, VM, VM, VM], out_specs=(VM,) * len(outs),
-        scratch_shapes=[pltpu.VMEM((t, D), f32), pltpu.VMEM((t, D), f32)] + [pltpu.VMEM(s, bf16) for s in W_SHAPES] + [pltpu.SemaphoreType.DMA((24,))],
-        compiler_params=pltpu.CompilerParams(vmem_limit_bytes=60 * 2**20),
-    )(x.reshape(t, D), w, bias_col, up_rows, vec)
-
-
 def norm_back(dz, n, inv):
     return inv * (dz - jnp.mean(dz, axis=-1, keepdims=True) - n * jnp.mean(dz * n, axis=-1, keepdims=True))
 
 
-def cls_kernel(n, own_ref, out_ref, a_ss, a_rs, b_ss, b_rs):
-    dp, t = lax.axis_index("dp"), lax.axis_index("tensor")
-    ring = [lax.rem(dp + j, n) for j in range(1, n)]
-    group = [lax.rem(t + j, 4) for j in range(1, 4)]
-    greet([(q, t) for q in ring] + [(dp, q) for q in group])
-    out_ref[t, dp] = own_ref[...]
-    first = [remote(own_ref, out_ref.at[t, dp], a_ss.at[j], a_rs.at[n - 2 - j], (q, t)) for j, q in enumerate(ring)]
-    for cp in first:
+CH = 6
+PLAN = ((0, 1), (1, 1), (2, 1), (0, 0), (1, 0), (2, 0))
+MADE = ("y", "qkv", "p", "o", "n1", "i1", "hb", "g", "d", "n2", "i2")
+
+
+def made_shapes(size):
+    t = size[0] * size[1]
+    group, groups, _ = spot(*size)
+    return dict(y=(t, D), qkv=(3 * D, t), p=(4, t, D) if groups > 1 else (12, group, group), o=(D, t), n1=(t, D), i1=(t, 1),
+                hb=(t, D), g=(4, t, D), d=(4, t, D), n2=(t, D), i2=(t, 1))
+
+
+def front_kernel(n, sizes, io_ref, up_ref, down_ref, b_ref, x0_ref, x1_ref, vec_ref, code_ref, *refs):
+    (out_ref, dc_ref, loss_ref), refs = refs[:3], refs[3:]
+    hbm = [dict(zip(MADE, refs[11 * e : 11 * e + 11])) for e in (0, 1)]
+    refs = refs[22:]
+    buf = [dict(zip(MADE, refs[11 * e : 11 * e + 11])) for e in (0, 1)]
+    refs = refs[22:]
+    (h0, f0, h1, f1, win, wout, up, down, bias_ref, bias_in, held, cls, full, codes, pay, w_sem, made_sem,
+     x_ss, x_rs, y_ss, y_rs, z_ss, z_rs, y2_ss, y2_rs, z2_ss, z2_rs, sib_ss, sib_rs, f_ss, f_rs, b_ss, b_rs, in_sem, back_sem,
+     r_ss, r_rs, g_ss, g_rs) = refs
+    xin, hs, fs = (x0_ref, x1_ref), (h0, h1), (f0, f1)
+    p = place()
+    zb = lax.rem(p["z"], 2)
+    sib, xp, yp = device(p, c=1 - p["c"]), device(p, x=1 - p["x"]), device(p, y=1 - p["y"])
+    zp = device(p, z=p["z"] + 1 - 2 * zb)
+    diag = device(p, x=1 - p["x"], c=1 - p["c"])
+    ring = [lax.rem(p["dp"] + j, n) for j in range(1, n)]
+    group4 = [lax.rem(p["t"] + j, 4) for j in range(1, 4)]
+    greet([(q, p["t"]) for q in ring] + [(p["dp"], q) for q in group4])
+    x, c, y = p["x"], p["c"], p["y"]
+    quarter, half = D // 4, D // 8
+    rows = lambda q: pl.ds(pl.multiple_of(q * quarter, 16), quarter)
+    hrows = lambda q, k: pl.ds(pl.multiple_of(q * quarter + k * half, 16), half)
+    mine, qy, qz, dg = y * 2 + zb, (1 - y) * 2 + zb, y * 2 + 1 - zb, (1 - y) * 2 + 1 - zb
+    source = lambda h: (io_ref, up_ref, down_ref)[PLAN[h][0]].at[PLAN[h][1]]
+    started = []
+
+    def go(cp):
         cp.start()
+        started.append(cp)
+
+    for i, dev in enumerate((sib, xp, diag)):
+        go(remote(b_ref, bias_ref.at[x, c], b_ss.at[i], b_rs.at[i], dev))
+    for h in range(CH):
+        go(remote(source(h).at[rows(mine)], out_ref.at[x, c, h, rows(mine)], x_ss.at[h], x_rs.at[h], xp))
+        go(remote(source(h), out_ref.at[x, c, h], sib_ss.at[h], sib_rs.at[h], sib))
+    ins = [pltpu.make_async_copy(source(h), held.at[h % 2], in_sem.at[h]) for h in range(CH)]
+    backs = [pltpu.make_async_copy(held.at[h % 2], out_ref.at[x, c, h], back_sem.at[h]) for h in range(CH)]
+    ins[0].start()
+    ins[1].start()
+    bias_ref[x, c] = b_ref[...]
+    def bounce(h):
+        ins[h].wait()
+        backs[h].start()
+        if h + 2 < CH:
+            backs[h].wait()
+            ins[h + 2].start()
+
+    def whole(h, q, ss, rs, dev):
+        a = out_ref.at[1 - x, c, h, rows(q)]
+        return remote(a, a, ss, rs, dev)
+
+    def part(h, q, k, ss, rs, dev):
+        a = out_ref.at[1 - x, c, h, hrows(q, k)]
+        return remote(a, a, ss.at[h], rs.at[h], dev)
+
+    def first(h):
+        whole(h, mine, x_ss.at[h], x_rs.at[h], xp).wait_recv()
+        go(whole(h, mine, y_ss.at[h], y_rs.at[h], yp))
+        go(whole(h, mine, z_ss.at[h], z_rs.at[h], zp))
+        go(whole(h, mine, f_ss.at[h, 0], f_rs.at[h, 0], sib))
+
+    def second(h):
+        whole(h, qy, y_ss.at[h], y_rs.at[h], yp).wait_recv()
+        go(part(h, qy, 1, z2_ss, z2_rs, zp))
+        go(whole(h, qy, f_ss.at[h, 1], f_rs.at[h, 1], sib))
+        whole(h, qz, z_ss.at[h], z_rs.at[h], zp).wait_recv()
+        go(part(h, qz, 0, y2_ss, y2_rs, yp))
+        go(whole(h, qz, f_ss.at[h, 2], f_rs.at[h, 2], sib))
+
+    def third(h):
+        part(h, dg, 0, y2_ss, y2_rs, yp).wait_recv()
+        part(h, dg, 1, z2_ss, z2_rs, zp).wait_recv()
+        go(whole(h, dg, f_ss.at[h, 3], f_rs.at[h, 3], sib))
+
+    def arrived(h):
+        a = out_ref.at[x, 1 - c, h]
+        remote(a, a, sib_ss.at[h], sib_rs.at[h], sib).wait_recv()
+        for i, q in enumerate((mine, qy, qz, dg)):
+            a = out_ref.at[1 - x, 1 - c, h, rows(q)]
+            remote(a, a, f_ss.at[h, i], f_rs.at[h, i], sib).wait_recv()
+        if h >= CH - 2:
+            backs[h].wait()
+
+    def weights(e, kind):
+        return weight_copies(e, out_ref, (win, wout, up, down), w_sem, kind)
+
+    def begin(*copies):
+        for cp in copies:
+            cp.start()
+
+    def ready(*copies):
+        for cp in copies:
+            cp.wait()
+
+    def keep(e, *names):
+        for k in names:
+            cp = pltpu.make_async_copy(buf[e][k], hbm[e][k], made_sem.at[e, MADE.index(k)])
+            cp.start()
+            keeps.append(cp)
+
+    keeps = []
+    vec = lambda e, i: vec_ref[e, i : i + 1, :]
+
+    def tokens(e, b):
+        m = spot(*sizes[e])[0]
+        return pl.ds(b * m, m)
+
+    def project(e, i):
+        r = pl.ds(pl.multiple_of(i * 256, 256), 256)
+        ones = jnp.ones((16, xin[e].shape[0]), bf16)
+        bias = bias_in[e, lax.div(i, 3), :, pl.ds(pl.multiple_of(lax.rem(i, 3) * 256, 128), 256)]
+        v = (dot(win[r, :], xin[e][...], 1, 1) + dot(bias, ones, 0, 0)).astype(bf16)
+        buf[e]["qkv"][r, :] = v * jnp.where(i < 3, 0.125, 1.0).astype(bf16)
+
+    def heads(e, g, i):
+        group, groups, per = spot(*sizes[e])
+        tok, w = tokens(e, g), buf[e]
+        for k in range(2):
+            h = i * 2 + k
+            at = lambda base: pl.ds(pl.multiple_of(base + h * HD, HD), HD)
+            s = dot(w["qkv"][at(D), tok], w["qkv"][at(0), tok], 0, 0)
+            if per > 1:
+                a = lax.broadcasted_iota(jnp.int32, s.shape, 0) // sizes[e][1]
+                b = lax.broadcasted_iota(jnp.int32, s.shape, 1) // sizes[e][1]
+                s = jnp.where(a == b, s, -1e30)
+            ex = jnp.exp(s - jnp.max(s, axis=0, keepdims=True))
+            pr = (ex * (1.0 / jnp.sum(ex, axis=0, keepdims=True))).astype(bf16)
+            w["p"][p_at(e, sizes[e], g, h)] = pr
+            w["o"][at(0), tok] = dot(w["qkv"][at(2 * D), tok], pr, 1, 0).astype(bf16)
+
+    def out_norm(e, b):
+        tok, w = tokens(e, b), buf[e]
+        r = dot(w["o"][:, tok], wout[...], 0, 0) + xin[e][tok, :].astype(f32) + vec(e, 4)
+        h, m, inv = norm(r, vec(e, 0), vec(e, 2))
+        hs[e][tok, :] = h
+        w["hb"][tok, :] = h.astype(bf16)
+        w["n1"][tok, :] = m.astype(bf16)
+        w["i1"][tok, :] = inv
+
+    def hidden(e, i, b):
+        tok, w = tokens(e, b), buf[e]
+        ub = bias_ref[i // 2, i % 2, 0:16, :].astype(f32)[4 + e : 5 + e]
+        for k in range(3):
+            cc = slice(k * 256, (k + 1) * 256)
+            u = dot(w["hb"][tok, :], up[i, :, cc], 1, 0) + ub[:, cc]
+            g, d = gelu_pair(u)
+            w["g"][i, tok, cc] = g.astype(bf16)
+            w["d"][i, tok, cc] = d.astype(bf16)
+
+    def shrink(e, i, b):
+        tok, w = tokens(e, b), buf[e]
+        part_ = dot(w["g"][i, tok, :], down[i], 1, 0)
+        fs[e][tok, :] = part_ if i == 0 else fs[e][tok, :] + part_
+
+    def norm2(e, b):
+        tok, w = tokens(e, b), buf[e]
+        v, m, inv = norm(hs[e][tok, :] + (fs[e][tok, :] + vec(e, 5)), vec(e, 1), vec(e, 3))
+        w["y"][tok, :] = v.astype(bf16)
+        w["n2"][tok, :] = m.astype(bf16)
+        w["i2"][tok, :] = inv
+
+    def projects(e, a, b):
+        lax.fori_loop(a, b, lambda i, cc: (project(e, i), cc)[1], 0)
+
+    def attend(e, g):
+        loop(6, lambda i: heads(e, g, i))
+
+    bounce(0)
+    bounce(1)
+    first(0)
+    bounce(2)
+    bounce(3)
+    for i, (a, b) in enumerate(((x, 1 - c), (1 - x, c), (1 - x, 1 - c))):
+        remote(b_ref, bias_ref.at[a, b], b_ss.at[i], b_rs.at[i], sib).wait_recv()
+    for e in (0, 1):
+        for j in range(3):
+            if j == 1:
+                bias_in[e, j] = jnp.zeros((16, D), bf16)
+            else:
+                r = 2 * e + j // 2
+                got = [bias_ref[t // 2, t % 2].astype(f32)[r : r + 1] for t in range(4)]
+                bias_in[e, j] = jnp.concatenate(got + [jnp.zeros((12, D), f32)], axis=0).astype(bf16)
+    first(1)
+    second(0)
+    bounce(4)
+    bounce(5)
+    first(2)
+    second(1)
+    third(0)
+    arrived(0)
+    begin(*weights(1, 0), *weights(1, 1))
+    ready(*weights(1, 0))
+    projects(1, 0, 4)
+    first(3)
+    projects(1, 4, 9)
+    second(2)
+    attend(1, 0)
+    third(1)
+    arrived(1)
+    first(4)
+    begin(*weights(1, 2))
+    attend(1, 1)
+    second(3)
+    first(5)
+    attend(1, 2)
+    keep(1, "qkv", "p", "o")
+    third(2)
+    arrived(2)
+    begin(*weights(1, 3))
+    ready(*weights(1, 1))
+    for b in range(3):
+        out_norm(1, b)
+    second(4)
+    keep(1, "n1", "i1", "hb")
+    ready(*weights(1, 2), *weights(1, 3))
+    for i in range(4):
+        for b in range(3):
+            hidden(1, i, b)
+            shrink(1, i, b)
+        if i == 0:
+            third(3)
+            arrived(3)
+            begin(*weights(0, 0), *weights(0, 1))
+        if i == 1:
+            second(5)
+        if i == 2:
+            third(4)
+            arrived(4)
+    keep(1, "g", "d")
+    begin(*weights(0, 2))
+    third(5)
+    arrived(5)
+    begin(*weights(0, 3))
+    for b in range(3):
+        norm2(1, b)
+    keep(1, "y", "n2", "i2")
+    ready(*weights(0, 0))
+    projects(0, 0, 9)
+    attend(0, 0)
+    keep(0, "qkv", "p", "o")
+    ready(*weights(0, 1))
+    out_norm(0, 0)
+    keep(0, "n1", "i1", "hb")
+    ready(*weights(0, 2), *weights(0, 3))
+    for i in range(4):
+        hidden(0, i, 0)
+        shrink(0, i, 0)
+    norm2(0, 0)
+    nq, np_ = sizes[0][0], sizes[1][0]
+    got = [buf[e]["y"][i * sizes[e][1] : i * sizes[e][1] + 16, :].astype(f32)[0:1] for e in (0, 1) for i in range(sizes[e][0])]
+    blank = jnp.zeros((16 - 2 * (nq + np_), HALF), f32)
+    pay[...] = (jnp.concatenate([v[:, :HALF] for v in got] + [v[:, HALF:] for v in got] + [blank], axis=0) + code_ref[...]).astype(bf16)
+    place_of = lambda t, d: pl.ds(pl.multiple_of((t * n + d) * 16, 16), 16)
+    here = cls.at[place_of(p["t"], p["dp"])]
+    cls[place_of(p["t"], p["dp"]), :] = pay[...]
     for j, q in enumerate(ring):
-        a = out_ref.at[t, q]
-        remote(a, a, a_ss.at[j], a_rs.at[j], (q, t)).wait_recv()
-    second = [remote(out_ref.at[t], out_ref.at[t], b_ss.at[j], b_rs.at[2 - j], (dp, q)) for j, q in enumerate(group)]
-    for cp in second:
-        cp.start()
-    for j, q in enumerate(group):
-        a = out_ref.at[q]
-        remote(a, a, b_ss.at[j], b_rs.at[j], (dp, q)).wait_recv()
-    for cp in first + second:
+        go(remote(pay, here, r_ss.at[j], r_rs.at[n - 2 - j], (q, p["t"])))
+    keep(0, "g", "d", "y", "n2", "i2")
+    for j, q in enumerate(ring):
+        remote(pay, cls.at[place_of(p["t"], q)], r_ss.at[j], r_rs.at[j], (q, p["t"])).wait_recv()
+    band = lambda x_, c_: cls.at[pl.ds(pl.multiple_of((x_ * 2 + c_) * n * 16, 16), n * 16)]
+    go(remote(band(x, c), band(x, c), g_ss.at[0], g_rs.at[0], xp))
+    go(remote(band(x, c), band(x, c), g_ss.at[1], g_rs.at[1], sib))
+    remote(band(1 - x, c), band(1 - x, c), g_ss.at[0], g_rs.at[0], xp).wait_recv()
+    go(remote(band(1 - x, c), band(1 - x, c), g_ss.at[2], g_rs.at[2], sib))
+    remote(band(x, 1 - c), band(x, 1 - c), g_ss.at[1], g_rs.at[1], sib).wait_recv()
+    remote(band(1 - x, 1 - c), band(1 - x, 1 - c), g_ss.at[2], g_rs.at[2], sib).wait_recv()
+
+    total = 4 * n * 16
+    scale = 2.7 * D**-0.5
+    count = nq + np_
+
+    def unfold(v):
+        v = v.astype(f32)
+        k = v.shape[0]
+        return jnp.concatenate([v, pltpu.roll(v, k - count, 0), pltpu.roll(v[:, 0:128], k - 2 * count, 0)], axis=1)
+
+    own = unfold(pay[...])
+    own_code, own = own[:, D:], own[:, :D].astype(bf16)
+    wide = unfold(cls[...])
+    full[...] = wide[:, :D].astype(bf16)
+    codes[...] = wide[:, D:]
+    at = lax.broadcasted_iota(jnp.int32, (1, total), 1)
+    block, pos = at // 16, at % 16
+    name = (((block % n) * 4 + block // n) * np_ + (pos - nq)).astype(f32)
+    live = jnp.logical_and(pos >= nq, pos < nq + np_)
+
+    def marks(code, names):
+        m = jnp.zeros((code.shape[0], names.shape[1]), f32)
+        for k in range(4):
+            m = m + (code[:, k : k + 1] * 16.0 + code[:, 4 + k : 5 + k] == names).astype(f32)
+        return m
+
+    def spread(block_rows, code):
+        s = jnp.where(live, dot(block_rows, full[...], 1, 1) * scale, -1e30)
+        top = jnp.max(s, axis=1, keepdims=True)
+        ex = jnp.exp(s - top)
+        m = jnp.where(live, marks(code, name), 0.0)
+        return top, ex, jnp.sum(ex, axis=1, keepdims=True), m, jnp.sum(m * ex, axis=1, keepdims=True)
+
+    row = lax.broadcasted_iota(jnp.int32, (16, 1), 0)
+    top, ex, z, m, pz = spread(own, own_code)
+    loss_ref[...] = jnp.broadcast_to(jnp.log(z) - jnp.log(pz), loss_ref.shape)
+    ds = jnp.where(row < nq, ex / z - m * ex / pz, 0.0).astype(bf16)
+    dc_ref[0] = dot(ds, full[...], 1, 0) * scale
+    own_pos = lax.broadcasted_iota(jnp.int32, (1, 16), 1)
+    own_name = ((p["dp"] * 4 + p["t"]) * np_ + (own_pos - nq)).astype(f32)
+    own_live = jnp.logical_and(own_pos >= nq, own_pos < nq + np_)
+    step = min(total, max(16, 131072 // total))
+    dc_ref[1] = jnp.zeros((16, D), f32)
+
+    def block_of(i):
+        r = pl.ds(pl.multiple_of(i * step, 16), step)
+        rows_ = full[r, :]
+        code = codes[r, :]
+        top, _, z, _, pz = spread(rows_, code)
+        e_ = jnp.exp(dot(rows_, own, 1, 1) * scale - top)
+        real = lax.broadcasted_iota(jnp.int32, (step, 1), 0) % 16 < nq
+        ds = jnp.where(jnp.logical_and(real, own_live), e_ / z - marks(code, own_name) * e_ / pz, 0.0).astype(bf16)
+        dc_ref[1] += dot(ds, rows_, 0, 0) * scale
+
+    loop(total // step, block_of)
+    for cp in keeps:
+        cp.wait()
+    for cp in started:
         cp.wait_send()
 
 
-def cls_gather(own, n, cid=2):
+def forward(io, up, down, bias_rows, xs_, vec, code, sizes, n, cid=1):
     dma = pltpu.SemaphoreType.DMA
+    vm = lambda s, t=bf16: pltpu.VMEM(s, t)
+    shapes = [made_shapes(z) for z in sizes]
+    kind = lambda k: f32 if k in ("i1", "i2") else bf16
+    tok = [a * b for a, b in sizes]
+    outs = [SDS(shapes[e][k], kind(k)) for e in (0, 1) for k in MADE]
+    scratch = [vm(shapes[e][k], kind(k)) for e in (0, 1) for k in MADE]
+    for t in tok:
+        scratch += [vm((t, D), f32), vm((t, D), f32)]
     return pl.pallas_call(
-        functools.partial(cls_kernel, n),
-        out_shape=jax.ShapeDtypeStruct((4, n, 16, D), bf16),
-        in_specs=[pl.BlockSpec(memory_space=pltpu.VMEM)],
-        out_specs=pl.BlockSpec(memory_space=pltpu.VMEM),
-        scratch_shapes=[dma((n - 1,)), dma((n - 1,)), dma((3,)), dma((3,))],
-        compiler_params=pltpu.CompilerParams(collective_id=cid, has_side_effects=True, vmem_limit_bytes=48 * 2**20),
-    )(own)
-
-
-def mm(a, b, dims):
-    return lax.dot_general(a, b, (dims, ((), ())), preferred_element_type=f32)
+        functools.partial(front_kernel, n, sizes),
+        out_shape=[SDS((2, 2, CH, D, D), bf16), SDS((2, 16, D), f32), SDS((16, 128), f32)] + outs,
+        in_specs=[ANY, ANY, ANY, VM, VM, VM, VM, VM],
+        out_specs=[ANY, VM, VM] + [ANY] * 22,
+        scratch_shapes=scratch + [vm(s) for s in W_SHAPES] + [
+            vm((2, 2, 16, D)), vm((2, 3, 16, D)), vm((2, D, D)), vm((4 * n * 16, HALF)), vm((4 * n * 16, D)), vm((4 * n * 16, 128), f32), vm((16, HALF)), dma((24,)), dma((2, 11))]
+        + [dma((CH,))] * 12 + [dma((CH, 4))] * 2 + [dma((3,))] * 2 + [dma((CH,))] * 2 + [dma((n - 1,))] * 2 + [dma((3,))] * 2,
+        compiler_params=pltpu.CompilerParams(collective_id=cid, has_side_effects=True, vmem_limit_bytes=VMEM_LIMIT),
+    )(io, up, down, bias_rows, *xs_, vec, code)
 
 
 def body(n_dp, questions, passages, question_cotangent, passage_cotangent, positives, positive_counts,
          attention_in, attention_bias, attention_out, branch_biases, norm_gains, norm_shifts, up_weight, up_bias, down_weight):
     q4 = D // 4
+    nq = questions.shape[0]
+    sizes = (questions.shape[:2], passages.shape[:2])
     io = jnp.concatenate([attention_in.transpose(0, 1, 3, 2).reshape(2, 3 * q4, D), attention_out], axis=1)
-    bias_rows = jnp.concatenate([attention_bias.reshape(1, D), up_bias, jnp.zeros((13, D), bf16)])
-    weights, biases = weight_gather(io, up_weight, down_weight, bias_rows)
-    biases = biases.reshape(4, 16, D).astype(f32)
-    full_att = biases[:, 0].reshape(4, 2, 2, q4).transpose(1, 2, 0, 3).reshape(2, 2, D)
-    nothing = jnp.zeros((2, D), f32)
-    kept, ys, vecs = [], [], []
-    for e, x in enumerate((questions, passages)):
-        vec = jnp.concatenate([norm_gains[e].astype(f32), norm_shifts[e].astype(f32), branch_biases[e].astype(f32), nothing])
-        bias_col = jnp.concatenate([full_att[e, 0], nothing[0], full_att[e, 1]]).reshape(3 * D, 1)
-        y, *k = encoder_forward(e, x, weights, bias_col, biases[:, 1 + e : 2 + e], vec)
-        kept.append(k)
-        ys.append(y)
-        vecs.append(vec)
-    nq, np_ = questions.shape[0], passages.shape[0]
-    total = np_ * n_dp * 4
-    cq = ys[0].reshape(questions.shape)[:, 0]
-    cp = ys[1].reshape(passages.shape)[:, 0]
-    live = jnp.arange(positives.shape[1], dtype=jnp.int32)[None, :] < positive_counts[:, None]
-    marks = jnp.sum(((positives[:, :, None] == jnp.arange(D, dtype=jnp.int32)[None, None, :]) & live[:, :, None]).astype(f32), axis=1)
-    payload = jnp.concatenate([cq, cp, marks.astype(bf16), jnp.zeros((16 - 2 * nq - np_, D), bf16)])
-    every = cls_gather(payload, n_dp).transpose(1, 0, 2, 3).reshape(n_dp * 4, 16, D)
-    all_q = every[:, :nq].reshape(-1, D)
-    all_p = every[:, nq : nq + np_].reshape(-1, D)
-    all_m = every[:, nq + np_ : 2 * nq + np_].reshape(-1, D)[:, :total].astype(f32)
-    scale = 2.7 * D**-0.5
-    scores = mm(all_q, all_p, ((1,), (1,))) * scale
-    shifted = jnp.exp(scores - jnp.max(scores, axis=1, keepdims=True))
-    all_total = jnp.sum(shifted, axis=1, keepdims=True)
-    positive_total = jnp.sum(all_m * shifted, axis=1, keepdims=True)
-    losses = (jnp.log(all_total) - jnp.log(positive_total))[:, 0]
-    ds = (shifted / all_total - all_m * shifted / positive_total).astype(bf16)
-    index = lax.axis_index("dp") * 4 + lax.axis_index("tensor")
-    losses = lax.dynamic_slice_in_dim(losses, index * nq, nq, 0)
-    dcq = mm(lax.dynamic_slice_in_dim(ds, index * nq, nq, 0), all_p, ((1,), (0,))) * scale
-    dcp = mm(lax.dynamic_slice_in_dim(ds, index * np_, np_, 1), all_q, ((0,), (0,))) * scale
-    pad = jnp.zeros((8 - nq, D), f32)
-    dc = jnp.stack([jnp.concatenate([dcq, pad]), jnp.concatenate([dcp, pad])])
-    for e, (cot, x) in enumerate(((question_cotangent, questions), (passage_cotangent, passages))):
-        qkv, p, o, n1, i1, hb, g, d, n2, i2 = kept[e]
-        kept[e] = dict(cot=cot.reshape(-1, D), n2=n2, i2=i2, d=d, g=g, hb=hb, n1=n1, i1=i1, qkv=qkv, o=o, x=x.reshape(-1, D), p=p)
-    sizes = (questions.shape[:2], passages.shape[:2])
-    out, own_rows, small, *dxs = backward(weights, dc, jnp.stack(vecs), kept, sizes, n_dp)
+    own_columns = jnp.arange(D, dtype=jnp.int32)[None, :] // q4 == lax.axis_index("tensor")
+    att_rows = jnp.where(own_columns, jnp.tile(attention_bias.reshape(4, q4), (1, 4)), 0.0)
+    bias_rows = jnp.concatenate([att_rows.astype(bf16), up_bias, jnp.zeros((10, D), bf16)])
+    vec = jnp.concatenate([norm_gains, norm_shifts, branch_biases, jnp.zeros((2, 2, D), bf16)], axis=1).astype(f32)
+    slots = positives.shape[1]
+    live = jnp.arange(slots, dtype=jnp.int32)[None, :] < positive_counts[:, None]
+    named = jnp.where(live, positives, -16)
+    code = jnp.concatenate([named // 16, named % 16], axis=1)
+    code = jnp.pad(code, ((2 * (nq + passages.shape[0]), 16 - 3 * nq - 2 * passages.shape[0]), (0, HALF - 2 * slots))).astype(f32)
+    xs_ = (questions.reshape(-1, D), passages.reshape(-1, D))
+    weights, dc, losses, *made = forward(io, up_weight, down_weight, bias_rows, xs_, vec, code, sizes, n_dp)
+    kept = []
+    for e, cot in enumerate((question_cotangent, passage_cotangent)):
+        kept.append(dict(zip(MADE, made[11 * e : 11 * e + 11]), cot=cot.reshape(-1, D), x=xs_[e]))
+    out, own_rows, small, *dxs = backward(weights, dc, vec, kept, sizes, n_dp)
     res = out.reshape(3, 2, D, D)
     own_small = own_rows[:16].astype(f32)
     rep = small.reshape(4, 16, D)[:, 6:9].reshape(12, D).astype(f32)
     att = lax.dynamic_slice_in_dim(own_small[0:4], lax.axis_index("tensor") * q4, q4, 1)
     return (
-        ys[0].reshape(questions.shape), ys[1].reshape(passages.shape), losses,
+        kept[0]["y"].reshape(questions.shape), kept[1]["y"].reshape(passages.shape), losses[:nq, 0],
         dxs[0].reshape(questions.shape), dxs[1].reshape(passages.shape),
         res[2, :, : 3 * q4].reshape(2, 3, q4, D).transpose(0, 1, 3, 2).astype(f32), att.reshape(2, 2, q4),
         res[2, :, 3 * q4 :].astype(f32), rep[0:4].reshape(2, 2, D), rep[4:8].reshape(2, 2, D), rep[8:12].reshape(2, 2, D),

time: 397 us -> 351 us (0.88)
  Pallas kernels: 360 us -> 317 us
  local copies, waits for them, and re-layouts: 16.5 us -> 11.8 us
    pallas_call x4 -> x1, Pallas kernels: 154 us -> 112 us  [forward(): pl.pallas_call(functools.partial(front_kernel, n, sizes), out_shape=[SDS(...]
    reshape x7 -> x0, local copies, waits for them, and re-layouts: 4.03 us -> none  [the longest x2 2.79 us: body(): jnp.concatenate([full_att[e, 0], nothing[0], full_att[e, 1]])]
where the time goes in v3:
time: 351 us; the launch traced here: 348 us
  Pallas kernels  317 us (90%)
  other arithmetic  18 us (5%)
  local copies, waits for them, and re-layouts  11.8 us (3%)
    pallas_call x1, Pallas kernels, backward(): pl.pallas_call(functools.partial(back_kernel, outer, sizes), out_shape=(S...  205 us
    pallas_call x1, Pallas kernels, forward(): pl.pallas_call(functools.partial(front_kernel, n, sizes), out_shape=[SDS(...  112 us

profile of v3, /device:TPU:0, one launch (start us, length us, event | category | flops | bytes accessed | tf_op | source)
XLA Modules:
  0.0 347.6 jit_solution(15442074773319198401)
XLA Ops:
  0.7 0.1 pad.13.clone
  0.8 0.1 pad.10.clone
  0.8 0.7 tile.10
  1.5 0.8 add_select_fusion.2
  2.3 0.1 pad_add_fusion
  2.4 0.1 tile.12
  2.5 1.4 maximum_maximum_fusion.b_ref
  3.9 0.6 pad_convert_fusion.code_ref
  4.5 1.4 maximum_convert_fusion.vec_ref.refs_2_
  5.9 3.2 pad_maximum_fusion.io_ref
  9.1 111.7 %shard_map.254 = (bf16[2,2,6,768,768]{4,3,2,1,0:T(8,128)(2,1)}, f32[2,16,768]{2,1,0:T(8,128)}, f32[16,128]{1,0:T(8,128)}, bf16[192,768]{1,0:T(8,128)(2,1)}, bf16...) custom-call(bf16[2,768,768]{2,1,0:T(8,128)(2,1)} %pad_maximum_fusion, ...), custom_call_target="tpu_custom_call" | custom-call | tf_op jit(solution)/shard_map/pallas_call | solution.py:920
  120.8 1.3 slice_reduce_fusion
  122.1 205.2 %shard_map.255 = (bf16[18,256,768]{2,1,0:T(8,128)(2,1)}, bf16[64,768]{1,0:T(8,128)(2,1)}, bf16[2,2,16,768]{3,2,1,0:T(8,128)(2,1)}, bf16[192,768]{1,0:T(8,128)(2,1)}, bf16[768,768]{1,0:T(8,128)(2,1)}) custom-call(bf16[2,2,6,768,768]{4,3,2,1,0:T(8,128)(2,1)} %get-tuple-element.47.refs_0_, f32[2,16,768]{2,1,0:T(8,128)} %get-tuple-element.48.refs_1_, ...), custom_call_target="tpu_custom_call" | custom-call | tf_op jit(solution)/shard_map/pallas_call | solution.py:479
  327.4 0.7 slice_convert_fusion.1
  328.1 0.6 slice.57
  328.7 0.1 constant_dynamic-slice_fusion
  328.8 0.6 reshape.128
  329.4 0.9 slice_convert_fusion
  330.3 0.6 reshape.132
  331.0 0.6 reshape.131
  331.6 0.6 reshape.130
  332.2 2.2 fusion
  334.3 0.0 copy-start
  334.3 1.7 slice.50
  336.1 2.1 convert_bitcast_fusion
  338.2 0.8 copy-done
  339.0 0.3 fusion.7
  339.4 0.0 copy-start.3
  339.4 0.0 copy-start.1
  339.4 4.6 %bitcast_convert_fusion = (f32[2,768,768]{2,1,0:T(8,128)}, f32[2,768,768]{2,1,0:T(8,128)}) fusion(bf16[2,768,768]{2,1,0:T(8,128)(2,1)S(1)} %bitcast.29, bf16[2,768,768]{2,1,0:T(8,128)(2,1)S(1)} %bitcast.30), kind=kLoop, calls=%fused_computation.2 | loop fusion | flops 2359296 | bytes 14155776 | tf_op jit(solution)/shard_map/convert_element_type | solution.py:962
  344.0 0.0 copy-start.4
  344.0 0.0 copy-start.2
  344.0 0.0 copy-done.3
  344.0 0.7 copy.33
  344.7 0.0 copy-done.1
  344.7 1.0 copy.34
  345.7 0.0 copy-done.4
  345.7 0.7 copy.35
  346.4 0.0 copy-done.2
  346.4 1.0 copy.36
  (8 shorter events, 0.1 us)
Async XLA Ops:
  334.3 4.7 %copy-start = (bf16[18,256,768]{2,1,0:T(8,128)(2,1)S(1)}, bf16[18,256,768]{2,1,0:T(8,128)(2,1)}, u32[]{:S(2)}) copy-start(bf16[18,256,768]{2,1,0:T(8,128)(2,1)} %get-tuple-element.71) | copy-start | bytes 21233668
  339.4 4.6 %copy-start.3 = (bf16[192,768]{1,0:T(8,128)(2,1)S(1)}, bf16[192,768]{1,0:T(8,128)(2,1)}, u32[]{:S(2)}) copy-start(bf16[192,768]{1,0:T(8,128)(2,1)} %get-tuple-element.44) | copy-start | bytes 884740
  339.4 5.3 %copy-start.1 = (bf16[768,768]{1,0:T(8,128)(2,1)S(1)}, bf16[768,768]{1,0:T(8,128)(2,1)}, u32[]{:S(2)}) copy-start(bf16[768,768]{1,0:T(8,128)(2,1)} %get-tuple-element.45) | copy-start | bytes 3538948
  344.0 1.7 copy-start.4
  344.0 2.5 copy-start.2

commit v4 on v3

--- a/solution.py
+++ b/solution.py
@@ -43,7 +43,7 @@
 MACROS = 18
 STEPS = MACROS * 4 + 1
 VMEM_LIMIT = 64 * 2**20
-LAG = dict(c=2, x=3, y=3, z=2, a=2)
+LAG = dict(c=2, x=3, y=3, z=3, a=3)
 
 
 KEPT = ("cot", "n2", "i2", "d", "g", "hb", "n1", "i1", "qkv", "o", "x", "p")
@@ -58,10 +58,11 @@
 
 
 def back_kernel(outer, sizes, *refs):
-    w_ref, dc_ref, vec_ref = refs[:3]
-    hbm = [dict(zip(KEPT, refs[3 + 12 * e : 15 + 12 * e])) for e in (0, 1)]
-    refs = refs[27:]
-    (out_ref, rows_ref, small_ref, *dx_ref), refs = refs[:5], refs[5:]
+    w_ref, dc_ref, *vec_ref = refs[:5]
+    hbm = [dict(zip(KEPT, refs[5 + 12 * e : 17 + 12 * e])) for e in (0, 1)]
+    refs = refs[29:]
+    (down_out, up_out, io_out, rows_ref, small_ref, *shared_ref), refs = refs[:8], refs[8:]
+    dx_ref, refs = refs[:2], refs[2:]
     buf = []
     for e in (0, 1):
         names = held_names(e) + ("df", "da", "r", "dh", "do")
@@ -93,7 +94,7 @@
     begin(*[load(0, k) for k in ("g", "d")], *[load(1, k) for k in ("hb", "qkv")])
     begin(*[load(0, k) for k in ("hb", "n1", "i1", "qkv", "o", "x", "p")], *weights(1, 0))
 
-    vec = lambda e, i: vec_ref[e, i : i + 1, :]
+    vec = lambda e, i: vec_ref[i // 2][e].astype(f32)[i % 2 : i % 2 + 1]
     col = lambda a: jnp.sum(a, axis=0, keepdims=True)
     sums[...] = jnp.zeros_like(sums)
 
@@ -299,10 +300,11 @@
         c.wait_send()
         c.wait_recv()
 
-    def target(u):
-        m = lax.div(u, 4)
-        g = lax.div(m, 3)
-        return out_ref.at[(lax.div(g, 2) * 2 + 1 - lax.rem(g, 2)) * 3 + lax.rem(m, 3), m16(lax.rem(u, 4) * R, R), half(p["y"])]
+    def targets(u):
+        m, g = lax.div(u, 4), lax.div(u, 12)
+        at = m16(lax.rem(m, 3) * MACRO + lax.rem(u, 4) * R, R)
+        found = [(lax.div(g, 2) == k, ref.at[1 - lax.rem(g, 2), at, half(p["y"])]) for k, ref in enumerate((down_out, up_out, io_out))]
+        return found + [(u == STEPS - 1, rows_ref.at[:, half(p["y"])])]
 
     def w_remote(u, dst):
         k = lax.rem(u, 3 * da)
@@ -319,27 +321,18 @@
 
     def finish(u):
         both(a_all(u))
-
-        @pl.when(u < STEPS - 1)
-        def _():
-            w_remote(u, target(u)).start()
-            w_local(u, target(u)).start()
-
-        @pl.when(u == STEPS - 1)
-        def _():
-            w_remote(u, rows_ref.at[:, half(p["y"])]).start()
-            w_local(u, rows_ref.at[:, half(p["y"])]).start()
+        for here, dst in targets(u):
+            @pl.when(here)
+            def _():
+                w_remote(u, dst).start()
+                w_local(u, dst).start()
 
     def finished(u):
-        @pl.when(u < STEPS - 1)
-        def _():
-            both(w_remote(u, target(u)))
-            w_local(u, target(u)).wait()
-
-        @pl.when(u == STEPS - 1)
-        def _():
-            both(w_remote(u, rows_ref.at[:, half(p["y"])]))
-            w_local(u, rows_ref.at[:, half(p["y"])]).wait()
+        for here, dst in targets(u):
+            @pl.when(here)
+            def _():
+                both(w_remote(u, dst))
+                w_local(u, dst).wait()
 
     def take_z(u):
         both(z_all(u))
@@ -462,6 +455,9 @@
     for i, (a, b) in enumerate(((x, 1 - c), (1 - x, c), (1 - x, 1 - c))):
         sends[i].wait_send()
         remote(own, small_ref.at[a, b], t_ss.at[i], t_rs.at[i], sib).wait_recv()
+    got = [small_ref[t // 2, t % 2].astype(f32) for t in range(4)]
+    for r in range(12):
+        shared_ref[r // 4][(r // 2) % 2, r % 2 : r % 2 + 1] = got[r // 3][6 + r % 3 : 7 + r % 3]
 
 
 def backward(w_all, dc, vec, kept, sizes, dp, cid=3):
@@ -475,13 +471,13 @@
         n = sizes[e][0] * sizes[e][1]
         scratch += [vm(kept[e][k].shape, kept[e][k].dtype) for k in held_names(e)]
         scratch += [vm((n, D)), vm((n, D)), vm((n, D), f32), vm((n, D), f32), vm((D, n))]
-    args = [w_all, dc, vec] + [kept[e][k] for e in (0, 1) for k in KEPT]
+    args = [w_all, dc, *vec] + [kept[e][k] for e in (0, 1) for k in KEPT]
     return pl.pallas_call(
         functools.partial(back_kernel, outer, sizes),
-        out_shape=(SDS((MACROS, MACRO, D), bf16), SDS((R, D), bf16), SDS((2, 2, 16, D), bf16),
+        out_shape=(*[SDS((2, D, D), bf16)] * 3, SDS((R, D), bf16), SDS((2, 2, 16, D), bf16), *[SDS((2, 2, D), f32)] * 3,
                    SDS(kept[0]["x"].shape, bf16), SDS(kept[1]["x"].shape, bf16)),
-        in_specs=[ANY, VM, VM] + [ANY] * 24,
-        out_specs=(ANY, VM, VM, ANY, ANY),
+        in_specs=[ANY] + [VM] * 4 + [ANY] * 24,
+        out_specs=(ANY, ANY, ANY, VM, VM, VM, VM, VM, ANY, ANY),
         scratch_shapes=scratch + [
             vm(kept[0]["p"].shape), *[vm(s) for s in W_SHAPES], vm((2, 16, D), f32), dma((2, 12)), dma((2,)), dma((24,)),
             vm((2, 2, 2, MACRO, D)), vm((2 * lc, 2, R, D)), vm((2 * lx, 2, R, D)), vm((2 * lx, R, D)),
@@ -569,6 +565,8 @@
 
 CH = 6
 PLAN = ((0, 1), (1, 1), (2, 1), (0, 0), (1, 0), (2, 0))
+PIECES = [(h, 0, D) for h in range(CH)]
+NP_ = len(PIECES)
 MADE = ("y", "qkv", "p", "o", "n1", "i1", "hb", "g", "d", "n2", "i2")
 
 
@@ -579,7 +577,8 @@
                 hb=(t, D), g=(4, t, D), d=(4, t, D), n2=(t, D), i2=(t, 1))
 
 
-def front_kernel(n, sizes, io_ref, up_ref, down_ref, b_ref, x0_ref, x1_ref, vec_ref, code_ref, *refs):
+def front_kernel(n, sizes, io_ref, up_ref, down_ref, b_ref, x0_ref, x1_ref, *refs):
+    (*vec_ref, code_ref), refs = refs[:4], refs[4:]
     (out_ref, dc_ref, loss_ref), refs = refs[:3], refs[3:]
     hbm = [dict(zip(MADE, refs[11 * e : 11 * e + 11])) for e in (0, 1)]
     refs = refs[22:]
@@ -587,7 +586,7 @@
     refs = refs[22:]
     (h0, f0, h1, f1, win, wout, up, down, bias_ref, bias_in, held, cls, full, codes, pay, w_sem, made_sem,
      x_ss, x_rs, y_ss, y_rs, z_ss, z_rs, y2_ss, y2_rs, z2_ss, z2_rs, sib_ss, sib_rs, f_ss, f_rs, b_ss, b_rs, in_sem, back_sem,
-     r_ss, r_rs, g_ss, g_rs) = refs
+     r_ss, r_rs, g_ss, g_rs, x2_ss, x2_rs) = refs
     xin, hs, fs = (x0_ref, x1_ref), (h0, h1), (f0, f1)
     p = place()
     zb = lax.rem(p["z"], 2)
@@ -598,9 +597,14 @@
     group4 = [lax.rem(p["t"] + j, 4) for j in range(1, 4)]
     greet([(q, p["t"]) for q in ring] + [(p["dp"], q) for q in group4])
     x, c, y = p["x"], p["c"], p["y"]
-    quarter, half = D // 4, D // 8
-    rows = lambda q: pl.ds(pl.multiple_of(q * quarter, 16), quarter)
-    hrows = lambda q, k: pl.ds(pl.multiple_of(q * quarter + k * half, 16), half)
+    def rows(i, q):
+        _, r, k = PIECES[i]
+        return pl.ds(pl.multiple_of(r + q * (k // 4), 16), k // 4)
+
+    def hrows(i, q, j):
+        _, r, k = PIECES[i]
+        return pl.ds(pl.multiple_of(r + q * (k // 4) + j * (k // 12), 16), k // 12)
+
     mine, qy, qz, dg = y * 2 + zb, (1 - y) * 2 + zb, y * 2 + 1 - zb, (1 - y) * 2 + 1 - zb
     source = lambda h: (io_ref, up_ref, down_ref)[PLAN[h][0]].at[PLAN[h][1]]
     started = []
@@ -611,9 +615,15 @@
 
     for i, dev in enumerate((sib, xp, diag)):
         go(remote(b_ref, bias_ref.at[x, c], b_ss.at[i], b_rs.at[i], dev))
-    for h in range(CH):
-        go(remote(source(h).at[rows(mine)], out_ref.at[x, c, h, rows(mine)], x_ss.at[h], x_rs.at[h], xp))
-        go(remote(source(h), out_ref.at[x, c, h], sib_ss.at[h], sib_rs.at[h], sib))
+    for i in range(NP_ + 1):
+        if i < NP_:
+            h = PIECES[i][0]
+            go(remote(source(h).at[rows(i, mine)], out_ref.at[x, c, h, rows(i, mine)], x_ss.at[i], x_rs.at[i], xp))
+            if PIECES[i][1] == 0:
+                go(remote(source(h), out_ref.at[x, c, h], sib_ss.at[h], sib_rs.at[h], sib))
+        if i > 0:
+            h, r = PIECES[i - 1][0], hrows(i - 1, dg, 2)
+            go(remote(source(h).at[r], out_ref.at[x, c, h, r], x2_ss.at[i - 1], x2_rs.at[i - 1], xp))
     ins = [pltpu.make_async_copy(source(h), held.at[h % 2], in_sem.at[h]) for h in range(CH)]
     backs = [pltpu.make_async_copy(held.at[h % 2], out_ref.at[x, c, h], back_sem.at[h]) for h in range(CH)]
     ins[0].start()
@@ -626,39 +636,42 @@
             backs[h].wait()
             ins[h + 2].start()
 
-    def whole(h, q, ss, rs, dev):
-        a = out_ref.at[1 - x, c, h, rows(q)]
+    def whole(i, q, ss, rs, dev):
+        a = out_ref.at[1 - x, c, PIECES[i][0], rows(i, q)]
         return remote(a, a, ss, rs, dev)
 
-    def part(h, q, k, ss, rs, dev):
-        a = out_ref.at[1 - x, c, h, hrows(q, k)]
-        return remote(a, a, ss.at[h], rs.at[h], dev)
-
-    def first(h):
-        whole(h, mine, x_ss.at[h], x_rs.at[h], xp).wait_recv()
-        go(whole(h, mine, y_ss.at[h], y_rs.at[h], yp))
-        go(whole(h, mine, z_ss.at[h], z_rs.at[h], zp))
-        go(whole(h, mine, f_ss.at[h, 0], f_rs.at[h, 0], sib))
-
-    def second(h):
-        whole(h, qy, y_ss.at[h], y_rs.at[h], yp).wait_recv()
-        go(part(h, qy, 1, z2_ss, z2_rs, zp))
-        go(whole(h, qy, f_ss.at[h, 1], f_rs.at[h, 1], sib))
-        whole(h, qz, z_ss.at[h], z_rs.at[h], zp).wait_recv()
-        go(part(h, qz, 0, y2_ss, y2_rs, yp))
-        go(whole(h, qz, f_ss.at[h, 2], f_rs.at[h, 2], sib))
-
-    def third(h):
-        part(h, dg, 0, y2_ss, y2_rs, yp).wait_recv()
-        part(h, dg, 1, z2_ss, z2_rs, zp).wait_recv()
-        go(whole(h, dg, f_ss.at[h, 3], f_rs.at[h, 3], sib))
+    def part(i, q, k, ss, rs, dev):
+        a = out_ref.at[1 - x, c, PIECES[i][0], hrows(i, q, k)]
+        return remote(a, a, ss.at[i], rs.at[i], dev)
+
+    def first(i):
+        whole(i, mine, x_ss.at[i], x_rs.at[i], xp).wait_recv()
+        go(whole(i, mine, y_ss.at[i], y_rs.at[i], yp))
+        go(whole(i, mine, z_ss.at[i], z_rs.at[i], zp))
+        go(whole(i, mine, f_ss.at[i, 0], f_rs.at[i, 0], sib))
+
+    def second(i):
+        whole(i, qy, y_ss.at[i], y_rs.at[i], yp).wait_recv()
+        go(part(i, qy, 1, z2_ss, z2_rs, zp))
+        whole(i, qz, z_ss.at[i], z_rs.at[i], zp).wait_recv()
+        go(part(i, qz, 0, y2_ss, y2_rs, yp))
+        go(whole(i, qy, f_ss.at[i, 1], f_rs.at[i, 1], sib))
+        go(whole(i, qz, f_ss.at[i, 2], f_rs.at[i, 2], sib))
+
+    def third(i):
+        part(i, dg, 0, y2_ss, y2_rs, yp).wait_recv()
+        part(i, dg, 1, z2_ss, z2_rs, zp).wait_recv()
+        part(i, dg, 2, x2_ss, x2_rs, xp).wait_recv()
+        go(whole(i, dg, f_ss.at[i, 3], f_rs.at[i, 3], sib))
 
     def arrived(h):
         a = out_ref.at[x, 1 - c, h]
         remote(a, a, sib_ss.at[h], sib_rs.at[h], sib).wait_recv()
-        for i, q in enumerate((mine, qy, qz, dg)):
-            a = out_ref.at[1 - x, 1 - c, h, rows(q)]
-            remote(a, a, f_ss.at[h, i], f_rs.at[h, i], sib).wait_recv()
+        for i in range(NP_):
+            if PIECES[i][0] == h:
+                for j, q in enumerate((mine, qy, qz, dg)):
+                    a = out_ref.at[1 - x, 1 - c, h, rows(i, q)]
+                    remote(a, a, f_ss.at[i, j], f_rs.at[i, j], sib).wait_recv()
         if h >= CH - 2:
             backs[h].wait()
 
@@ -680,7 +693,7 @@
             keeps.append(cp)
 
     keeps = []
-    vec = lambda e, i: vec_ref[e, i : i + 1, :]
+    vec = lambda e, i: vec_ref[i // 2][e].astype(f32)[i % 2 : i % 2 + 1]
 
     def tokens(e, b):
         m = spot(*sizes[e])[0]
@@ -743,90 +756,105 @@
     def projects(e, a, b):
         lax.fori_loop(a, b, lambda i, cc: (project(e, i), cc)[1], 0)
 
-    def attend(e, g):
-        loop(6, lambda i: heads(e, g, i))
-
-    bounce(0)
-    bounce(1)
-    first(0)
-    bounce(2)
-    bounce(3)
-    for i, (a, b) in enumerate(((x, 1 - c), (1 - x, c), (1 - x, 1 - c))):
-        remote(b_ref, bias_ref.at[a, b], b_ss.at[i], b_rs.at[i], sib).wait_recv()
-    for e in (0, 1):
-        for j in range(3):
-            if j == 1:
-                bias_in[e, j] = jnp.zeros((16, D), bf16)
-            else:
-                r = 2 * e + j // 2
-                got = [bias_ref[t // 2, t % 2].astype(f32)[r : r + 1] for t in range(4)]
-                bias_in[e, j] = jnp.concatenate(got + [jnp.zeros((12, D), f32)], axis=0).astype(bf16)
-    first(1)
-    second(0)
-    bounce(4)
-    bounce(5)
-    first(2)
-    second(1)
-    third(0)
-    arrived(0)
-    begin(*weights(1, 0), *weights(1, 1))
-    ready(*weights(1, 0))
-    projects(1, 0, 4)
-    first(3)
-    projects(1, 4, 9)
-    second(2)
-    attend(1, 0)
-    third(1)
-    arrived(1)
-    first(4)
-    begin(*weights(1, 2))
-    attend(1, 1)
-    second(3)
-    first(5)
-    attend(1, 2)
-    keep(1, "qkv", "p", "o")
-    third(2)
-    arrived(2)
-    begin(*weights(1, 3))
-    ready(*weights(1, 1))
-    for b in range(3):
-        out_norm(1, b)
-    second(4)
-    keep(1, "n1", "i1", "hb")
-    ready(*weights(1, 2), *weights(1, 3))
-    for i in range(4):
-        for b in range(3):
-            hidden(1, i, b)
-            shrink(1, i, b)
-        if i == 0:
-            third(3)
-            arrived(3)
-            begin(*weights(0, 0), *weights(0, 1))
-        if i == 1:
-            second(5)
-        if i == 2:
-            third(4)
-            arrived(4)
-    keep(1, "g", "d")
-    begin(*weights(0, 2))
-    third(5)
-    arrived(5)
-    begin(*weights(0, 3))
-    for b in range(3):
-        norm2(1, b)
-    keep(1, "y", "n2", "i2")
-    ready(*weights(0, 0))
-    projects(0, 0, 9)
-    attend(0, 0)
-    keep(0, "qkv", "p", "o")
-    ready(*weights(0, 1))
-    out_norm(0, 0)
-    keep(0, "n1", "i1", "hb")
-    ready(*weights(0, 2), *weights(0, 3))
-    for i in range(4):
-        hidden(0, i, 0)
-        shrink(0, i, 0)
-    norm2(0, 0)
+    def biases():
+        for i, (a, b) in enumerate(((x, 1 - c), (1 - x, c), (1 - x, 1 - c))):
+            remote(b_ref, bias_ref.at[a, b], b_ss.at[i], b_rs.at[i], sib).wait_recv()
+        for e in (0, 1):
+            for j in range(3):
+                if j == 1:
+                    bias_in[e, j] = jnp.zeros((16, D), bf16)
+                else:
+                    r = 2 * e + j // 2
+                    got = [bias_ref[t // 2, t % 2].astype(f32)[r : r + 1] for t in range(4)]
+                    bias_in[e, j] = jnp.concatenate(got + [jnp.zeros((12, D), f32)], axis=0).astype(bf16)
+
+    def attend(e, g, lo, hi):
+        lax.fori_loop(lo, hi, lambda i, cc: (heads(e, g, i), cc)[1], 0)
+
+    tasks = []
+
+    def task(name, us, needs, fn):
+        tasks.append((name, us, tuple(needs), fn))
+
+    for h in range(2):
+        task(f"bounce{h}", 1.0, (), functools.partial(bounce, h))
+    task("biases", 0.3, (), biases)
+    for h in range(2, CH):
+        task(f"bounce{h}", 1.0, (f"bounce{h - 2}",), functools.partial(bounce, h))
+    for e in (1, 0):
+        base = 0 if e else 3
+        k, blocks, groups = (1.0, 3, 3) if e else (0.45, 1, 1)
+        free = lambda *names: () if e else names
+        task(f"w0{e}", 0.3, (f"arrived{base}", *free("project1")), lambda e=e: begin(*weights(e, 0)))
+        task(f"w1{e}", 0.1, (f"arrived{base}", *free("out1")), lambda e=e: begin(*weights(e, 1)))
+        task(f"w2{e}", 0.1, (f"arrived{base + 1}", *free("hidden1")), lambda e=e: begin(*weights(e, 2)))
+        task(f"w3{e}", 0.1, (f"arrived{base + 2}", *free("shrink1")), lambda e=e: begin(*weights(e, 3)))
+        task(f"r0{e}", 0.8, (f"w0{e}", "biases"), lambda e=e: ready(*weights(e, 0)))
+        for i in range(3):
+            last = "project%d" % e if i == 2 else "project%d_%d" % (e, i)
+            task(last, 2.2 * k, (f"r0{e}",), lambda e=e, i=i: projects(e, 3 * i, 3 * i + 3))
+        for g in range(groups):
+            for half_ in (0, 1):
+                task(f"att{e}_{g}_{half_}", 2.6, (f"project{e}",), lambda e=e, g=g, q=half_: attend(e, g, 3 * q, 3 * q + 3))
+        every = [f"att{e}_{g}_{q}" for g in range(groups) for q in (0, 1)]
+        task(f"keepa{e}", 0.1, every, lambda e=e: keep(e, "qkv", "p", "o"))
+        task(f"r1{e}", 0.3, (f"w1{e}", *every), lambda e=e: ready(*weights(e, 1)))
+        for b in range(blocks):
+            task(f"out{e}" if b == blocks - 1 else f"out{e}_{b}", 1.4, (f"r1{e}",), lambda e=e, b=b: out_norm(e, b))
+        task(f"keepb{e}", 0.1, (f"out{e}",), lambda e=e: keep(e, "n1", "i1", "hb"))
+        task(f"r2{e}", 0.6, (f"w2{e}", f"out{e}"), lambda e=e: ready(*weights(e, 2)))
+        task(f"r3{e}", 0.6, (f"w3{e}", f"out{e}"), lambda e=e: ready(*weights(e, 3)))
+        for i in range(4):
+            for b in range(blocks):
+                end = i == 3 and b == blocks - 1
+                task(f"hidden{e}" if end else f"hidden{e}_{i}_{b}", 1.2, (f"r2{e}",), lambda e=e, i=i, b=b: hidden(e, i, b))
+        for i in range(4):
+            for b in range(blocks):
+                end = i == 3 and b == blocks - 1
+                task(f"shrink{e}" if end else f"shrink{e}_{i}_{b}", 0.6,
+                     (f"r3{e}", "hidden%d" % e if i == 3 and b == blocks - 1 else f"hidden{e}_{i}_{b}"),
+                     lambda e=e, i=i, b=b: shrink(e, i, b))
+        task(f"keepc{e}", 0.1, (f"hidden{e}",), lambda e=e: keep(e, "g", "d"))
+        for b in range(blocks):
+            task(f"norm{e}" if b == blocks - 1 else f"norm{e}_{b}", 0.8, (f"shrink{e}",), lambda e=e, b=b: norm2(e, b))
+        task(f"keepd{e}", 0.1, (f"norm{e}",), lambda e=e: keep(e, "y", "n2", "i2"))
+
+    span_ = [k * 2 * D * 2 / 4 / 75e3 for _, _, k in PIECES]
+    at_x, at_x2, t_ = {}, {}, 3.0
+    for i in range(NP_ + 1):
+        if i < NP_:
+            t_ += span_[i]
+            at_x[i] = t_ + 1.5
+        if i > 0:
+            t_ += span_[i - 1] / 3
+            at_x2[i - 1] = t_ + 1.5
+    order = [("f", 0)]
+    for i in range(NP_ + 2):
+        order += [("f", i + 1)] if i + 1 < NP_ else []
+        order += [("s", i)] if i < NP_ else []
+        order += [("t", i - 1)] if 0 <= i - 1 < NP_ else []
+    line, landed, done, now = 3.0, {}, set(), 3.0
+    comm = {"f": first, "s": second, "t": third}
+    while order or tasks:
+        kind, i = order[0] if order else (None, None)
+        due = {"f": lambda: at_x[i], "s": lambda: landed["f", i], "t": lambda: max(landed["s", i], at_x2[i])}[kind]() if kind else 1e9
+        pick = next((k for k in tasks if all(d in done for d in k[2])), None)
+        if due <= now or pick is None:
+            now = max(now, due) + 0.25
+            comm[kind](i)
+            order.pop(0)
+            if kind in "fs":
+                line = max(line, now) + span_[i] / (1 if kind == "f" else 3)
+                landed[kind, i] = line + 1.5
+            elif i + 1 == NP_ or PIECES[i + 1][0] != PIECES[i][0]:
+                arrived(PIECES[i][0])
+                now += 0.8
+                done.add(f"arrived{PIECES[i][0]}")
+        else:
+            pick[3]()
+            now += pick[1]
+            done.add(pick[0])
+            tasks.remove(pick)
     nq, np_ = sizes[0][0], sizes[1][0]
     got = [buf[e]["y"][i * sizes[e][1] : i * sizes[e][1] + 16, :].astype(f32)[0:1] for e in (0, 1) for i in range(sizes[e][0])]
     blank = jnp.zeros((16 - 2 * (nq + np_), HALF), f32)
@@ -836,7 +864,6 @@
     cls[place_of(p["t"], p["dp"]), :] = pay[...]
     for j, q in enumerate(ring):
         go(remote(pay, here, r_ss.at[j], r_rs.at[n - 2 - j], (q, p["t"])))
-    keep(0, "g", "d", "y", "n2", "i2")
     for j, q in enumerate(ring):
         remote(pay, cls.at[place_of(p["t"], q)], r_ss.at[j], r_rs.at[j], (q, p["t"])).wait_recv()
     band = lambda x_, c_: cls.at[pl.ds(pl.multiple_of((x_ * 2 + c_) * n * 16, 16), n * 16)]
@@ -920,13 +947,13 @@
     return pl.pallas_call(
         functools.partial(front_kernel, n, sizes),
         out_shape=[SDS((2, 2, CH, D, D), bf16), SDS((2, 16, D), f32), SDS((16, 128), f32)] + outs,
-        in_specs=[ANY, ANY, ANY, VM, VM, VM, VM, VM],
+        in_specs=[ANY] * 3 + [VM] * 7,
         out_specs=[ANY, VM, VM] + [ANY] * 22,
         scratch_shapes=scratch + [vm(s) for s in W_SHAPES] + [
             vm((2, 2, 16, D)), vm((2, 3, 16, D)), vm((2, D, D)), vm((4 * n * 16, HALF)), vm((4 * n * 16, D)), vm((4 * n * 16, 128), f32), vm((16, HALF)), dma((24,)), dma((2, 11))]
-        + [dma((CH,))] * 12 + [dma((CH, 4))] * 2 + [dma((3,))] * 2 + [dma((CH,))] * 2 + [dma((n - 1,))] * 2 + [dma((3,))] * 2,
+        + [dma((NP_,))] * 10 + [dma((CH,))] * 2 + [dma((NP_, 4))] * 2 + [dma((3,))] * 2 + [dma((CH,))] * 2 + [dma((n - 1,))] * 2 + [dma((3,))] * 2 + [dma((NP_,))] * 2,
         compiler_params=pltpu.CompilerParams(collective_id=cid, has_side_effects=True, vmem_limit_bytes=VMEM_LIMIT),
-    )(io, up, down, bias_rows, *xs_, vec, code)
+    )(io, up, down, bias_rows, *xs_, *vec, code)
 
 
 def body(n_dp, questions, passages, question_cotangent, passage_cotangent, positives, positive_counts,
@@ -938,7 +965,7 @@
     own_columns = jnp.arange(D, dtype=jnp.int32)[None, :] // q4 == lax.axis_index("tensor")
     att_rows = jnp.where(own_columns, jnp.tile(attention_bias.reshape(4, q4), (1, 4)), 0.0)
     bias_rows = jnp.concatenate([att_rows.astype(bf16), up_bias, jnp.zeros((10, D), bf16)])
-    vec = jnp.concatenate([norm_gains, norm_shifts, branch_biases, jnp.zeros((2, 2, D), bf16)], axis=1).astype(f32)
+    vec = (norm_gains, norm_shifts, branch_biases)
     slots = positives.shape[1]
     live = jnp.arange(slots, dtype=jnp.int32)[None, :] < positive_counts[:, None]
     named = jnp.where(live, positives, -16)
@@ -949,17 +976,15 @@
     kept = []
     for e, cot in enumerate((question_cotangent, passage_cotangent)):
         kept.append(dict(zip(MADE, made[11 * e : 11 * e + 11]), cot=cot.reshape(-1, D), x=xs_[e]))
-    out, own_rows, small, *dxs = backward(weights, dc, vec, kept, sizes, n_dp)
-    res = out.reshape(3, 2, D, D)
+    down_g, up_g, io_g, own_rows, _, branch_g, gains_g, shifts_g, *dxs = backward(weights, dc, vec, kept, sizes, n_dp)
     own_small = own_rows[:16].astype(f32)
-    rep = small.reshape(4, 16, D)[:, 6:9].reshape(12, D).astype(f32)
     att = lax.dynamic_slice_in_dim(own_small[0:4], lax.axis_index("tensor") * q4, q4, 1)
     return (
         kept[0]["y"].reshape(questions.shape), kept[1]["y"].reshape(passages.shape), losses[:nq, 0],
         dxs[0].reshape(questions.shape), dxs[1].reshape(passages.shape),
-        res[2, :, : 3 * q4].reshape(2, 3, q4, D).transpose(0, 1, 3, 2).astype(f32), att.reshape(2, 2, q4),
-        res[2, :, 3 * q4 :].astype(f32), rep[0:4].reshape(2, 2, D), rep[4:8].reshape(2, 2, D), rep[8:12].reshape(2, 2, D),
-        res[1].astype(f32), own_small[4:6], res[0].astype(f32))
+        io_g[:, : 3 * q4].reshape(2, 3, q4, D).transpose(0, 1, 3, 2).astype(f32), att.reshape(2, 2, q4),
+        io_g[:, 3 * q4 :].astype(f32), branch_g, gains_g, shifts_g,
+        up_g.astype(f32), own_small[4:6], down_g.astype(f32))
 
 
 def solution(mesh):

time: 351 us -> 337 us (0.960)
  Pallas kernels: 317 us -> 305 us
    pallas_call x1, Pallas kernels: 205 us -> 195 us  [backward(): pl.pallas_call(functools.partial(back_kernel, outer, sizes), out_shape=(*...]
    convert_element_type x5 -> x4, other arithmetic: 11.2 us -> 9.36 us  [the longest x1 2.55 us: body(): down_g.astype(f32)]
where the time goes in v4:
time: 337 us; the launch traced here: 333 us
  Pallas kernels  305 us (91%)
  other arithmetic  16.2 us (5%)
  local copies, waits for them, and re-layouts  10.8 us (3%)
    pallas_call x1, Pallas kernels, backward(): pl.pallas_call(functools.partial(back_kernel, outer, sizes), out_shape=(*...  195 us
    pallas_call x1, Pallas kernels, forward(): pl.pallas_call(functools.partial(front_kernel, n, sizes), out_shape=[SDS(...  110 us

profile of v4, /device:TPU:0, one launch (start us, length us, event | category | flops | bytes accessed | tf_op | source)
XLA Modules:
  0.0 332.8 jit_solution(18249029568064681630)
XLA Ops:
  0.7 0.1 pad.9.clone
  0.8 0.7 tile.10
  1.5 0.8 add_select_fusion.2
  2.2 0.1 pad_add_fusion
  2.3 0.1 tile.12
  2.4 1.4 maximum_maximum_fusion.b_ref
  3.8 0.6 pad_convert_fusion.refs_3_
  4.4 3.2 pad_maximum_fusion.io_ref
  7.6 109.7 %shard_map.254 = (bf16[2,2,6,768,768]{4,3,2,1,0:T(8,128)(2,1)}, f32[2,16,768]{2,1,0:T(8,128)}, f32[16,128]{1,0:T(8,128)}, bf16[192,768]{1,0:T(8,128)(2,1)}, bf16...) custom-call(bf16[2,768,768]{2,1,0:T(8,128)(2,1)} %pad_maximum_fusion, ...), custom_call_target="tpu_custom_call" | custom-call | tf_op jit(solution)/shard_map/pallas_call | solution.py:947
  117.3 1.3 slice_reduce_fusion
  118.6 195.2 %shard_map.255 = (bf16[2,768,768]{2,1,0:T(8,128)(2,1)}, bf16[2,768,768]{2,1,0:T(8,128)(2,1)}, bf16[2,768,768]{2,1,0:T(8,128)(2,1)}, bf16[64,768]{1,0:T(8,128)(2,...) custom-call(bf16[2,2,6,768,768]{4,3,2,1,0:T(8,128)(2,1)} %get-tuple-, ...), custom_call_target="tpu_custom_call" | custom-call | tf_op jit(solution)/shard_map/pallas_call | solution.py:475
  313.8 0.7 slice_convert_fusion.1
  314.6 0.6 slice.25
  315.2 0.1 constant_dynamic-slice_fusion
  315.3 0.6 reshape.100
  315.9 2.2 slice_convert_fusion
  318.0 1.6 slice.19
  319.6 0.0 copy-start.1
  319.6 2.1 convert_bitcast_fusion
  321.7 0.5 copy-done.1
  322.2 0.0 copy-start
  322.2 2.5 convert_element_type.32
  324.8 0.0 copy-done
  324.8 0.0 copy-start.4
  324.8 0.0 copy-start.2
  324.8 2.5 convert_element_type.33
  327.3 0.0 copy-done.4
  327.3 0.0 copy-start.5
  327.3 0.0 copy-start.3
  327.3 0.7 copy.36
  328.0 0.0 copy-done.2
  328.0 0.0 copy-start.8
  328.1 0.0 copy-start.7
  328.1 0.0 copy-start.6
  328.1 1.0 copy.37
  329.1 0.0 copy-done.5
  329.1 0.7 copy.38
  329.8 0.0 copy-done.3
  329.8 1.0 copy.39
  330.8 0.0 copy-done.8
  330.8 0.6 copy.40
  331.4 0.0 copy-done.7
  331.4 0.6 copy.41
  332.0 0.0 copy-done.6
  332.0 0.6 copy.42
  (5 shorter events, 0.0 us)
Async XLA Ops:
  319.6 2.6 copy-start.1
  322.2 2.6 copy-start
  324.8 2.6 copy-start.4
  324.8 3.3 copy-start.2
  327.3 1.7 copy-start.5
  327.3 2.5 copy-start.3
  328.0 2.8 copy-start.8
  328.1 3.4 %copy-start.7 = (f32[2,2,768]{2,1,0:T(2,128)S(1)}, f32[2,2,768]{2,1,0:T(2,128)}, u32[]{:S(2)}) copy-start(f32[2,2,768]{2,1,0:T(2,128)} %get-tuple-element.107) | copy-start | bytes 36868
  328.1 4.0 %copy-start.6 = (f32[2,2,768]{2,1,0:T(2,128)S(1)}, f32[2,2,768]{2,1,0:T(2,128)}, u32[]{:S(2)}) copy-start(f32[2,2,768]{2,1,0:T(2,128)} %get-tuple-element.108) | copy-start | bytes 36868

commit v5 on v4

--- a/solution.py
+++ b/solution.py
@@ -61,7 +61,7 @@
     w_ref, dc_ref, *vec_ref = refs[:5]
     hbm = [dict(zip(KEPT, refs[5 + 12 * e : 17 + 12 * e])) for e in (0, 1)]
     refs = refs[29:]
-    (down_out, up_out, io_out, rows_ref, small_ref, *shared_ref), refs = refs[:8], refs[8:]
+    (down_out, up_out, in_out, wo_out, rows_ref, small_ref, *shared_ref), refs = refs[:9], refs[9:]
     dx_ref, refs = refs[:2], refs[2:]
     buf = []
     for e in (0, 1):
@@ -302,9 +302,12 @@
 
     def targets(u):
         m, g = lax.div(u, 4), lax.div(u, 12)
-        at = m16(lax.rem(m, 3) * MACRO + lax.rem(u, 4) * R, R)
-        found = [(lax.div(g, 2) == k, ref.at[1 - lax.rem(g, 2), at, half(p["y"])]) for k, ref in enumerate((down_out, up_out, io_out))]
-        return found + [(u == STEPS - 1, rows_ref.at[:, half(p["y"])])]
+        r, e, kind = lax.rem(m, 3) * MACRO + lax.rem(u, 4) * R, 1 - lax.rem(g, 2), lax.div(g, 2)
+        whole = [(kind == k, ref.at[e, m16(r, R), half(p["y"])]) for k, ref in enumerate((down_out, up_out))]
+        split = 3 * D // 4
+        parts = [(jnp.logical_and(kind == 2, r < split), in_out.at[e, m16(r, R), half(p["y"])]),
+                 (jnp.logical_and(kind == 2, r >= split), wo_out.at[e, m16(r - split, R), half(p["y"])])]
+        return whole + parts + [(u == STEPS - 1, rows_ref.at[:, half(p["y"])])]
 
     def w_remote(u, dst):
         k = lax.rem(u, 3 * da)
@@ -474,10 +477,10 @@
     args = [w_all, dc, *vec] + [kept[e][k] for e in (0, 1) for k in KEPT]
     return pl.pallas_call(
         functools.partial(back_kernel, outer, sizes),
-        out_shape=(*[SDS((2, D, D), bf16)] * 3, SDS((R, D), bf16), SDS((2, 2, 16, D), bf16), *[SDS((2, 2, D), f32)] * 3,
+        out_shape=(*[SDS((2, D, D), bf16)] * 2, SDS((2, 3 * D // 4, D), bf16), SDS((2, D // 4, D), bf16), SDS((R, D), bf16), SDS((2, 2, 16, D), bf16), *[SDS((2, 2, D), f32)] * 3,
                    SDS(kept[0]["x"].shape, bf16), SDS(kept[1]["x"].shape, bf16)),
         in_specs=[ANY] + [VM] * 4 + [ANY] * 24,
-        out_specs=(ANY, ANY, ANY, VM, VM, VM, VM, VM, ANY, ANY),
+        out_specs=(ANY, ANY, ANY, ANY, VM, VM, VM, VM, VM, ANY, ANY),
         scratch_shapes=scratch + [
             vm(kept[0]["p"].shape), *[vm(s) for s in W_SHAPES], vm((2, 16, D), f32), dma((2, 12)), dma((2,)), dma((24,)),
             vm((2, 2, 2, MACRO, D)), vm((2 * lc, 2, R, D)), vm((2 * lx, 2, R, D)), vm((2 * lx, R, D)),
@@ -976,14 +979,14 @@
     kept = []
     for e, cot in enumerate((question_cotangent, passage_cotangent)):
         kept.append(dict(zip(MADE, made[11 * e : 11 * e + 11]), cot=cot.reshape(-1, D), x=xs_[e]))
-    down_g, up_g, io_g, own_rows, _, branch_g, gains_g, shifts_g, *dxs = backward(weights, dc, vec, kept, sizes, n_dp)
+    down_g, up_g, in_g, wo_g, own_rows, _, branch_g, gains_g, shifts_g, *dxs = backward(weights, dc, vec, kept, sizes, n_dp)
     own_small = own_rows[:16].astype(f32)
     att = lax.dynamic_slice_in_dim(own_small[0:4], lax.axis_index("tensor") * q4, q4, 1)
     return (
         kept[0]["y"].reshape(questions.shape), kept[1]["y"].reshape(passages.shape), losses[:nq, 0],
         dxs[0].reshape(questions.shape), dxs[1].reshape(passages.shape),
-        io_g[:, : 3 * q4].reshape(2, 3, q4, D).transpose(0, 1, 3, 2).astype(f32), att.reshape(2, 2, q4),
-        io_g[:, 3 * q4 :].astype(f32), branch_g, gains_g, shifts_g,
+        in_g.reshape(2, 3, q4, D).transpose(0, 1, 3, 2).astype(f32), att.reshape(2, 2, q4),
+        wo_g.astype(f32), branch_g, gains_g, shifts_g,
         up_g.astype(f32), own_small[4:6], down_g.astype(f32))
 
 

time: 337 us -> 336 us (level)
  no operation moved by 1% of the time
where the time goes in v5:
time: 336 us; the launch traced here: 331 us
  Pallas kernels  305 us (91%)
  other arithmetic  16.3 us (5%)
  local copies, waits for them, and re-layouts  9.25 us (3%)
    pallas_call x1, Pallas kernels, backward(): pl.pallas_call(functools.partial(back_kernel, outer, sizes), out_shape=(*...  195 us
    pallas_call x1, Pallas kernels, forward(): pl.pallas_call(functools.partial(front_kernel, n, sizes), out_shape=[SDS(...  110 us

profile of v5, /device:TPU:0, one launch (start us, length us, event | category | flops | bytes accessed | tf_op | source)
XLA Modules:
  0.0 331.4 jit_solution(2598828697972841031)
XLA Ops:
  0.7 0.1 pad.9.clone
  0.8 0.7 tile.10
  1.5 0.8 add_select_fusion.2
  2.2 0.1 pad_add_fusion
  2.3 0.1 tile.12
  2.4 1.4 maximum_maximum_fusion.b_ref
  3.8 0.6 pad_convert_fusion.refs_3_
  4.4 3.2 pad_maximum_fusion.io_ref
  7.6 109.7 %shard_map.254 = (bf16[2,2,6,768,768]{4,3,2,1,0:T(8,128)(2,1)}, f32[2,16,768]{2,1,0:T(8,128)}, f32[16,128]{1,0:T(8,128)}, bf16[192,768]{1,0:T(8,128)(2,1)}, bf16...) custom-call(bf16[2,768,768]{2,1,0:T(8,128)(2,1)} %pad_maximum_fusion, ...), custom_call_target="tpu_custom_call" | custom-call | tf_op jit(solution)/shard_map/pallas_call | solution.py:950
  117.3 1.3 slice_reduce_fusion
  118.6 195.3 %shard_map.255 = (bf16[2,768,768]{2,1,0:T(8,128)(2,1)}, bf16[2,768,768]{2,1,0:T(8,128)(2,1)}, bf16[2,576,768]{2,1,0:T(8,128)(2,1)}, bf16[2,192,768]{2,1,0:T(8,12...) custom-call(bf16[2,2,6,768,768]{4,3,2,1,0:T(8,128)(2,1)} %get-tuple-, ...), custom_call_target="tpu_custom_call" | custom-call | tf_op jit(solution)/shard_map/pallas_call | solution.py:478
  313.9 0.0 copy-start.2
  313.9 0.9 slice_convert_fusion
  314.8 0.6 slice.17
  315.4 0.1 constant_dynamic-slice_fusion
  315.5 0.6 reshape.100
  316.1 2.2 convert_element_type.31
  318.2 0.0 copy-done.2
  318.2 0.0 copy-start.1
  318.2 2.1 convert_bitcast_fusion
  320.3 0.5 copy-done.1
  320.8 0.0 copy-start
  320.8 2.5 convert_element_type.32
  323.4 0.0 copy-done
  323.4 0.0 copy-start.5
  323.4 0.0 copy-start.3
  323.4 2.5 convert_element_type.33
  325.9 0.0 copy-done.5
  325.9 0.0 copy-start.6
  325.9 0.0 copy-start.4
  326.0 0.7 copy.36
  326.7 0.0 copy-done.3
  326.7 0.0 copy-start.9
  326.7 0.0 copy-start.8
  326.7 0.0 copy-start.7
  326.7 1.0 copy.37
  327.7 0.0 copy-done.6
  327.7 0.7 copy.38
  328.4 0.0 copy-done.4
  328.4 1.0 copy.39
  329.4 0.0 copy-done.9
  329.4 0.6 copy.40
  330.0 0.0 copy-done.8
  330.0 0.6 copy.41
  330.6 0.0 copy-done.7
  330.6 0.6 copy.42
  (5 shorter events, 0.0 us)
Async XLA Ops:
  313.9 4.3 %copy-start.2 = (bf16[2,576,768]{2,1,0:T(8,128)(2,1)S(1)}, bf16[2,576,768]{2,1,0:T(8,128)(2,1)}, u32[]{:S(2)}) copy-start(bf16[2,576,768]{2,1,0:T(8,128)(2,1)} %get-tuple-element.76) | copy-start | bytes 5308420
  318.2 2.6 copy-start.1
  320.8 2.6 copy-start
  323.4 2.6 copy-start.5
  323.4 3.3 copy-start.3
  325.9 1.7 copy-start.6
  325.9 2.5 copy-start.4
  326.7 2.8 copy-start.9
  326.7 3.4 %copy-start.8 = (f32[2,2,768]{2,1,0:T(2,128)S(1)}, f32[2,2,768]{2,1,0:T(2,128)}, u32[]{:S(2)}) copy-start(f32[2,2,768]{2,1,0:T(2,128)} %get-tuple-element.109) | copy-start | bytes 36868
  326.7 4.0 %copy-start.7 = (f32[2,2,768]{2,1,0:T(2,128)S(1)}, f32[2,2,768]{2,1,0:T(2,128)}, u32[]{:S(2)}) copy-start(f32[2,2,768]{2,1,0:T(2,128)} %get-tuple-element.110) | copy-start | bytes 36868
